TPU v7x, 128 devices: a whole 4x4x4 slice. The times are simulated.
128 devices in a mesh: group: 4 (over y), dp: 32 (over z, x, core).
Axes of the slice: x: 4, y: 4, z: 4, core: 2. Of those that a mesh axis runs over, the one named last changes fastest.
Arguments:
- tokens: bfloat16 [32768, 1152], P(('group', 'dp')), may hold values from -6 to 6
- out_grad: bfloat16 [32768, 1152], P(('group', 'dp')), may hold values from -24 to 24
- timesteps: int32 [8], P('group'), may hold values from 0 to 999
- labels: int32 [8], P('group'), may hold values from 0 to 100
- grid_ids: int32 [8], P('group'), may hold values from 0 to 2, as said below
- w_qkv: bfloat16 [1152, 3456], replicated, may hold values from -0.1875 to 0.1875
- b_qv: float32 [2304], replicated, may hold values from -3 to 3
- w_proj: bfloat16 [1152, 1152], replicated, may hold values from -0.75 to 0.75
- b_proj: float32 [1152], replicated, may hold values from -3 to 3
- w_fc1: bfloat16 [1152, 4608], replicated, may hold values from -0.1875 to 0.1875
- b_fc1: float32 [4608], replicated, may hold values from -3 to 3
- w_fc2: bfloat16 [4608, 1152], replicated, may hold values from -0.09375 to 0.09375
- b_fc2: float32 [1152], replicated, may hold values from -3 to 3
- w_ada: bfloat16 [1152, 6912], P(None, 'dp'), may hold values from -0.125 to 0.125
- b_ada: float32 [6912], P('dp'), may hold values from -3 to 3
- w_t1: bfloat16 [256, 1152], replicated, may hold values from -0.375 to 0.375
- b_t1: float32 [1152], replicated, may hold values from -3 to 3
- w_t2: bfloat16 [1152, 1152], replicated, may hold values from -0.1875 to 0.1875
- b_t2: float32 [1152], replicated, may hold values from -3 to 3
- table: float32 [101, 1152], replicated, may hold values from -5 to 5
Outputs:
- block_out: bfloat16 [32768, 1152], P(('group', 'dp'))
- input_grad: bfloat16 [32768, 1152], P(('group', 'dp'))
- d_w_qkv: float32 [1152, 3456], P('dp')
- d_b_qv: float32 [2304], P('dp')
- d_w_proj: float32 [1152, 1152], P('dp')
- d_b_proj: float32 [1152], P('dp')
- d_w_fc1: float32 [1152, 4608], P('dp')
- d_b_fc1: float32 [4608], P('dp')
- d_w_fc2: float32 [4608, 1152], P('dp')
- d_b_fc2: float32 [1152], P('dp')
- d_w_ada: float32 [1152, 6912], P(None, 'dp')
- d_b_ada: float32 [6912], P('dp')
- d_w_t1: float32 [256, 1152], P('dp')
- d_b_t1: float32 [1152], P('dp')
- d_w_t2: float32 [1152, 1152], P('dp')
- d_b_t2: float32 [1152], P('dp')
- d_table: float32 [101, 1152], replicated
Inputs may be any that keep to these rules, and one draw needn't show every extreme that they name: `grid_ids`: all 2 items of one group share one grid id; 0 is the 16 x 16 grid, 1 the 12 x 20 grid, 2 the 20 x 12 grid.
All inputs are finite; a program needn't handle non-finite values.
Results may differ from a plain program's by a relative error of at most 0.014.
Values sent between devices are 32-bit elements; how exact they have to be, the bound alone decides.
A program may use at most 256 MiB of HBM per device.

v0:
```python
import functools
import math

import jax
import jax.numpy as jnp
from jax import lax
from jax.sharding import PartitionSpec as P

HEADS = 16
SLOTS = 256
ITEM_FRAMES = 16


EPS = 1e-06
NEG = -1e30


def hdot(left_op, right_op):
    return jnp.dot(
        left_op, right_op, precision=lax.Precision.HIGHEST, preferred_element_type=jnp.float32
    )


def hdot_t(left_op, right_op):
    return lax.dot_general(
        left_op,
        right_op,
        (((0,), (0,)), ((), ())),
        precision=lax.Precision.HIGHEST,
        preferred_element_type=jnp.float32,
    )


def weight_term(left_op, right_op):
    return lax.dot_general(
        left_op, right_op, (((0,), (0,)), ((), ())), preferred_element_type=jnp.float32
    )


def norm_rows(matrix):
    row_mean = jnp.mean(matrix, axis=-1, keepdims=True)
    centered = matrix - row_mean
    inv_std = lax.rsqrt(jnp.mean(centered * centered, axis=-1, keepdims=True) + EPS)
    return (centered * inv_std, inv_std)


def norm_back(grad_in, normed, inv_std):
    return inv_std * (
        grad_in
        - jnp.mean(grad_in, axis=-1, keepdims=True)
        - normed * jnp.mean(grad_in * normed, axis=-1, keepdims=True)
    )


def silu_back(pre_vals, grad_in):
    sigmoid = jax.nn.sigmoid(pre_vals)
    return grad_in * sigmoid * (1.0 + pre_vals * (1.0 - sigmoid))


def time_embed(step_ids, width_half):
    frequency = jnp.exp(
        jnp.arange(width_half, dtype=jnp.float32) * (-math.log(10000.0) / width_half)
    )
    angles = step_ids.astype(jnp.float32)[:, None] * frequency[None, :]
    return jnp.concatenate([jnp.cos(angles), jnp.sin(angles)], axis=1)


def own_block(vector, dp_place, dp_count):
    block_rows = vector.shape[0] // dp_count
    return lax.dynamic_slice_in_dim(vector, dp_place * block_rows, block_rows, 0)


def on_device(
    tokens,
    out_grad,
    timesteps,
    labels,
    grid_ids,
    w_qkv,
    b_qv,
    w_proj,
    b_proj,
    w_fc1,
    b_fc1,
    w_fc2,
    b_fc2,
    w_ada,
    b_ada,
    w_t1,
    b_t1,
    w_t2,
    b_t2,
    table,
):
    dp_count = lax.axis_size("dp")
    dp_place = lax.axis_index("dp")
    row_count, model_width = tokens.shape
    frame_count = row_count // SLOTS
    head_count = HEADS
    head_dim = model_width // head_count
    score_scale = 1.0 / math.sqrt(head_dim)
    frame_shape = (frame_count, SLOTS, head_count, head_dim)
    item_count = timesteps.shape[0]
    time_feats = time_embed(timesteps, w_t1.shape[0] // 2)
    onehot = (labels[:, None] == jnp.arange(table.shape[0], dtype=jnp.int32)[None, :]).astype(
        jnp.float32
    )
    pre_time = hdot(time_feats, w_t1.astype(jnp.float32)) + b_t1
    act_time = jax.nn.silu(pre_time)
    condition = hdot(act_time, w_t2.astype(jnp.float32)) + b_t2 + hdot(onehot, table)
    act_cond = jax.nn.silu(condition)
    ada_cols = w_ada.astype(jnp.float32)
    mod_part = hdot(act_cond, ada_cols) + b_ada
    mod_all = lax.all_gather(mod_part, "dp", axis=1, tiled=True)
    own_item = dp_place * frame_count // ITEM_FRAMES
    item_mod = lax.dynamic_index_in_dim(mod_all, own_item, 0, keepdims=False)
    shift_attn, scale_attn, gate_attn, shift_mlp, scale_mlp, gate_mlp = jnp.split(item_mod, 6)
    grid_value = lax.dynamic_index_in_dim(grid_ids, own_item, 0, keepdims=False)
    first_live = jnp.where(grid_value == 2, SLOTS // 16, 0)
    end_live = jnp.where(grid_value == 1, SLOTS - SLOTS // 16, SLOTS)
    slot_pos = jnp.arange(SLOTS, dtype=jnp.int32)
    valid_keys = (slot_pos >= first_live) & (slot_pos < end_live)
    live_rows = jnp.tile(valid_keys, frame_count).astype(jnp.float32)[:, None]
    token_vals = tokens.astype(jnp.float32)
    normed_one, inv_one = norm_rows(token_vals)
    attn_in = (normed_one * (1.0 + scale_attn) + shift_attn).astype(jnp.bfloat16)
    qkv_rows = jnp.dot(attn_in, w_qkv, preferred_element_type=jnp.float32)
    queries = (
        (qkv_rows[:, :model_width] + b_qv[:model_width]).astype(jnp.bfloat16).reshape(frame_shape)
    )
    key_rows = qkv_rows[:, model_width : 2 * model_width].astype(jnp.bfloat16).reshape(frame_shape)
    values = (
        (qkv_rows[:, 2 * model_width :] + b_qv[model_width:])
        .astype(jnp.bfloat16)
        .reshape(frame_shape)
    )

    def masked_scores():
        raw = (
            jnp.einsum("fqhd,fkhd->fhqk", queries, key_rows, preferred_element_type=jnp.float32)
            * score_scale
        )
        return jnp.where(valid_keys[None, None, None, :], raw, NEG)

    scores = masked_scores()
    row_max = jnp.max(scores, axis=-1, keepdims=True)
    shifted = jnp.exp(scores - row_max)
    row_total = jnp.sum(shifted, axis=-1, keepdims=True)
    log_total = row_max + jnp.log(row_total)
    attn_weights = (shifted / row_total).astype(jnp.bfloat16)
    mixed = jnp.einsum("fhqk,fkhd->fqhd", attn_weights, values, preferred_element_type=jnp.float32)
    mixed_rows = mixed.reshape(row_count, model_width).astype(jnp.bfloat16)
    attn_out = jnp.dot(mixed_rows, w_proj, preferred_element_type=jnp.float32) + b_proj
    resid_one = token_vals + gate_attn * attn_out
    normed_two, inv_two = norm_rows(resid_one)
    mlp_in = (normed_two * (1.0 + scale_mlp) + shift_mlp).astype(jnp.bfloat16)
    hidden = jnp.dot(mlp_in, w_fc1, preferred_element_type=jnp.float32) + b_fc1
    gelu_vals, gelu_pull = jax.vjp(functools.partial(jax.nn.gelu, approximate=True), hidden)
    activated = gelu_vals.astype(jnp.bfloat16)
    branch = jnp.dot(activated, w_fc2, preferred_element_type=jnp.float32) + b_fc2
    block_out = (resid_one + gate_mlp * branch).astype(jnp.bfloat16)
    cotangent = out_grad.astype(jnp.float32) * live_rows
    d_gate_mlp = jnp.sum(cotangent * branch, axis=0)
    grad_branch = (cotangent * gate_mlp).astype(jnp.bfloat16)
    grad_act = jnp.dot(grad_branch, w_fc2.T, preferred_element_type=jnp.float32)
    grad_hidden = gelu_pull(grad_act)[0].astype(jnp.bfloat16)
    grad_mlp_in = jnp.dot(grad_hidden, w_fc1.T, preferred_element_type=jnp.float32)
    d_shift_mlp = jnp.sum(grad_mlp_in, axis=0)
    d_scale_mlp = jnp.sum(grad_mlp_in * normed_two, axis=0)
    grad_resid = cotangent + norm_back(grad_mlp_in * (1.0 + scale_mlp), normed_two, inv_two)
    d_gate_attn = jnp.sum(grad_resid * attn_out, axis=0)
    grad_attn = (grad_resid * gate_attn).astype(jnp.bfloat16)
    grad_mixed = (
        jnp.dot(grad_attn, w_proj.T, preferred_element_type=jnp.float32)
        .astype(jnp.bfloat16)
        .reshape(frame_shape)
    )
    probs_again = jnp.exp(masked_scores() - log_total)
    grad_weights = jnp.einsum(
        "fqhd,fkhd->fhqk", grad_mixed, values, preferred_element_type=jnp.float32
    )
    row_dot = jnp.sum(probs_again * grad_weights, axis=-1, keepdims=True)
    grad_scores = (probs_again * (grad_weights - row_dot)).astype(jnp.bfloat16)
    grad_query = (
        jnp.einsum("fhqk,fkhd->fqhd", grad_scores, key_rows, preferred_element_type=jnp.float32)
        * score_scale
    )
    grad_key = (
        jnp.einsum("fhqk,fqhd->fkhd", grad_scores, queries, preferred_element_type=jnp.float32)
        * score_scale
    )
    grad_value = jnp.einsum(
        "fhqk,fqhd->fkhd",
        probs_again.astype(jnp.bfloat16),
        grad_mixed,
        preferred_element_type=jnp.float32,
    )
    grad_qkv = jnp.concatenate(
        [
            grad_query.reshape(row_count, model_width),
            grad_key.reshape(row_count, model_width),
            grad_value.reshape(row_count, model_width),
        ],
        axis=1,
    ).astype(jnp.bfloat16)
    grad_attn_in = jnp.dot(grad_qkv, w_qkv.T, preferred_element_type=jnp.float32)
    d_shift_attn = jnp.sum(grad_attn_in, axis=0)
    d_scale_attn = jnp.sum(grad_attn_in * normed_one, axis=0)
    input_grad = (
        grad_resid + norm_back(grad_attn_in * (1.0 + scale_attn), normed_one, inv_one)
    ).astype(jnp.bfloat16)
    bias_qv = jnp.concatenate(
        [
            jnp.sum(grad_qkv[:, :model_width], axis=0, dtype=jnp.float32),
            jnp.sum(grad_qkv[:, 2 * model_width :], axis=0, dtype=jnp.float32),
        ]
    )
    bias_proj = jnp.sum(grad_attn, axis=0, dtype=jnp.float32)
    bias_fc1 = jnp.sum(grad_hidden, axis=0, dtype=jnp.float32)
    bias_fc2 = jnp.sum(grad_branch, axis=0, dtype=jnp.float32)
    d_mod_item = jnp.concatenate(
        [d_shift_attn, d_scale_attn, d_gate_attn, d_shift_mlp, d_scale_mlp, d_gate_mlp]
    )
    d_mod_all = lax.dynamic_update_index_in_dim(
        jnp.zeros((item_count, 6 * model_width), jnp.float32), d_mod_item, own_item, 0
    )
    d_mod_cols = lax.psum_scatter(d_mod_all, "dp", scatter_dimension=1, tiled=True)
    grad_w_ada = hdot_t(act_cond, d_mod_cols)
    grad_b_ada = jnp.sum(d_mod_cols, axis=0)
    cond_part = hdot(d_mod_cols, ada_cols.T)
    grad_act_cond, bias_qv, bias_proj, bias_fc1, bias_fc2 = lax.psum(
        (cond_part, bias_qv, bias_proj, bias_fc1, bias_fc2), "dp"
    )
    grad_cond = silu_back(condition, grad_act_cond)
    grad_table = hdot_t(onehot, grad_cond)
    grad_w_t2 = hdot_t(act_time, grad_cond)
    grad_b_t2 = jnp.sum(grad_cond, axis=0)
    grad_pre = silu_back(pre_time, hdot(grad_cond, w_t2.astype(jnp.float32).T))
    grad_w_t1 = hdot_t(time_feats, grad_pre)
    grad_b_t1 = jnp.sum(grad_pre, axis=0)
    slice_qv = own_block(bias_qv, dp_place, dp_count)
    slice_proj = own_block(bias_proj, dp_place, dp_count)
    slice_fc1 = own_block(bias_fc1, dp_place, dp_count)
    slice_fc2 = own_block(bias_fc2, dp_place, dp_count)
    slice_w_t1 = own_block(grad_w_t1, dp_place, dp_count)
    slice_b_t1 = own_block(grad_b_t1, dp_place, dp_count)
    slice_w_t2 = own_block(grad_w_t2, dp_place, dp_count)
    slice_b_t2 = own_block(grad_b_t2, dp_place, dp_count)
    term_qkv = weight_term(attn_in, grad_qkv)
    term_proj = weight_term(mixed_rows, grad_attn)
    term_fc1 = weight_term(mlp_in, grad_hidden)
    term_fc2 = weight_term(activated, grad_branch)
    shard_qkv, shard_proj, shard_fc1, shard_fc2 = (
        lax.psum_scatter(term_qkv, "dp", scatter_dimension=0, tiled=True),
        lax.psum_scatter(term_proj, "dp", scatter_dimension=0, tiled=True),
        lax.psum_scatter(term_fc1, "dp", scatter_dimension=0, tiled=True),
        lax.psum_scatter(term_fc2, "dp", scatter_dimension=0, tiled=True),
    )
    totals = lax.psum(
        (
            shard_qkv,
            shard_proj,
            shard_fc1,
            shard_fc2,
            slice_qv,
            slice_proj,
            slice_fc1,
            slice_fc2,
            grad_w_ada,
            grad_b_ada,
            slice_w_t1,
            slice_b_t1,
            slice_w_t2,
            slice_b_t2,
            grad_table,
        ),
        "group",
    )
    sum_qkv, sum_proj, sum_fc1, sum_fc2 = (totals[0], totals[1], totals[2], totals[3])
    rest = totals[4:]
    return (
        block_out,
        input_grad,
        sum_qkv,
        rest[0],
        sum_proj,
        rest[1],
        sum_fc1,
        rest[2],
        sum_fc2,
        rest[3],
        rest[4],
        rest[5],
        rest[6],
        rest[7],
        rest[8],
        rest[9],
        rest[10],
    )


def solution(mesh):
    placed = (
        P(("group", "dp"), None),
        P(("group", "dp"), None),
        P("group"),
        P("group"),
        P("group"),
        P(),
        P(),
        P(),
        P(),
        P(),
        P(),
        P(),
        P(),
        P(None, "dp"),
        P("dp"),
        P(),
        P(),
        P(),
        P(),
        P(),
    )
    return jax.shard_map(
        on_device,
        mesh=mesh,
        in_specs=placed,
        out_specs=(
            P(("group", "dp"), None),
            P(("group", "dp"), None),
            P("dp", None),
            P("dp"),
            P("dp", None),
            P("dp"),
            P("dp", None),
            P("dp"),
            P("dp", None),
            P("dp"),
            P(None, "dp"),
            P("dp"),
            P("dp", None),
            P("dp"),
            P("dp", None),
            P("dp"),
            P(),
        ),
        check_vma=False,
    )
```

profile of v0, /device:TPU:1, one launch (start us, length us, event | category | flops | bytes accessed | tf_op | source)
XLA Modules:
  0.0 1051.8 jit_solution(8840885134122161930)
XLA Ops:
  9.8 2.9 convolution_add_fusion.4
  13.5 26.9 %all-gather = f32[32,216,2]{1,2,0:T(2,128)S(1)} all-gather(f32[1,216,2]{1,2,0:T(2,128)S(1)} %fusion.40), channel_id=1, replica_groups=mesh['group'=4,'dp'=32] {'dp'}, dimensions={0}, use_global_device_ids=true | all-gather | bytes 57024 | tf_op jit(solution)/shard_map/all_gather | solution.py:114
  41.2 6.0 fusion.67
  49.2 2.1 copy.60
  55.3 2.1 copy.59
  57.5 2.3 fusion.78
  63.5 2.2 fusion.75
  66.2 3.3 convolution_add_fusion
  69.6 2.2 copy-done.15
  71.8 20.9 %fusion.69 = f32[4608,1152]{1,0:T(8,128)} fusion(bf16[256,1152]{1,0:T(8,128)(2,1)S(1)} %copy-done.29, f32[256]{0:T(256)S(1)} %get-tuple-element.64, f32[1152]{0:T(1024)S(1)} %get-tuple-element.27, f32[256,4608]{1,0:T(8,128)S(1)} %convolution_add_fusion), kind=kOutput, calls=%fused_computation.141 | convolution fusion | flops 2729705472 | bytes 26547712 | tf_op jit(solution)/shard_map/dot_general | solution.py:35
  92.7 8.6 convert_reduce_fusion
  101.4 10.2 multiply_reduce_fusion.2
  111.6 11.1 %multiply_reduce_fusion.1 = (f32[1152]{0:T(1024)}, f32[1152]{0:T(1024)S(1)}, bf16[256,1152]{1,0:T(8,128)(2,1)}, f32[1152]{0:T(1024)S(1)}, bf16[256,1152]{1,0:T(8,128)(2,1)S(1)}, /*index=5*/f32[256,1152]{1,0:T(8,128)}) fusion(bf16[256,1152]{1,0:T(8,128)(2,1)S(1)} %copy-done.30, f32[256]{0:T(256)S(1)} %get-tuple-element.64, f32[1152]{0:T(1024)S(1)} %get-tuple-element.27, ...), kind=kOutput, calls=%fused_computation.61 | convolution fusion | flops 2735600640 | bytes 20681216 | tf_op jit(solution)/shard_map/dot_general | solution.py:160
  126.8 4.2 multiply_reduce_fusion
  136.9 3.3 fusion.80
  140.2 8.6 fusion.41
  148.8 9.1 fusion.71
  157.9 322.7 %fusion.72 = (f32[48,3456]{1,0:T(8,128)S(1)}, f32[48,1152]{1,0:T(8,128)S(1)}, f32[40,4608]{1,0:T(8,128)S(1)}) fusion(f32[1152,3456]{1,0:T(8,128)} %fusion.41, f32[1152,1152]{1,0:T(8,128)} %fusion.80, f32[1152,4608]{1,0:T(8,128)} %fusion.71), kind=kCustom, calls=%all-reduce-scatter.3 | all-reduce-scatter fusion | flops 12976130 | bytes 44089856
  480.6 6.9 collective-permute-start.10
  487.5 5.3 collective-permute-start.11
  495.4 3.1 collective-permute-start.15
  499.3 3.3 collective-permute-start.7
  502.6 6.5 fusion.36
  512.3 119.5 %all-reduce.3 = f32[2,6912]{1,0:T(2,128)S(1)} all-reduce(f32[2,6912]{1,0:T(2,128)S(1)} %dynamic_update_slice.4), channel_id=6, replica_groups=mesh['group'=4,'dp'=32] {'dp'}, use_global_device_ids=true, to_apply=%region_38.39.clone | all-reduce | flops 13824 | bytes 110592
  638.2 3.6 collective-permute-start.8
  646.2 3.4 collective-permute-done.14
  649.5 2.1 collective-permute-start.1
  651.7 129.3 %all-reduce.7 = (f32[2304]{0:T(1024)}, f32[1152]{0:T(1024)}, f32[4608]{0:T(1024)}, f32[1152]{0:T(1024)S(1)}, f32[2,1152]{1,0:T(2,128)S(1)}) all-reduce(f32[2304]{0:T(1024)S(1)} %pad_maximum_fusion.3, f32[1152]{0:T(1024)S(1)} %get-tuple-element.71, f32[4608]{0:T(1024)S(1)} %get-tuple-element.89, ...), channel_id=1, replica_groups=mesh['group'=4,'dp'=32] {'dp'}, use_global_device_ids=true, to_apply=%region_15.16 | all-reduce | flops 11520 | bytes 92160 | tf_op jit(solution)/shard_map/psum | solution.py:231
  781.0 2.2 collective-permute-start.2
  783.2 2.1 collective-permute-start.3
  785.3 2.3 collective-permute-start.4
  787.7 4.8 fusion.63
  792.5 2.2 collective-permute-start.5
  794.7 2.5 collective-permute-start.6
  798.4 8.0 collective-permute-start.16
  806.4 3.6 collective-permute-start.17
  810.0 11.8 %collective-permute-done.4 = f32[48,3456]{1,0:T(8,128)} collective-permute-done((f32[48,3456]{1,0:T(8,128)S(1)}, f32[48,3456]{1,0:T(8,128)}, u32[]{:S(2)}, u32[]{:S(2)}) %collective-permute-start.4) | collective-permute-done | bytes 663584
  821.9 3.6 collective-permute-start.18
  827.5 14.7 %concatenate.18 = f32[420,1152]{1,0:T(8,128)} concatenate(f32[36,1152]{1,0:T(8,128)} %collective-permute-done.15, f32[48,1152]{1,0:T(8,128)S(1)} %collective-permute-done.14, f32[48,1152]{1,0:T(8,128)S(1)} %collective-permute-done.13, f32[48,1152]{1,0:T(8,128)} %collective-permute-done.12, f32[48,1152]{1,0:T(8,128)} %collective-permute-done.11, ...), dimensions={0} | concatenate | bytes 3870720
  843.8 11.6 %collective-permute-start.19 = (f32[4,4608]{1,0:T(4,128)S(1)}, f32[4,4608]{1,0:T(4,128)S(1)}, u32[]{:S(2)}, u32[]{:S(2)}) collective-permute-start(f32[4,4608]{1,0:T(4,128)S(1)} %slice.34), channel_id=1, source_target_pairs={{0,4},{1,5},{2,6},{3,7},{4,8},{5,9},{6,10},{7,11},{8,12},{9,13},{1... | collective-permute-start | bytes 221192
  855.4 35.2 %collective-permute-done.6 = f32[48,3456]{1,0:T(8,128)} collective-permute-done((f32[48,3456]{1,0:T(8,128)S(1)}, f32[48,3456]{1,0:T(8,128)}, u32[]{:S(2)}, u32[]{:S(2)}) %collective-permute-start.6) | collective-permute-done | bytes 663584
  890.6 36.7 %concatenate.17 = f32[420,3456]{1,0:T(8,128)} concatenate(f32[36,3456]{1,0:T(8,128)} %collective-permute-done.7, f32[48,3456]{1,0:T(8,128)} %collective-permute-done.6, f32[48,3456]{1,0:T(8,128)} %collective-permute-done.5, f32[48,3456]{1,0:T(8,128)} %collective-permute-done.4, f32[48,3456]{1,0:T(8,128)} %collective-permute-done.3, f32[48,3456]{1,0:T(8,128)} %collective-permute-done.2, ...), dimensions={0} | concatenate | bytes 11612160
  929.3 17.1 %concatenate.19 = f32[164,4608]{1,0:T(8,128)} concatenate(f32[4,4608]{1,0:T(4,128)S(1)} %collective-permute-done.19, f32[40,4608]{1,0:T(8,128)} %collective-permute-done.18, f32[40,4608]{1,0:T(8,128)} %collective-permute-done.17, f32[40,4608]{1,0:T(8,128)S(1)} %collective-permute-done.16, f32[40,4608]{1,0:T(8,128)S(1)} %get-tuple-element.58), dimensions={0} | concatenate | bytes 6045696
  946.4 2.2 constant_dynamic-slice_fusion
  948.7 2.2 fusion.79
  954.8 16.7 %all-reduce.8 = (f32[72]{0:T(128)}, f32[36]{0:T(128)}, f32[144]{0:T(256)}, f32[36]{0:T(128)}, f32[216]{0:T(256)}, /*index=5*/f32[8,1152]{1,0:T(8,128)}, f32[36]{0:T(128)}, f32[36]{0:T(128)}) all-reduce(f32[72]{0:T(128)S(1)} %dynamic_slice.34, f32[36]{0:T(128)S(1)} %dynamic_slice.35, ...), channel_id=1, replica_groups=mesh['group'=4,'dp'=32] {'group'}, use_global_device_ids=true, to_apply=%region_16.17 | all-reduce | flops 9792 | bytes 78336 | tf_op jit(solution)/shard_map/psum | solution.py:259
  971.5 64.2 %all-reduce.13.cloned.1.call-done = (f32[36,3456]{1,0:T(8,128)}, f32[36,1152]{1,0:T(8,128)}, f32[36,4608]{1,0:T(8,128)}, f32[144,1152]{1,0:T(8,128)}, f32[1152,2...) async-done(((f32[36,3456]{1,0:T(8,128)}, f32[36,1152]{1,0:T(8,128)}, f32[36,4608]{1,0:T(8,128)}, f32[144,1152]{1,0:T(8,128)}, f32[1152,216]{0,1:T(8,128)}, ...) | async-done | bytes 3617296 | tf_op jit(solution)/shard_map/psum | solution.py:259
  1039.3 2.2 copy.89
  (202 shorter events, 55.9 us)
Async XLA Ops:
  7.2 55.0 %copy-start = (bf16[1152,1152]{1,0:T(8,128)(2,1)S(1)}, bf16[1152,1152]{1,0:T(8,128)(2,1)}, u32[]{:S(2)}) copy-start(bf16[1152,1152]{1,0:T(8,128)(2,1)} %param.27) | copy-start | bytes 7962628
  7.2 5.5 copy-start.41
  7.2 5.8 copy-start.43
  7.2 941.4 %reduce-scatter.9.cloned.1.call-start = ((), (), s32[]{:S(2)}) async-start(), calls=%async_computation.1 | async-start | bytes 21897216 | tf_op jit(solution)/shard_map/reduce_scatter | solution.py:257
  7.3 5.4 copy-start.33
  7.3 5.7 copy-start.24
  8.3 32.4 %copy-start.4 = (bf16[256,1152]{1,0:T(8,128)(2,1)S(1)}, bf16[256,1152]{1,0:T(8,128)(2,1)}, u32[]{:S(2)}) copy-start(bf16[256,1152]{1,0:T(8,128)(2,1)} %param.20) | copy-start | bytes 1769476
  9.8 31.4 %copy-start.36 = (f32[2304]{0:T(1024)S(1)}, f32[2304]{0:T(1024)}, u32[]{:S(2)}) copy-start(f32[2304]{0:T(1024)} %param.26) | copy-start | bytes 27652
  48.0 5.4 copy-start.46
  59.8 6.1 slice-start
  61.3 4.9 slice-start.2
  66.2 5.5 copy-start.29
  92.7 943.0 %all-reduce.13.cloned.1.call-start = ((), (), s32[]{:S(2)}) async-start(), calls=%async_computation.2 | async-start | bytes 7593984 | tf_op jit(solution)/shard_map/psum | solution.py:259
  92.7 8.6 copy-start.6
  101.3 10.3 copy-start.20
  101.3 10.3 copy-start.16
  101.4 10.2 copy-start.30
  101.4 10.2 copy-start.45
  133.9 6.2 copy-start.9
  140.1 8.6 copy-start.7
  140.2 8.6 copy-start.21
  157.9 344.7 %copy-start.10 = (bf16[16,72,256]{2,1,0:T(8,128)(2,1)S(1)}, bf16[16,72,256]{2,1,0:T(8,128)(2,1)}, u32[]{:S(2)}) copy-start(bf16[16,72,256]{2,1,0:T(8,128)(2,1)} %copy-done.9) | copy-start | bytes 1769476
  480.6 156.0 %collective-permute-start.10 = (f32[48,1152]{1,0:T(8,128)S(1)}, f32[48,1152]{1,0:T(8,128)}, u32[]{:S(2)}, u32[]{:S(2)}) collective-permute-start(f32[48,1152]{1,0:T(8,128)S(1)} %get-tuple-element.57), channel_id=1, source_target_pairs={{0,3},{1,4},{2,5},{3,6},{4,7},{5,8},{6,9},{7,10},{8,11},{9,12},{10... | collective-permute-start | bytes 663560
  487.5 150.7 %collective-permute-start.11 = (f32[48,1152]{1,0:T(8,128)S(1)}, f32[48,1152]{1,0:T(8,128)}, u32[]{:S(2)}, u32[]{:S(2)}) collective-permute-start(f32[48,1152]{1,0:T(8,128)S(1)} %get-tuple-element.57), channel_id=1, source_target_pairs={{0,4},{1,5},{2,6},{3,7},{4,8},{5,9},{6,10},{7,11},{8,12},{9,13},{1... | collective-permute-start | bytes 663560
  492.7 149.1 %collective-permute-start.12 = (f32[48,1152]{1,0:T(8,128)S(1)}, f32[48,1152]{1,0:T(8,128)}, u32[]{:S(2)}, u32[]{:S(2)}) collective-permute-start(f32[48,1152]{1,0:T(8,128)S(1)} %get-tuple-element.57), channel_id=1, source_target_pairs={{0,5},{1,6},{2,7},{3,8},{4,9},{5,10},{6,11},{7,12},{8,13},{9,14},{... | collective-permute-start | bytes 663560
  495.4 139.9 %collective-permute-start.15 = (f32[36,1152]{1,0:T(8,128)}, f32[36,1152]{1,0:T(8,128)}, u32[]{:S(2)}, u32[]{:S(2)}) collective-permute-start(f32[36,1152]{1,0:T(8,128)} %slice.33), channel_id=1, source_target_pairs={{0,8},{1,9},{2,10},{3,11},{4,12},{5,13},{6,14},{7,15},{8,16},{9,17... | collective-permute-start | bytes 497672
  499.3 286.0 %collective-permute-start.7 = (f32[36,3456]{1,0:T(8,128)}, f32[36,3456]{1,0:T(8,128)}, u32[]{:S(2)}, u32[]{:S(2)}) collective-permute-start(f32[36,3456]{1,0:T(8,128)} %slice.32), channel_id=1, source_target_pairs={{0,8},{1,9},{2,10},{3,11},{4,12},{5,13},{6,14},{7,15},{8,16},{9,17... | collective-permute-start | bytes 1493000
  502.6 6.6 copy-start.17
  502.6 6.6 copy-start.25
  635.3 8.8 collective-permute-start.13
  636.6 12.9 %collective-permute-start.14 = (f32[48,1152]{1,0:T(8,128)S(1)}, f32[48,1152]{1,0:T(8,128)S(1)}, u32[]{:S(2)}, u32[]{:S(2)}) collective-permute-start(f32[48,1152]{1,0:T(8,128)S(1)} %get-tuple-element.57), channel_id=1, source_target_pairs={{0,7},{1,8},{2,9},{3,10},{4,11},{5,12},{6,13},{7,14},{8,15},{9,16}... | collective-permute-start | bytes 663560
  638.2 142.8 %collective-permute-start.8 = (f32[48,1152]{1,0:T(8,128)S(1)}, f32[48,1152]{1,0:T(8,128)}, u32[]{:S(2)}, u32[]{:S(2)}) collective-permute-start(f32[48,1152]{1,0:T(8,128)S(1)} %get-tuple-element.57), channel_id=1, source_target_pairs={{0,1},{1,2},{2,3},{3,4},{4,5},{5,6},{6,7},{7,8},{8,9},{9,10},{10,1... | collective-permute-start | bytes 663560
  641.8 141.3 %collective-permute-start.9 = (f32[48,1152]{1,0:T(8,128)S(1)}, f32[48,1152]{1,0:T(8,128)}, u32[]{:S(2)}, u32[]{:S(2)}) collective-permute-start(f32[48,1152]{1,0:T(8,128)S(1)} %get-tuple-element.57), channel_id=1, source_target_pairs={{0,2},{1,3},{2,4},{3,5},{4,6},{5,7},{6,8},{7,9},{8,10},{9,11},{10,... | collective-permute-start | bytes 663560
  644.1 148.4 %collective-permute-start = (f32[48,3456]{1,0:T(8,128)S(1)}, f32[48,3456]{1,0:T(8,128)S(1)}, u32[]{:S(2)}, u32[]{:S(2)}) collective-permute-start(f32[48,3456]{1,0:T(8,128)S(1)} %get-tuple-element.56), channel_id=1, source_target_pairs={{0,1},{1,2},{2,3},{3,4},{4,5},{5,6},{6,7},{7,8},{8,9},{9,10},{10,1... | collective-permute-start | bytes 1990664
  649.5 145.2 %collective-permute-start.1 = (f32[48,3456]{1,0:T(8,128)S(1)}, f32[48,3456]{1,0:T(8,128)}, u32[]{:S(2)}, u32[]{:S(2)}) collective-permute-start(f32[48,3456]{1,0:T(8,128)S(1)} %get-tuple-element.56), channel_id=1, source_target_pairs={{0,2},{1,3},{2,4},{3,5},{4,6},{5,7},{6,8},{7,9},{8,10},{9,11},{10,... | collective-permute-start | bytes 1990664
  781.0 17.4 %collective-permute-start.2 = (f32[48,3456]{1,0:T(8,128)S(1)}, f32[48,3456]{1,0:T(8,128)}, u32[]{:S(2)}, u32[]{:S(2)}) collective-permute-start(f32[48,3456]{1,0:T(8,128)S(1)} %get-tuple-element.56), channel_id=1, source_target_pairs={{0,3},{1,4},{2,5},{3,6},{4,7},{5,8},{6,9},{7,10},{8,11},{9,12},{10... | collective-permute-start | bytes 1990664
  783.2 23.3 %collective-permute-start.3 = (f32[48,3456]{1,0:T(8,128)S(1)}, f32[48,3456]{1,0:T(8,128)}, u32[]{:S(2)}, u32[]{:S(2)}) collective-permute-start(f32[48,3456]{1,0:T(8,128)S(1)} %get-tuple-element.56), channel_id=1, source_target_pairs={{0,4},{1,5},{2,6},{3,7},{4,8},{5,9},{6,10},{7,11},{8,12},{9,13},{1... | collective-permute-start | bytes 1990664
  785.3 36.6 %collective-permute-start.4 = (f32[48,3456]{1,0:T(8,128)S(1)}, f32[48,3456]{1,0:T(8,128)}, u32[]{:S(2)}, u32[]{:S(2)}) collective-permute-start(f32[48,3456]{1,0:T(8,128)S(1)} %get-tuple-element.56), channel_id=1, source_target_pairs={{0,5},{1,6},{2,7},{3,8},{4,9},{5,10},{6,11},{7,12},{8,13},{9,14},{... | collective-permute-start | bytes 1990664
  792.5 5.9 copy-start.27
  792.5 51.2 %collective-permute-start.5 = (f32[48,3456]{1,0:T(8,128)S(1)}, f32[48,3456]{1,0:T(8,128)}, u32[]{:S(2)}, u32[]{:S(2)}) collective-permute-start(f32[48,3456]{1,0:T(8,128)S(1)} %get-tuple-element.56), channel_id=1, source_target_pairs={{0,6},{1,7},{2,8},{3,9},{4,10},{5,11},{6,12},{7,13},{8,14},{9,15},... | collective-permute-start | bytes 1990664
  794.7 95.9 %collective-permute-start.6 = (f32[48,3456]{1,0:T(8,128)S(1)}, f32[48,3456]{1,0:T(8,128)}, u32[]{:S(2)}, u32[]{:S(2)}) collective-permute-start(f32[48,3456]{1,0:T(8,128)S(1)} %get-tuple-element.56), channel_id=1, source_target_pairs={{0,7},{1,8},{2,9},{3,10},{4,11},{5,12},{6,13},{7,14},{8,15},{9,16}... | collective-permute-start | bytes 1990664
  798.4 130.8 %collective-permute-start.16 = (f32[40,4608]{1,0:T(8,128)S(1)}, f32[40,4608]{1,0:T(8,128)S(1)}, u32[]{:S(2)}, u32[]{:S(2)}) collective-permute-start(f32[40,4608]{1,0:T(8,128)S(1)} %get-tuple-element.58), channel_id=1, source_target_pairs={{0,1},{1,2},{2,3},{3,4},{4,5},{5,6},{6,7},{7,8},{8,9},{9,10},{10,1... | collective-permute-start | bytes 2211848
  806.4 122.8 %collective-permute-start.17 = (f32[40,4608]{1,0:T(8,128)S(1)}, f32[40,4608]{1,0:T(8,128)}, u32[]{:S(2)}, u32[]{:S(2)}) collective-permute-start(f32[40,4608]{1,0:T(8,128)S(1)} %get-tuple-element.58), channel_id=1, source_target_pairs={{0,2},{1,3},{2,4},{3,5},{4,6},{5,7},{6,8},{7,9},{8,10},{9,11},{10,... | collective-permute-start | bytes 2211848
  821.9 107.4 %collective-permute-start.18 = (f32[40,4608]{1,0:T(8,128)S(1)}, f32[40,4608]{1,0:T(8,128)}, u32[]{:S(2)}, u32[]{:S(2)}) collective-permute-start(f32[40,4608]{1,0:T(8,128)S(1)} %get-tuple-element.58), channel_id=1, source_target_pairs={{0,3},{1,4},{2,5},{3,6},{4,7},{5,8},{6,9},{7,10},{8,11},{9,12},{10... | collective-permute-start | bytes 2211848
  843.8 85.5 %collective-permute-start.19 = (f32[4,4608]{1,0:T(4,128)S(1)}, f32[4,4608]{1,0:T(4,128)S(1)}, u32[]{:S(2)}, u32[]{:S(2)}) collective-permute-start(f32[4,4608]{1,0:T(4,128)S(1)} %slice.34), channel_id=1, source_target_pairs={{0,4},{1,5},{2,6},{3,7},{4,8},{5,9},{6,10},{7,11},{8,12},{9,13},{1... | collective-permute-start | bytes 221192
  1035.7 5.8 copy-start.28
  1035.7 6.6 copy-start.26
  1039.3 5.4 copy-start.1
  (24 other events, 61.3 us)
Sparse Core Ops, SparseCore 0:
  92.8 390.9 reduce-scatter.8
  948.8 86.8 all-reduce.12
where the time goes:
time: 1060 us; the launch traced here: 1050 us
  blocking collectives  615 us (58%)
  matrix products  119 us (11%)
  waiting for transfers between devices  115 us (11%)
  local copies, waits for them, and re-layouts  107 us (10%)
  starting transfers between devices  71 us (7%)
  between operations  18.3 us (2%)
    unnamed x2, blocking collectives  442 us
    psum x1, blocking collectives, on_device(): lax.psum((cond_part, bias_qv, bias_proj, bias_fc1, bias_fc2), 'dp')  129 us
    unnamed x123, local copies, waits for them, and re-layouts  94 us
    unnamed x20, starting transfers between devices  70.9 us
    psum x1, waiting for transfers between devices, on_device(): lax.psum((shard_qkv, shard_proj, shard_fc1, shard_fc2, slice_qv, slice_pr...  64.2 us
    unnamed x22, waiting for transfers between devices  50.5 us
    dot_general x4, matrix products, weight_term(): lax.dot_general(left_op, right_op, (((0,), (0,)), ((), ())), preferred_el...  41.9 us
    all_gather x1, blocking collectives, on_device(): mod_all = lax.all_gather(mod_part, 'dp', axis=1, tiled=True)  26.9 us
  transfers between devices with their start and end apart: 22, of which 4 were waited for; matrix products, arithmetic and copies ran while one was open for 46% of the time, Pallas kernels for 0%

commit v1 on v0

--- a/solution.py
+++ b/solution.py
@@ -4,6 +4,8 @@
 import jax
 import jax.numpy as jnp
 from jax import lax
+from jax.experimental import pallas as pl
+from jax.experimental.pallas import tpu as pltpu
 from jax.sharding import PartitionSpec as P
 
 HEADS = 16
@@ -68,6 +70,441 @@
 def own_block(vector, dp_place, dp_count):
     block_rows = vector.shape[0] // dp_count
     return lax.dynamic_slice_in_dim(vector, dp_place * block_rows, block_rows, 0)
+
+
+MESH = pl.DeviceIdType.MESH
+ORDERS = (("y", "z", "x"), ("z", "x", "y"), ("x", "y", "z"))
+STREAMS = tuple((order, pairing) for pairing in (0, 1) for order in ORDERS)
+BLOCKS = (32, 16, 8, 4, 2, 1)
+LANDS_AT = (0, 32, 48, 56, 60, 62)
+PIECE = 56
+OWN = 72
+
+
+def coords():
+    place = lax.axis_index("dp")
+    return {
+        "y": lax.axis_index("group"),
+        "z": lax.div(place, 8),
+        "x": lax.rem(lax.div(place, 2), 4),
+        "core": lax.rem(place, 2),
+    }
+
+
+def device_at(at):
+    return (at["y"], (at["z"] * 4 + at["x"]) * 2 + at["core"])
+
+
+def sibling_of(at):
+    return device_at({**at, "core": 1 - at["core"]})
+
+
+def partner_of(at, axis, pairing):
+    here = at[axis]
+    if pairing == 0:
+        there = here + 1 - 2 * lax.rem(here, 2)
+    else:
+        there = lax.rem(here + 3 + 2 * lax.rem(here, 2), 4)
+    return device_at({**at, axis: there})
+
+
+def slot_of(pairing, value):
+    if pairing == 1:
+        return value
+    if isinstance(value, int):
+        return (0, 2, 3, 1)[value]
+    return lax.rem(value + lax.div(value + 1, 2), 4)
+
+
+def grad_kernel(
+    act_own,
+    act_wide,
+    gbr_own,
+    gbr_wide,
+    mlp_own,
+    mlp_wide,
+    ghid_own,
+    ghid_wide,
+    two_own,
+    two_wide,
+    gqkv_own,
+    gqkv_wide,
+    out_qkv,
+    out_proj,
+    out_fc1,
+    out_fc2,
+    parts,
+    landed,
+    lhs,
+    rhs,
+    stage_lhs,
+    stage_rhs,
+    final,
+    other,
+    send_sem,
+    recv_sem,
+    credit,
+    swap_send,
+    swap_recv,
+    swap_credit,
+    own_sem,
+    ring_send,
+    ring_recv,
+    pair_send,
+    pair_recv,
+):
+    at = coords()
+    core = at["core"]
+    sibling = sibling_of(at)
+    barrier = pltpu.get_barrier_semaphore()
+    peers = [partner_of(at, axis, pairing) for axis in "xyz" for pairing in (0, 1)]
+    peers.append(device_at({**at, "y": lax.rem(at["y"] + 2, 4)}))
+    peers.append(sibling)
+    for peer in peers:
+        pl.semaphore_signal(barrier, inc=1, device_id=peer, device_id_type=MESH)
+    pl.semaphore_wait(barrier, len(peers))
+
+    def swap(phase):
+        if phase == 0:
+            pairs = [(act_wide.at[1 - core], stage_lhs), (gbr_wide, stage_rhs.at[:, 0:1152])]
+        elif phase == 1:
+            pairs = [(mlp_wide, stage_lhs.at[0:8]), (ghid_wide.at[1 - core], stage_rhs)]
+        else:
+            pairs = [(two_wide, stage_lhs), (gqkv_wide.at[1 - core], stage_rhs)]
+        return [
+            pltpu.make_async_remote_copy(
+                src_ref=source,
+                dst_ref=target,
+                send_sem=swap_send.at[place],
+                recv_sem=swap_recv.at[place],
+                device_id=sibling,
+                device_id_type=MESH,
+            )
+            for place, (source, target) in enumerate(pairs)
+        ]
+
+    def own_loads(phase):
+        if phase == 0:
+            pairs = [
+                (act_own.at[core], lhs.at[:, :, 0:256]),
+                (gbr_own, rhs.at[0:256, 0:1152]),
+            ]
+        elif phase == 1:
+            pairs = [
+                (mlp_own, lhs.at[0:8, :, 0:256]),
+                (ghid_own.at[core], rhs.at[0:256]),
+            ]
+        else:
+            pairs = [
+                (two_own, lhs.at[:, :, 0:256]),
+                (gqkv_own.at[core], rhs.at[0:256]),
+            ]
+        return [
+            pltpu.make_async_copy(source, target, own_sem.at[place])
+            for place, (source, target) in enumerate(pairs)
+        ]
+
+    def swap_start(phase):
+        if phase:
+            pl.semaphore_wait(swap_credit, 1)
+        for copy in swap(phase):
+            copy.start()
+
+    def swap_finish(phase):
+        for copy in own_loads(phase):
+            copy.start()
+        for copy in swap(phase):
+            copy.wait()
+
+        def narrow_lhs(step, _):
+            lhs[step, :, 256:512] = stage_lhs[step].astype(jnp.bfloat16)
+            return _
+
+        lax.fori_loop(0, 8 if phase == 1 else 16, narrow_lhs, 0)
+        wide = 1152 if phase == 0 else 2304
+
+        def narrow_rhs(step, _):
+            rows = pl.ds(pl.multiple_of(step * 32, 32), 32)
+            into = pl.ds(pl.multiple_of(256 + step * 32, 32), 32)
+            rhs[into, 0:wide] = stage_rhs[rows, 0:wide].astype(jnp.bfloat16)
+            return _
+
+        lax.fori_loop(0, 8, narrow_rhs, 0)
+        if phase < 2:
+            pl.semaphore_signal(swap_credit, inc=1, device_id=sibling, device_id_type=MESH)
+        for copy in own_loads(phase):
+            copy.wait()
+
+    def base_of(stream, z_place, x_place, y_slot):
+        order, pairing = STREAMS[stream]
+        slots = {"y": y_slot, "z": slot_of(pairing, z_place), "x": slot_of(pairing, x_place)}
+        return (slots[order[0]] * 4 + slots[order[1]]) * 4 + slots[order[2]]
+
+    def keep(half, stream, chip, rows):
+        z_place, x_place = lax.div(chip, 4), lax.rem(chip, 4)
+        for y_slot in range(4):
+            block = base_of(stream, z_place, x_place, y_slot)
+            first = y_slot * PIECE
+            for unit in range(3):
+                low, high = max(first, OWN * unit), min(first + PIECE, OWN * unit + OWN)
+                if low < high:
+                    parts[half, stream, block, low - first : high - first, :] = rows[
+                        low - OWN * unit : high - OWN * unit, unit * 128 : unit * 128 + 128
+                    ]
+
+    def halving(phase, stream, step):
+        order, pairing = STREAMS[stream]
+        axis = order[step // 2]
+        slots = [slot_of(pairing, at[name]) for name in order]
+        base = 0
+        for level in range(step // 2):
+            base = base + slots[level] * (64 // 4 ** (level + 1))
+        slot = slots[step // 2]
+        side = lax.div(slot, 2) if step % 2 == 0 else slot
+        away = 1 - side if step % 2 == 0 else slot + 1 - 2 * lax.rem(slot, 2)
+        count = BLOCKS[step]
+        kept, sent = base + side * count, base + away * count
+        partner = partner_of(at, axis, pairing if step % 2 == 0 else 1 - pairing)
+        copy = pltpu.make_async_remote_copy(
+            src_ref=parts.at[phase % 2, stream, pl.ds(sent, count)],
+            dst_ref=landed.at[stream, pl.ds(LANDS_AT[step], count)],
+            send_sem=send_sem.at[stream, step],
+            recv_sem=recv_sem.at[stream, step],
+            device_id=partner,
+            device_id_type=MESH,
+        )
+        return copy, kept, partner
+
+    def send(phase, stream, step):
+        copy, _, _ = halving(phase, stream, step)
+        if phase:
+            pl.semaphore_wait(credit.at[stream, step], 1)
+        copy.start()
+
+    def receive(phase, step):
+        for stream in range(6):
+            copy, kept, partner = halving(phase, stream, step)
+            copy.wait()
+            half = phase % 2
+            count = BLOCKS[step]
+            if step < 5:
+
+                def add(block, _):
+                    parts[half, stream, kept + block] += landed[stream, LANDS_AT[step] + block]
+                    return _
+
+                lax.fori_loop(0, count, add, 0, unroll=min(count, 4))
+            else:
+                final[phase, at["y"], stream] = (
+                    parts[half, stream, kept] + landed[stream, LANDS_AT[step]]
+                )
+            if phase < 2:
+                pl.semaphore_signal(
+                    credit.at[stream, step], inc=1, device_id=partner, device_id_type=MESH
+                )
+            if step < 5:
+                send(phase, stream, step + 1)
+
+    def products(phase):
+        half = phase % 2
+        if phase == 0:
+            for third in range(3):
+
+                def pair(chip, _):
+                    rows = jnp.dot(
+                        lhs[chip],
+                        rhs[:, third * 384 : third * 384 + 384],
+                        preferred_element_type=jnp.float32,
+                    )
+                    keep(half, third, chip, rows[0:72])
+                    keep(half, third + 3, chip, rows[72:144])
+                    return _
+
+                lax.fori_loop(0, 16, pair, 0)
+                send(phase, third, 0)
+                send(phase, third + 3, 0)
+            return
+        for stream in range(6):
+            shift = core * 8 if phase == 2 and stream >= 3 else 0
+
+            def duo(pair_at, _):
+                rows = jnp.dot(
+                    lhs[pair_at + shift],
+                    rhs[:, stream * 384 : stream * 384 + 384],
+                    preferred_element_type=jnp.float32,
+                )
+                keep(half, stream, pair_at * 2, rows[0:72])
+                keep(half, stream, pair_at * 2 + 1, rows[72:144])
+                return _
+
+            lax.fori_loop(0, 8, duo, 0)
+            send(phase, stream, 0)
+
+    def ring(phase):
+        return [
+            pltpu.make_async_remote_copy(
+                src_ref=final.at[phase, at["y"]],
+                dst_ref=final.at[phase, at["y"]],
+                send_sem=ring_send.at[phase, hop - 1],
+                recv_sem=ring_recv.at[phase, hop - 1],
+                device_id=device_at({**at, "y": lax.rem(at["y"] + hop, 4)}),
+                device_id_type=MESH,
+            )
+            for hop in (1, 2, 3)
+        ]
+
+    def across(phase):
+        return pltpu.make_async_remote_copy(
+            src_ref=final.at[phase],
+            dst_ref=other.at[phase - 1],
+            send_sem=pair_send.at[phase - 1],
+            recv_sem=pair_recv.at[phase - 1],
+            device_id=sibling,
+            device_id_type=MESH,
+        )
+
+    def whole(get, stream):
+        pairing = STREAMS[stream][1]
+        order = sorted(range(4), key=lambda y_place: slot_of(pairing, y_place))
+        return jnp.concatenate([get(y_place, stream) for y_place in order], axis=0)
+
+    def write_rows(phase, low):
+        for side in range(2):
+            mine = side == (0 if low == 0 else 1)
+            for stream in range(6):
+                if mine:
+                    rows = whole(lambda y_place, stream: final[phase, y_place, stream], stream)
+                else:
+                    rows = whole(lambda y_place, stream: other[phase - 1, y_place, stream], stream)
+                for unit in range(3):
+                    block = rows[OWN * unit + low : OWN * unit + low + 36]
+                    column = side * 18 + stream * 3 + unit
+                    if phase == 1:
+                        out_fc1[:, column * 128 : column * 128 + 128] = block
+                    elif column < 27:
+                        out_qkv[:, column * 128 : column * 128 + 128] = block
+                    else:
+                        out_proj[:, (column - 27) * 128 : (column - 27) * 128 + 128] = block
+
+    def write(phase):
+        if phase == 0:
+            for stream in range(6):
+                rows = whole(lambda y_place, stream: final[0, y_place, stream], stream)
+                half, third = stream // 3, stream % 3
+                for unit in range(3):
+                    column = third * 3 + unit
+                    out_fc2[half * 72 : half * 72 + 72, column * 128 : column * 128 + 128] = rows[
+                        OWN * unit : OWN * unit + 72
+                    ]
+            return
+
+        @pl.when(core == 0)
+        def _():
+            write_rows(phase, 0)
+
+        @pl.when(core == 1)
+        def _():
+            write_rows(phase, 36)
+
+    def ring_start(phase):
+        for copy in ring(phase):
+            copy.start()
+
+    def ring_finish(phase):
+        for copy in ring(phase):
+            copy.wait()
+        if phase:
+            across(phase).start()
+
+    def clear(block, _):
+        for half in range(2):
+            for stream in range(6):
+                z_place, x_place = lax.div(block, 4), lax.rem(block, 4)
+                parts[half, stream, base_of(stream, z_place, x_place, 3), 48:56, :] = jnp.zeros(
+                    (8, 128), jnp.float32
+                )
+        return _
+
+    swap_start(0)
+    lax.fori_loop(0, 16, clear, 0)
+    swap_finish(0)
+    products(0)
+    swap_start(1)
+    swap_finish(1)
+    receive(0, 0)
+    products(1)
+    swap_start(2)
+    swap_finish(2)
+    receive(0, 1)
+    receive(0, 2)
+    receive(0, 3)
+    receive(1, 0)
+    receive(0, 4)
+    receive(0, 5)
+    ring_start(0)
+    products(2)
+    receive(1, 1)
+    receive(1, 2)
+    ring_finish(0)
+    write(0)
+    receive(1, 3)
+    receive(1, 4)
+    receive(2, 0)
+    receive(1, 5)
+    ring_start(1)
+    receive(2, 1)
+    ring_finish(1)
+    receive(2, 2)
+    receive(2, 3)
+    across(1).wait()
+    write(1)
+    receive(2, 4)
+    receive(2, 5)
+    ring_start(2)
+    ring_finish(2)
+    across(2).wait()
+    write(2)
+
+
+def reduce_grads(operands):
+    dma = pltpu.SemaphoreType.DMA
+    regular = pltpu.SemaphoreType.REGULAR
+    vmem = pl.BlockSpec(memory_space=pltpu.VMEM)
+    return pl.pallas_call(
+        grad_kernel,
+        out_shape=(
+            jax.ShapeDtypeStruct((36, 3456), jnp.float32),
+            jax.ShapeDtypeStruct((36, 1152), jnp.float32),
+            jax.ShapeDtypeStruct((36, 4608), jnp.float32),
+            jax.ShapeDtypeStruct((144, 1152), jnp.float32),
+        ),
+        in_specs=[pl.BlockSpec(memory_space=pl.ANY)] * 12,
+        out_specs=(vmem, vmem, vmem, vmem),
+        scratch_shapes=[
+            pltpu.VMEM((2, 6, 64, PIECE, 128), jnp.float32),
+            pltpu.VMEM((6, 63, PIECE, 128), jnp.float32),
+            pltpu.VMEM((16, 144, 512), jnp.bfloat16),
+            pltpu.VMEM((512, 2304), jnp.bfloat16),
+            pltpu.VMEM((16, 144, 256), jnp.float32),
+            pltpu.VMEM((256, 2304), jnp.float32),
+            pltpu.VMEM((3, 4, 6, PIECE, 128), jnp.float32),
+            pltpu.VMEM((2, 4, 6, PIECE, 128), jnp.float32),
+            dma((6, 6)),
+            dma((6, 6)),
+            regular((6, 6)),
+            dma((2,)),
+            dma((2,)),
+            regular,
+            dma((2,)),
+            dma((3, 3)),
+            dma((3, 3)),
+            dma((2,)),
+            dma((2,)),
+        ],
+        compiler_params=pltpu.CompilerParams(
+            collective_id=1, has_side_effects=True, vmem_limit_bytes=60 * 2**20
+        ),
+    )(*operands)
 
 
 def on_device(
@@ -246,22 +683,20 @@
     slice_b_t1 = own_block(grad_b_t1, dp_place, dp_count)
     slice_w_t2 = own_block(grad_w_t2, dp_place, dp_count)
     slice_b_t2 = own_block(grad_b_t2, dp_place, dp_count)
-    term_qkv = weight_term(attn_in, grad_qkv)
-    term_proj = weight_term(mixed_rows, grad_attn)
-    term_fc1 = weight_term(mlp_in, grad_hidden)
-    term_fc2 = weight_term(activated, grad_branch)
-    shard_qkv, shard_proj, shard_fc1, shard_fc2 = (
-        lax.psum_scatter(term_qkv, "dp", scatter_dimension=0, tiled=True),
-        lax.psum_scatter(term_proj, "dp", scatter_dimension=0, tiled=True),
-        lax.psum_scatter(term_fc1, "dp", scatter_dimension=0, tiled=True),
-        lax.psum_scatter(term_fc2, "dp", scatter_dimension=0, tiled=True),
-    )
+    wide = lambda array: array.astype(jnp.float32)
+    act_own = activated.T.reshape(16, 2, 144, row_count).transpose(1, 0, 2, 3)
+    mlp_own = mlp_in.T.reshape(8, 144, row_count)
+    ghid_own = grad_hidden.reshape(row_count, 2, 2304).transpose(1, 0, 2)
+    two_own = jnp.stack([attn_in.T, mixed_rows.T]).reshape(16, 144, row_count)
+    gqkv_own = jnp.stack(
+        [grad_qkv[:, :2304], jnp.concatenate([grad_qkv[:, 2304:], grad_attn], axis=1)]
+    )
+    operands = []
+    for array in (act_own, grad_branch, mlp_own, ghid_own, two_own, gqkv_own):
+        operands += [array, wide(array)]
+    sum_qkv, sum_proj, sum_fc1, sum_fc2 = reduce_grads(operands)
     totals = lax.psum(
         (
-            shard_qkv,
-            shard_proj,
-            shard_fc1,
-            shard_fc2,
             slice_qv,
             slice_proj,
             slice_fc1,
@@ -276,8 +711,7 @@
         ),
         "group",
     )
-    sum_qkv, sum_proj, sum_fc1, sum_fc2 = (totals[0], totals[1], totals[2], totals[3])
-    rest = totals[4:]
+    rest = totals
     return (
         block_out,
         input_grad,

time: 1060 us -> 667 us (0.63)
  blocking collectives: 615 us -> 284 us
  Pallas kernels: 0 us -> 194 us
  waiting for transfers between devices: 115 us -> 0.02 us
  starting transfers between devices: 71 us -> 0.04 us
  local copies, waits for them, and re-layouts: 107 us -> 43.8 us
  matrix products: 119 us -> 90.6 us
  other arithmetic: 6.58 us -> 33.4 us
    unnamed x2 -> x1, blocking collectives: 442 us -> 121 us
    pallas_call x0 -> x1, Pallas kernels: none -> 194 us  [reduce_grads(): pl.pallas_call(grad_kernel, out_shape=(jax.ShapeDtypeStruct((36, 3456), j...]
    unnamed x123 -> x106, local copies, waits for them, and re-layouts: 94 us -> 12.7 us
    unnamed x20 -> x0, starting transfers between devices: 70.9 us -> none
    psum x1, waiting for transfers between devices: 64.2 us -> 0.01 us  [on_device(): lax.psum((slice_qv, slice_proj, slice_fc1, slice_fc2, grad_w_ada, grad_b_...]
    unnamed x22 -> x1, waiting for transfers between devices: 50.5 us -> 0.02 us
    dot_general x4 -> x0, matrix products: 41.9 us -> none  [weight_term(): lax.dot_general(left_op, right_op, (((0,), (0,)), ((), ())), preferred_el...]
    convert_element_type x0 -> x8, other arithmetic: none -> 21.6 us  [the longest x6 13.7 us: on_device(): wide = lambda array: array.astype(jnp.float32)]
  transfers between devices with their start and end apart: 22 -> 1, of which waited for: 4 -> 0; matrix products, arithmetic and copies ran while one was open for 46% -> 7% of each run, Pallas kernels for 0% -> 29%
where the time goes in v1:
time: 667 us; the launch traced here: 663 us
  blocking collectives  284 us (43%)
  Pallas kernels  194 us (29%)
  matrix products  90.6 us (14%)
  local copies, waits for them, and re-layouts  43.8 us (7%)
  other arithmetic  33.4 us (5%)
  between operations  16.9 us (3%)
    pallas_call x1, Pallas kernels, reduce_grads(): pl.pallas_call(grad_kernel, out_shape=(jax.ShapeDtypeStruct((36, 3456), j...  194 us
    psum x1, blocking collectives, on_device(): lax.psum((cond_part, bias_qv, bias_proj, bias_fc1, bias_fc2), 'dp')  124 us
    unnamed x1, blocking collectives  121 us
    all_gather x1, blocking collectives, on_device(): mod_all = lax.all_gather(mod_part, 'dp', axis=1, tiled=True)  26.9 us
    dot_general x1, matrix products, on_device(): grad_act = jnp.dot(grad_branch, w_fc2.T, preferred_element_type=jnp.float32)  18.3 us
    convert_element_type x6, other arithmetic, on_device(): wide = lambda array: array.astype(jnp.float32)  13.7 us
  transfers between devices with their start and end apart: 1, of which 0 were waited for; matrix products, arithmetic and copies ran while one was open for 7% of the time, Pallas kernels for 29%

profile of v1, /device:TPU:1, one launch (start us, length us, event | category | flops | bytes accessed | tf_op | source)
XLA Modules:
  0.0 662.9 jit_solution(2624982239005391370)
XLA Ops:
  7.3 1.4 dynamic_slice.33
  10.8 1.5 convolution_add_fusion.5
  12.3 2.9 convolution_add_fusion.4
  16.0 26.9 %all-gather = f32[32,216,2]{1,2,0:T(2,128)S(1)} all-gather(f32[1,216,2]{1,2,0:T(2,128)S(1)} %fusion.55), channel_id=1, replica_groups=mesh['group'=4,'dp'=32] {'dp'}, dimensions={0}, use_global_device_ids=true | all-gather | bytes 57024 | tf_op jit(solution)/shard_map/all_gather | solution.py:551
  43.7 6.0 fusion.83
  51.7 2.1 copy.75
  53.9 2.1 copy.76
  56.0 2.1 copy.77
  58.1 2.3 fusion.93
  64.6 18.3 %fusion.95 = f32[256,4608]{1,0:T(8,128)S(1)} fusion(bf16[256,1152]{1,0:T(8,128)(2,1)S(1)} %get-tuple-element.60.gbr_own, bf16[4608,1152]{1,0:T(8,128)(2,1)} %param.31), kind=kOutput, calls=%fused_computation.173 | convolution fusion | flops 2717908992 | bytes 15925248 | tf_op jit(solution)/shard_map/dot_general | solution.py:602
  82.9 8.8 %convert_reduce_fusion = (f32[4608]{0:T(1024)S(1)}, bf16[256,4608]{1,0:T(8,128)(2,1)S(1)}, f32[256,4608]{1,0:T(8,128)S(1)}) fusion(f32[256,4608]{1,0:T(8,128)S(1)} %fusion.95, f32[4608]{0:T(1024)S(1)} %copy-done.43, bf16[1152,4608]{1,0:T(8,128)(2,1)} %param.29, f32[256,1152]{1,0:T(8,128)S(1)} %get-tuple-element.68, f32[1152]{0:T(1024)S(1)} %get-tuple-element.34, ...), kind=kOutput, calls=%fused_computation.19 | convolution fusion | flops 2746510848 | bytes 23641088 | tf_op jit(solution)/shard_map/dot_general | solution.py:594
  91.8 8.6 %fusion.96 = f32[256,1152]{1,0:T(8,128)S(1)} fusion(bf16[256,4608]{1,0:T(8,128)(2,1)S(1)} %get-tuple-element.62, bf16[1152,4608]{1,0:T(8,128)(2,1)} %param.29), kind=kOutput, calls=%fused_computation.174 | convolution fusion | flops 2717908992 | bytes 14155776 | tf_op jit(solution)/shard_map/dot_general | solution.py:604
  100.4 1.3 multiply_reduce_fusion.2
  101.7 8.9 %multiply_reduce_fusion.1 = (f32[1152]{0:T(1024)S(1)}, bf16[256,1152]{1,0:T(8,128)(2,1)}, f32[1152]{0:T(1024)S(1)}, f32[256,1152]{1,0:T(8,128)S(1)}) fusion(bf16[256,1152]{1,0:T(8,128)(2,1)S(1)} %copy-done.34, f32[256]{0:T(256)S(1)} %get-tuple-element.65, f32[256,1152]{1,0:T(8,128)S(1)} %get-tuple-element.68, f32[1152]{0:T(1024)S(1)} %get-tuple-element.33, ...), kind=kOutput, calls=%fused_computation.84 | convolution fusion | flops 2733832192 | bytes 21261824 | tf_op jit(solution)/shard_map/dot_general | solution.py:597
  111.9 1.9 convolution_convert_fusion
  113.8 1.3 copy.79
  115.1 4.0 fusion.41
  121.1 1.6 fusion.40
  122.7 1.3 fusion.39
  124.0 1.3 convert_reduce_fusion.3
  125.3 1.3 convert_reduce_fusion.4
  126.7 6.4 fusion.26
  133.1 1.7 fusion.51
  135.2 120.9 %all-reduce = f32[2,6912]{1,0:T(2,128)S(1)} all-reduce(f32[2,6912]{1,0:T(2,128)S(1)} %dynamic_update_slice.4), channel_id=2, replica_groups=mesh['group'=4,'dp'=32] {'dp'}, use_global_device_ids=true, to_apply=%region_30.31.clone | all-reduce | flops 13824 | bytes 110592
  257.7 2.1 fusion.62
  259.8 123.9 %all-reduce.1 = (f32[2304]{0:T(1024)S(1)}, f32[1152]{0:T(1024)S(1)}, f32[4608]{0:T(1024)S(1)}, f32[1152]{0:T(1024)S(1)}, f32[2,1152]{1,0:T(2,128)S(1)}) all-reduce(f32[2304]{0:T(1024)S(1)} %pad_maximum_fusion.2, f32[1152]{0:T(1024)S(1)} %get-tuple-element.63, ...), channel_id=1, replica_groups=mesh['group'=4,'dp'=32] {'dp'}, use_global_device_ids=true, to_apply=%region_13.14 | all-reduce | flops 11520 | bytes 92160 | tf_op jit(solution)/shard_map/psum | solution.py:668
  383.8 7.2 %fusion.79 = f32[1152,1152]{1,0:T(8,128)} fusion(f32[2,1152]{1,0:T(2,128)S(1)} %get-tuple-element.56, f32[2,1152]{1,0:T(2,128)S(1)} %convolution_add_fusion.5), kind=kOutput, calls=%fused_computation.161 | convolution fusion | flops 31859712 | bytes 5326848 | tf_op jit(solution)/shard_map/dot_general | solution.py:27
  390.9 1.3 fusion.58
  392.2 1.6 constant_dynamic-slice_fusion
  393.8 5.3 fusion.14
  399.2 2.4 copy.86
  401.6 2.3 copy.88
  403.9 2.1 copy.92
  406.0 2.1 copy.91
  408.2 2.1 copy.90
  410.3 2.2 fusion.94
  412.5 2.8 copy.83
  415.4 3.6 fusion.85
  419.0 3.0 copy.87
  422.0 2.5 bitcast_convert_fusion.ghid_wide
  426.3 3.5 fusion.87
  433.6 1.6 copy.89
  435.1 1.8 convert_element_type.141.two_wide
  437.0 194.0 %shard_map.323 = (f32[36,3456]{1,0:T(8,128)}, f32[36,1152]{1,0:T(8,128)}, f32[36,4608]{1,0:T(8,128)}, f32[144,1152]{1,0:T(8,128)}) custom-call(bf16[2,16,144,256]{3,2,1,0:T(8,128)(2,1)} %get-tuple-element.74.act_own, f32[2,16,144,256]{3,2,1,0:T(8,128)} %get-tuple-element.73.act_wide, bf16[256,1152]{1,0:T(8,128)(2,1)} %copy-done.9, ...), custom_call_target="tpu_custom_call" | custom-call | tf_op jit(solution)/shard_map/pallas_call | solution.py:473
  632.8 12.3 %all-reduce.2 = (f32[72]{0:T(128)}, f32[36]{0:T(128)}, f32[144]{0:T(256)}, f32[36]{0:T(128)}, f32[216]{0:T(256)}, /*index=5*/f32[8,1152]{1,0:T(8,128)}, f32[36]{0:T(128)}, f32[36]{0:T(128)}) all-reduce(f32[72]{0:T(128)S(1)} %dynamic_slice.34, f32[36]{0:T(128)S(1)} %dynamic_slice.35, ...), channel_id=1, replica_groups=mesh['group'=4,'dp'=32] {'group'}, use_global_device_ids=true, to_apply=%region_14.15 | all-reduce | flops 9792 | bytes 78336 | tf_op jit(solution)/shard_map/psum | solution.py:698
  645.2 2.5 fusion.50
  647.7 2.0 copy.116
  650.4 2.2 copy.118
  (160 shorter events, 24.5 us)
Async XLA Ops:
  7.2 55.6 %copy-start = (bf16[1152,1152]{1,0:T(8,128)(2,1)S(1)}, bf16[1152,1152]{1,0:T(8,128)(2,1)}, u32[]{:S(2)}) copy-start(bf16[1152,1152]{1,0:T(8,128)(2,1)} %param.27) | copy-start | bytes 7962628
  7.2 8.0 %copy-start.41 = (s32[2]{0:T(128)S(1)}, s32[2]{0:T(128)}, u32[]{:S(2)}) copy-start(s32[2]{0:T(128)} %param.23) | copy-start | bytes 28
  7.2 8.3 %copy-start.42 = (f32[216]{0:T(256)S(1)}, f32[216]{0:T(256)}, u32[]{:S(2)}) copy-start(f32[216]{0:T(256)} %param.34) | copy-start | bytes 2596
  7.2 640.5 %all-reduce.6.cloned.1.call-start = ((), (), s32[]{:S(2)}) async-start(), calls=%async_computation | async-start | bytes 3317760 | tf_op jit(solution)/shard_map/psum | solution.py:698
  7.3 7.9 %copy-start.35 = (f32[101,1152]{1,0:T(8,128)S(1)}, f32[101,1152]{1,0:T(8,128)}, u32[]{:S(2)}) copy-start(f32[101,1152]{1,0:T(8,128)} %param.39) | copy-start | bytes 1396228
  7.3 8.2 %copy-start.30 = (bf16[1152,216]{0,1:T(8,128)(2,1)S(1)}, bf16[1152,216]{0,1:T(8,128)(2,1)}, u32[]{:S(2)}) copy-start(bf16[1152,216]{0,1:T(8,128)(2,1)} %param.33) | copy-start | bytes 1492996
  10.8 32.4 %copy-start.5 = (bf16[256,1152]{1,0:T(8,128)(2,1)S(1)}, bf16[256,1152]{1,0:T(8,128)(2,1)}, u32[]{:S(2)}) copy-start(bf16[256,1152]{1,0:T(8,128)(2,1)} %param.20) | copy-start | bytes 1769476
  12.3 31.4 %copy-start.39 = (f32[2304]{0:T(1024)S(1)}, f32[2304]{0:T(1024)}, u32[]{:S(2)}) copy-start(f32[2304]{0:T(1024)} %param.26) | copy-start | bytes 27652
  60.4 2.4 copy-start.2
  60.4 1.5 copy-start.18
  61.9 0.9 copy-start.40
  62.8 1.2 copy-start.17
  62.8 1.5 copy-start.34
  64.6 18.3 %copy-start.9 = (bf16[256,1152]{1,0:T(8,128)(2,1)}, bf16[256,1152]{1,0:T(8,128)(2,1)S(1)}, u32[]{:S(2)}) copy-start(bf16[256,1152]{1,0:T(8,128)(2,1)S(1)} %get-tuple-element.60.gbr_own) | copy-start | bytes 1769476
  64.6 18.3 %copy-start.43 = (f32[4608]{0:T(1024)S(1)}, f32[4608]{0:T(1024)}, u32[]{:S(2)}) copy-start(f32[4608]{0:T(1024)} %param.30) | copy-start | bytes 55300
  91.8 8.6 %copy-start.20 = (bf16[256,4608]{1,0:T(8,128)(2,1)}, bf16[256,4608]{1,0:T(8,128)(2,1)S(1)}, u32[]{:S(2)}) copy-start(bf16[256,4608]{1,0:T(8,128)(2,1)S(1)} %get-tuple-element.62) | copy-start | bytes 7077892
  91.8 9.9 %copy-start.13 = (f32[256,4608]{1,0:T(8,128)}, f32[256,4608]{1,0:T(8,128)S(1)}, u32[]{:S(2)}) copy-start(f32[256,4608]{1,0:T(8,128)S(1)} %get-tuple-element.88) | copy-start | bytes 14155780
  100.4 1.3 copy-start.44
  110.7 1.0 copy-start.14
  110.8 1.1 copy-start.22
  115.1 4.0 copy-start.3
  115.1 4.0 copy-start.19
  120.1 1.1 copy-start.11
  121.1 1.6 copy-start.12
  133.1 257.9 %copy-start.16 = (f32[256,1152]{1,0:T(8,128)}, f32[256,1152]{1,0:T(8,128)S(1)}, u32[]{:S(2)}) copy-start(f32[256,1152]{1,0:T(8,128)S(1)} %fusion.26) | copy-start | bytes 3538948
  133.1 123.0 %copy-start.45 = (u32[128]{0:T(128)S(1)}, u32[128]{0:T(128)}, u32[]{:S(2)}) copy-start(u32[128]{0:T(128)} %constant.113) | copy-start | bytes 1540
  133.1 124.3 %copy-start.31 = (bf16[1152,216]{0,1:T(8,128)(2,1)S(1)}, bf16[1152,216]{0,1:T(8,128)(2,1)}, u32[]{:S(2)}) copy-start(bf16[1152,216]{0,1:T(8,128)(2,1)} %param.33) | copy-start | bytes 1492996
  393.8 5.4 copy-start.21
  401.6 8.6 %copy-start.7 = (bf16[1152,1152]{1,0:T(8,128)(2,1)S(1)}, bf16[1152,1152]{1,0:T(8,128)(2,1)}, u32[]{:S(2)}) copy-start(bf16[1152,1152]{1,0:T(8,128)(2,1)} %param.37) | copy-start | bytes 7962628
  422.0 3.0 copy-start.4
  422.0 3.0 copy-start.23
  422.0 3.0 copy-start.26
  425.0 1.1 copy-start.27
  425.0 1.2 copy-start.28
  426.3 3.5 copy-start.25
  426.3 3.5 copy-start.29
  429.8 1.2 copy-start.10
  429.8 2.3 copy-start.24
  432.4 4.6 copy-start.8
  435.1 1.8 copy-start.6
  437.0 208.2 %copy-start.15 = (f32[256,1152]{1,0:T(8,128)S(1)}, f32[256,1152]{1,0:T(8,128)}, u32[]{:S(2)}) copy-start(f32[256,1152]{1,0:T(8,128)} %copy-done.14) | copy-start | bytes 3538948
  632.8 16.9 %copy-start.38 = (f32[36,1152]{1,0:T(8,128)S(1)}, f32[36,1152]{1,0:T(8,128)}, u32[]{:S(2)}) copy-start(f32[36,1152]{1,0:T(8,128)} %get-tuple-element.116) | copy-start | bytes 497668
  647.7 4.9 copy-start.33
  647.7 5.7 copy-start.32
  650.4 4.0 copy-start.37
  650.4 4.7 copy-start.36
  650.4 5.4 copy-start.1
Sparse Core Ops, SparseCore 0:
  393.9 53.4 all-reduce.5

commit v2 on v1

v2 whole, which is shorter than its diff:
```python
import functools
import math

import jax
import jax.numpy as jnp
from jax import lax
from jax.experimental import pallas as pl
from jax.experimental.pallas import tpu as pltpu
from jax.sharding import PartitionSpec as P

HEADS = 16
SLOTS = 256
ITEM_FRAMES = 16


EPS = 1e-06
NEG = -1e30


def hdot(left_op, right_op):
    return jnp.dot(
        left_op, right_op, precision=lax.Precision.HIGHEST, preferred_element_type=jnp.float32
    )


def hdot_t(left_op, right_op):
    return lax.dot_general(
        left_op,
        right_op,
        (((0,), (0,)), ((), ())),
        precision=lax.Precision.HIGHEST,
        preferred_element_type=jnp.float32,
    )


def weight_term(left_op, right_op):
    return lax.dot_general(
        left_op, right_op, (((0,), (0,)), ((), ())), preferred_element_type=jnp.float32
    )


def norm_rows(matrix):
    row_mean = jnp.mean(matrix, axis=-1, keepdims=True)
    centered = matrix - row_mean
    inv_std = lax.rsqrt(jnp.mean(centered * centered, axis=-1, keepdims=True) + EPS)
    return (centered * inv_std, inv_std)


def norm_back(grad_in, normed, inv_std):
    return inv_std * (
        grad_in
        - jnp.mean(grad_in, axis=-1, keepdims=True)
        - normed * jnp.mean(grad_in * normed, axis=-1, keepdims=True)
    )


def silu_back(pre_vals, grad_in):
    sigmoid = jax.nn.sigmoid(pre_vals)
    return grad_in * sigmoid * (1.0 + pre_vals * (1.0 - sigmoid))


def time_embed(step_ids, width_half):
    frequency = jnp.exp(
        jnp.arange(width_half, dtype=jnp.float32) * (-math.log(10000.0) / width_half)
    )
    angles = step_ids.astype(jnp.float32)[:, None] * frequency[None, :]
    return jnp.concatenate([jnp.cos(angles), jnp.sin(angles)], axis=1)


def own_block(vector, dp_place, dp_count):
    block_rows = vector.shape[0] // dp_count
    return lax.dynamic_slice_in_dim(vector, dp_place * block_rows, block_rows, 0)


def split_three(values):
    high = values.astype(jnp.bfloat16)
    rest = values - high.astype(jnp.float32)
    middle = rest.astype(jnp.bfloat16)
    low = (rest - middle.astype(jnp.float32)).astype(jnp.bfloat16)
    return jnp.concatenate([high, middle, low], axis=0)


def exact_dot(values, weights, contract=0):
    rows = values.shape[0]
    thrice = lax.dot_general(
        split_three(values),
        weights,
        (((1,), (contract,)), ((), ())),
        preferred_element_type=jnp.float32,
    )
    return thrice[0:rows] + thrice[rows : 2 * rows] + thrice[2 * rows : 3 * rows]


def silu(values):
    return values / (1.0 + jnp.exp(-values))


def dot_nn(left, right):
    return jnp.dot(left, right, preferred_element_type=jnp.float32)


def dot_nt(left, right):
    return lax.dot_general(
        left, right, (((1,), (1,)), ((), ())), preferred_element_type=jnp.float32
    )


def dot_tn(left, right):
    return lax.dot_general(
        left, right, (((0,), (0,)), ((), ())), preferred_element_type=jnp.float32
    )


MESH = pl.DeviceIdType.MESH
ORDERS = ((("y", "z", "x"), ("z", "x", "y"), ("x", "y", "z")),) * 3
STREAMS = tuple(
    tuple((order, pairing) for pairing in (0, 1) for order in orders) for orders in ORDERS
)
BLOCKS = (32, 16, 8, 4, 2, 1)
LANDS_AT = (0, 32, 48, 56, 60, 62)
PIECE = 56
OWN = 72
CHUNK = 384
ROWS = 32
WINDOWS = ((0, 216, 3), (54, 72, 2), (72, 36, 2), (81, 144, 3), (117, 36, 2))


def coords():
    place = lax.axis_index("dp")
    return {
        "y": lax.axis_index("group"),
        "z": lax.div(place, 8),
        "x": lax.rem(lax.div(place, 2), 4),
        "core": lax.rem(place, 2),
    }


def device_at(at):
    return (at["y"], (at["z"] * 4 + at["x"]) * 2 + at["core"])


def dp_peer(hop):
    return (lax.axis_index("group"), lax.rem(lax.axis_index("dp") + hop, 32))


def sibling_of(at):
    return device_at({**at, "core": 1 - at["core"]})


def partner_of(at, axis, pairing):
    here = at[axis]
    if pairing == 0:
        there = here + 1 - 2 * lax.rem(here, 2)
    else:
        there = lax.rem(here + 3 + 2 * lax.rem(here, 2), 4)
    return device_at({**at, axis: there})


def slot_of(pairing, value):
    if pairing == 1:
        return value
    if isinstance(value, int):
        return (0, 2, 3, 1)[value]
    return lax.rem(value + lax.div(value + 1, 2), 4)


PACK = 4 * 1152 + 2 * 256 + 128


def backward_kernel(
    act_split,
    act_wide,
    act_flat,
    slope,
    gbr_own,
    gbr_wide,
    mlp_own,
    mlp_wide,
    two_own,
    two_wide,
    heads,
    bias_keys,
    cot,
    resid,
    attn_out,
    tokens,
    mods,
    b_fc2,
    pre_in,
    cond_in,
    feats,
    onehot,
    w_ada,
    w_t2,
    w_qkv,
    w_proj,
    w_fc1,
    w_fc2,
    out_qkv,
    out_proj,
    out_fc1,
    out_fc2,
    block_out,
    input_grad,
    packed,
    sums,
    parts,
    landed,
    lhs,
    rhs,
    stage_lhs,
    stage_rhs,
    leave,
    final,
    other,
    narrow,
    d_mod,
    bias_fc1,
    bias_qv,
    bias_proj,
    bias_fc2,
    flat,
    shares,
    got,
    conds,
    sums_all,
    out_rows,
    in_rows,
    wa,
    wb,
    slope_in,
    act_in,
    grad_t,
    branch,
    grad_resid,
    all_t,
    mixed_t,
    heads_in,
    rows_a,
    rows_b,
    rows_c,
    rows_d,
    send_sem,
    recv_sem,
    credit,
    swap_send,
    swap_recv,
    swap_credit,
    own_sem,
    ring_send,
    ring_recv,
    pair_send,
    pair_recv,
    load_sem,
    row_sem,
    head_sem,
    other_credit,
    out_sem,
    share_send,
    share_recv,
    cond_send,
    cond_recv,
    group_send,
    group_recv,
):
    at = coords()
    core = at["core"]
    sibling = sibling_of(at)
    barrier = pltpu.get_barrier_semaphore()
    place = lax.axis_index("dp")

    def group_peer(hop):
        return (lax.rem(at["y"] + hop, 4), place)

    def hello(hop, _):
        pl.semaphore_signal(barrier, inc=1, device_id=dp_peer(hop), device_id_type=MESH)
        return _

    lax.fori_loop(1, 32, hello, 0)
    for hop in (1, 2, 3):
        pl.semaphore_signal(barrier, inc=1, device_id=group_peer(hop), device_id_type=MESH)
    pl.semaphore_wait(barrier, 34)

    def swap(phase):
        if phase == 0:
            pairs = [
                (act_wide.at[:, 1 - core], stage_lhs),
                (gbr_wide, stage_rhs.at[0:1152]),
            ]
        elif phase == 1:
            pairs = [(mlp_wide, stage_lhs.at[0:8]), (leave, stage_rhs)]
        else:
            pairs = [(two_wide, stage_lhs), (leave, stage_rhs)]
        return [
            pltpu.make_async_remote_copy(
                src_ref=source,
                dst_ref=target,
                send_sem=swap_send.at[place],
                recv_sem=swap_recv.at[place],
                device_id=sibling,
                device_id_type=MESH,
            )
            for place, (source, target) in enumerate(pairs)
        ]

    def own_loads(phase):
        if phase == 0:
            pairs = [
                (act_split.at[:, core], lhs.at[:, :, 0:256]),
                (gbr_own, rhs.at[0:1152, 0:256]),
            ]
        elif phase == 1:
            pairs = [(mlp_own, lhs.at[0:8, :, 0:256])]
        else:
            pairs = [(two_own, lhs.at[:, :, 0:256])]
        return [
            pltpu.make_async_copy(source, target, own_sem.at[place])
            for place, (source, target) in enumerate(pairs)
        ]

    def swap_start(phase):
        if phase:
            pl.semaphore_wait(swap_credit, 1)
        for copy in swap(phase):
            copy.start()

    def swap_finish(phase):
        for copy in own_loads(phase):
            copy.start()
        for copy in swap(phase):
            copy.wait()

        def narrow_lhs(step, _):
            lhs[step, :, 256:512] = stage_lhs[step].astype(jnp.bfloat16)
            return _

        lax.fori_loop(0, 8 if phase == 1 else 16, narrow_lhs, 0)

        def narrow_rhs(step, _):
            rows = pl.ds(pl.multiple_of(step * 144, 144), 144)
            rhs[rows, 256:512] = stage_rhs[rows, :].astype(jnp.bfloat16)
            return _

        lax.fori_loop(0, 8 if phase == 0 else 16, narrow_rhs, 0)
        if phase < 2:
            pl.semaphore_signal(swap_credit, inc=1, device_id=sibling, device_id_type=MESH)
        for copy in own_loads(phase):
            copy.wait()

    def base_of(phase, stream, z_place, x_place, y_slot):
        order, pairing = STREAMS[phase][stream]
        slots = {"y": y_slot, "z": slot_of(pairing, z_place), "x": slot_of(pairing, x_place)}
        return (slots[order[0]] * 4 + slots[order[1]]) * 4 + slots[order[2]]

    def keep(phase, stream, chip, rows):
        half = phase % 2
        z_place, x_place = lax.div(chip, 4), lax.rem(chip, 4)
        for y_slot in range(4):
            block = base_of(phase, stream, z_place, x_place, y_slot)
            first = y_slot * PIECE
            for unit in range(3):
                low, high = max(first, OWN * unit), min(first + PIECE, OWN * unit + OWN)
                if low < high:
                    parts[half, stream, block, low - first : high - first, :] = rows[
                        low - OWN * unit : high - OWN * unit, unit * 128 : unit * 128 + 128
                    ]

    def halving(phase, stream, step):
        order, pairing = STREAMS[phase][stream]
        axis = order[step // 2]
        slots = [slot_of(pairing, at[name]) for name in order]
        base = 0
        for level in range(step // 2):
            base = base + slots[level] * (64 // 4 ** (level + 1))
        slot = slots[step // 2]
        side = lax.div(slot, 2) if step % 2 == 0 else slot
        away = 1 - side if step % 2 == 0 else slot + 1 - 2 * lax.rem(slot, 2)
        count = BLOCKS[step]
        kept, sent = base + side * count, base + away * count
        partner = partner_of(at, axis, pairing if step % 2 == 0 else 1 - pairing)
        source = parts.at[phase % 2, stream]
        if phase == 0 and step >= 3:
            origin = slots[0] * 16 + lax.div(slots[1], 2) * 8
            kept, sent = kept - origin, sent - origin
            source = narrow.at[stream]
        copy = pltpu.make_async_remote_copy(
            src_ref=source.at[pl.ds(sent, count)],
            dst_ref=landed.at[stream, pl.ds(LANDS_AT[step], count)],
            send_sem=send_sem.at[stream, step],
            recv_sem=recv_sem.at[stream, step],
            device_id=partner,
            device_id_type=MESH,
        )
        return copy, kept, partner

    def send(phase, stream, step):
        copy, _, _ = halving(phase, stream, step)
        if phase:
            pl.semaphore_wait(credit.at[stream, step], 1)
        copy.start()

    def receive(phase, step):
        for stream in range(6):
            copy, kept, partner = halving(phase, stream, step)
            copy.wait()
            half = phase % 2
            count = BLOCKS[step]
            late = phase == 0 and step >= 3
            if step < 5:

                def add(block, _):
                    arrived = landed[stream, LANDS_AT[step] + block]
                    if late:
                        narrow[stream, kept + block] += arrived
                    elif phase == 0 and step == 2:
                        narrow[stream, block] = parts[half, stream, kept + block] + arrived
                    else:
                        parts[half, stream, kept + block] += arrived
                    return _

                lax.fori_loop(0, count, add, 0, unroll=min(count, 4))
            else:
                mine = narrow[stream, kept] if late else parts[half, stream, kept]
                final[phase, at["y"], stream] = mine + landed[stream, LANDS_AT[step]]
            if phase < 2:
                pl.semaphore_signal(
                    credit.at[stream, step], inc=1, device_id=partner, device_id_type=MESH
                )
            if step < 5:
                send(phase, stream, step + 1)

    def products(phase):
        together, stacked = (3, 2) if phase == 2 else (2, 4)
        for group in range(6 // together):
            members = range(group * together, (group + 1) * together)
            if phase == 0:
                first = group * together // 2 * CHUNK
                width = together // 2 * CHUNK
                count = 16
            else:
                first = members[0] * CHUNK
                width = together * CHUNK
                count = 8
            shift = core * 8 if phase == 2 and members[0] >= 3 else 0

            def some(step, _):
                left = lhs[pl.ds(step * stacked + shift, stacked)]
                rows = dot_nt(
                    left.reshape(stacked * 144, 512), rhs[first : first + width, :]
                )
                for place in range(stacked):
                    at_row = place * 144
                    if phase == 0:
                        chip = step * stacked + place
                        for third in range(together // 2):
                            column = third * CHUNK
                            block = rows[at_row : at_row + 144, column : column + CHUNK]
                            stream = group * together // 2 + third
                            keep(phase, stream, chip, block[0:72])
                            keep(phase, stream + 3, chip, block[72:144])
                    else:
                        chip = (step * stacked + place) * 2
                        for place_at, stream in enumerate(members):
                            column = place_at * CHUNK
                            block = rows[at_row : at_row + 144, column : column + CHUNK]
                            keep(phase, stream, chip, block[0:72])
                            keep(phase, stream, chip + 1, block[72:144])
                return _

            lax.fori_loop(0, count // stacked, some, 0)
            for member in members:
                stream = member
                if phase == 0:
                    stream = group * together // 2 + (member - members[0]) // 2
                    stream += 3 * ((member - members[0]) % 2)
                send(phase, stream, 0)

    def ring(phase):
        mine = at["y"]
        copies = []
        for place, hop in enumerate((1, 3)):
            copies.append(
                pltpu.make_async_remote_copy(
                    src_ref=final.at[phase, mine],
                    dst_ref=final.at[phase, mine],
                    send_sem=ring_send.at[phase, place],
                    recv_sem=ring_recv.at[phase, place],
                    device_id=device_at({**at, "y": lax.rem(mine + hop, 4)}),
                    device_id_type=MESH,
                )
            )
        return copies

    def relay(phase):
        mine = at["y"]
        copies = []
        for place, hop in enumerate((1, 3)):
            origin = lax.rem(mine + 4 - hop, 4)
            half = pl.ds(place * 3, 3)
            copies.append(
                pltpu.make_async_remote_copy(
                    src_ref=final.at[phase, origin, half],
                    dst_ref=final.at[phase, origin, half],
                    send_sem=ring_send.at[phase, place + 2],
                    recv_sem=ring_recv.at[phase, place + 2],
                    device_id=device_at({**at, "y": lax.rem(mine + hop, 4)}),
                    device_id_type=MESH,
                )
            )
        return copies

    def across(phase):
        return pltpu.make_async_remote_copy(
            src_ref=final.at[phase],
            dst_ref=other,
            send_sem=pair_send.at[phase - 1],
            recv_sem=pair_recv.at[phase - 1],
            device_id=sibling,
            device_id_type=MESH,
        )

    def whole(get, stream):
        pairing = STREAMS[0][stream][1]
        order = sorted(range(4), key=lambda y_place: slot_of(pairing, y_place))
        return jnp.concatenate([get(y_place, stream) for y_place in order], axis=0)

    def write_rows(phase, low):
        for side in range(2):
            mine = side == (0 if low == 0 else 1)
            for stream in range(6):
                if mine:
                    rows = whole(lambda y_place, stream: final[phase, y_place, stream], stream)
                else:
                    rows = whole(lambda y_place, stream: other[y_place, stream], stream)
                for unit in range(3):
                    block = rows[OWN * unit + low : OWN * unit + low + 36]
                    column = side * 18 + stream * 3 + unit
                    if phase == 1:
                        out_fc1[:, column * 128 : column * 128 + 128] = block
                    elif column < 27:
                        out_qkv[:, column * 128 : column * 128 + 128] = block
                    else:
                        out_proj[:, (column - 27) * 128 : (column - 27) * 128 + 128] = block

    def write(phase):
        if phase == 0:
            for stream in range(6):
                rows = whole(lambda y_place, stream: final[0, y_place, stream], stream)
                half, third = stream // 3, stream % 3
                for unit in range(3):
                    column = third * 3 + unit
                    out_fc2[half * 72 : half * 72 + 72, column * 128 : column * 128 + 128] = rows[
                        OWN * unit : OWN * unit + 72
                    ]
            return

        @pl.when(core == 0)
        def _():
            write_rows(phase, 0)

        @pl.when(core == 1)
        def _():
            write_rows(phase, 36)

        if phase == 1:
            pl.semaphore_signal(other_credit, inc=1, device_id=sibling, device_id_type=MESH)

    def ring_start(phase):
        for copy in ring(phase):
            copy.start()

    def ring_relay(phase):
        for copy, onward in zip(ring(phase), relay(phase)):
            copy.wait()
            onward.start()

    def ring_finish(phase):
        for copy in relay(phase):
            copy.wait()
        if phase == 2:
            pl.semaphore_wait(other_credit, 1)
        if phase:
            across(phase).start()

    def clear(chip, _):
        z_place, x_place = lax.div(chip, 4), lax.rem(chip, 4)
        for half in range(2):
            for stream in range(6):
                block = base_of(half, stream, z_place, x_place, 3)
                parts[half, stream, block, 48:56, :] = jnp.zeros((8, 128), jnp.float32)
        return _

    ones = jnp.ones((8, 256), jnp.bfloat16)

    def mlp_loads(chunk):
        slot = lax.rem(chunk, 2)
        rows = pl.ds(pl.multiple_of(chunk * CHUNK, CHUNK), CHUNK)
        return [
            pltpu.make_async_copy(w_fc2.at[rows], wa.at[slot], load_sem.at[0, slot]),
            pltpu.make_async_copy(w_fc1.at[:, rows], wb.at[slot], load_sem.at[1, slot]),
            pltpu.make_async_copy(slope.at[rows], slope_in.at[slot], load_sem.at[2, slot]),
            pltpu.make_async_copy(act_flat.at[rows], act_in.at[slot], load_sem.at[3, slot]),
        ]

    def mlp_begin():
        for copy in mlp_loads(0):
            copy.start()

    def mlp_backward(low, high):
        if low == 0:
            rhs[0:1152, 256:512] = rhs[0:1152, 0:256]
            grad_t[...] = jnp.zeros((1152, 256), jnp.float32)
            branch[...] = jnp.zeros((256, 1152), jnp.float32)

        def chunk_step(chunk, carry):
            slot = lax.rem(chunk, 2)

            @pl.when(chunk < 11)
            def _():
                for copy in mlp_loads(chunk + 1):
                    copy.start()

            for copy in mlp_loads(chunk):
                copy.wait()
            grad_act = dot_nn(wa[slot], rhs[0:1152, 256:512])
            grad_hidden = (grad_act * slope_in[slot].astype(jnp.float32)).astype(jnp.bfloat16)
            side = lax.div(chunk, 6)
            rows = pl.ds(pl.multiple_of(lax.rem(chunk, 6) * CHUNK, CHUNK), CHUNK)

            @pl.when(side == core)
            def _():
                rhs[rows, 0:256] = grad_hidden

            @pl.when(side != core)
            def _():
                leave[rows, :] = grad_hidden.astype(jnp.float32)

            columns = pl.ds(pl.multiple_of(chunk * CHUNK, CHUNK), CHUNK)
            bias_fc1[:, columns] = dot_nt(ones, grad_hidden)[0:1]
            grad_t[...] += dot_nn(wb[slot], grad_hidden)
            branch[...] += dot_tn(act_in[slot], wa[slot])
            return carry

        lax.fori_loop(low, high, chunk_step, 0)

    def row_block(source, index):
        return source.at[pl.ds(pl.multiple_of(index * ROWS, ROWS), ROWS)]

    def norm(values):
        mean = jnp.mean(values, axis=-1, keepdims=True)
        centered = values - mean
        inverse = lax.rsqrt(jnp.mean(centered * centered, axis=-1, keepdims=True) + EPS)
        return centered * inverse, inverse

    def total(values):
        return jnp.sum(values, axis=0, keepdims=True)

    def middle_loads(index):
        slot = lax.rem(index, 2)
        return [
            pltpu.make_async_copy(row_block(source, index), target.at[slot], row_sem.at[place, slot])
            for place, (source, target) in enumerate(
                ((cot, rows_a), (resid, rows_b), (attn_out, rows_c))
            )
        ]

    def token_load(index):
        slot = lax.rem(index, 2)
        return pltpu.make_async_copy(
            row_block(tokens, index), rows_d.at[slot], row_sem.at[3, slot]
        )

    def proj_load(chunk):
        slot = lax.rem(chunk, 2)
        rows = pl.ds(pl.multiple_of(chunk * 288, 288), 288)
        return pltpu.make_async_copy(w_proj.at[rows], wa.at[slot, 0:288], load_sem.at[0, slot])

    def rows_out(kind, index):
        slot = lax.rem(index, 2)
        target = block_out if kind == 0 else input_grad
        buffer = out_rows if kind == 0 else in_rows
        return pltpu.make_async_copy(
            buffer.at[slot], row_block(target, index), out_sem.at[kind, slot]
        )

    def drain(kind):
        rows_out(kind, 256 // ROWS - 2).wait()
        rows_out(kind, 256 // ROWS - 1).wait()

    def middle_begin():
        for copy in middle_loads(0):
            copy.start()
        proj_load(0).start()
        d_mod[...] = jnp.zeros((8, 1152), jnp.float32)
        bias_proj[...] = jnp.zeros((1, 1152), jnp.float32)
        bias_fc2[...] = jnp.zeros((1, 1152), jnp.float32)
        grad_resid[...] = grad_t[...].T

    def middle_rows(low, high):
        scale_mlp, gate_mlp = mods[4:5], mods[5:6]
        gate_attn = mods[2:3]

        def rows_step(index, carry):
            rows = pl.ds(pl.multiple_of(index * ROWS, ROWS), ROWS)
            slot = lax.rem(index, 2)

            @pl.when(index < 256 // ROWS - 1)
            def _():
                for copy in middle_loads(index + 1):
                    copy.start()

            for copy in middle_loads(index):
                copy.wait()

            @pl.when(index >= 2)
            def _():
                rows_out(0, index - 2).wait()

            cotangent, stream_rows = rows_a[slot], rows_b[slot]
            branch_rows = branch[rows, :] + b_fc2[...]
            out_rows[slot] = (stream_rows + gate_mlp * branch_rows).astype(jnp.bfloat16)
            rows_out(0, index).start()
            d_mod[5:6, :] += total(cotangent * branch_rows)
            bias_fc2[...] += total(
                (cotangent * gate_mlp).astype(jnp.bfloat16).astype(jnp.float32)
            )
            normed, inverse = norm(stream_rows)
            grad_in = grad_resid[rows, :]
            d_mod[3:4, :] += total(grad_in)
            d_mod[4:5, :] += total(grad_in * normed)
            back = norm_back(grad_in * (1.0 + scale_mlp), normed, inverse)
            grads = cotangent + back
            grad_resid[rows, :] = grads
            d_mod[2:3, :] += total(grads * rows_c[slot])
            grad_attn = (grads * gate_attn).astype(jnp.bfloat16).astype(jnp.float32)
            bias_proj[...] += total(grad_attn)
            branch[rows, :] = grad_attn
            return carry

        lax.fori_loop(low, high, rows_step, 0)

    def middle_end():
        all_t[3456:4608, :] = branch[...].T.astype(jnp.bfloat16)

        def proj_step(chunk, carry):
            @pl.when(chunk < 3)
            def _():
                proj_load(chunk + 1).start()

            proj_load(chunk).wait()
            grads = dot_nn(wa[lax.rem(chunk, 2), 0:288], all_t[3456:4608, :])
            for head in range(4):
                padded = jnp.concatenate(
                    [grads[head * 72 : head * 72 + 72], jnp.zeros((8, 256), jnp.float32)], axis=0
                )
                mixed_t[chunk * 4 + head] = padded.astype(jnp.bfloat16)
            return carry

        lax.fori_loop(0, 4, proj_step, 0)

    def heads_load(pair_at):
        slot = lax.rem(pair_at, 2)
        return [
            pltpu.make_async_copy(
                heads.at[pl.ds(part * 16 + pair_at * 2, 2)],
                heads_in.at[slot, part],
                head_sem.at[part, slot],
            )
            for part in range(3)
        ]

    def attention_backward(low, high):
        scale = 1.0 / math.sqrt(72)

        def one_head(pair_at, side):
            slot = lax.rem(pair_at, 2)
            query, key, value = (heads_in[slot, part, side] for part in range(3))
            grad_mixed = mixed_t[pair_at * 2 + side]
            scores = dot_tn(key, query) * scale + jnp.concatenate([bias_keys[...]] * 2, axis=1)
            shifted = jnp.exp(scores - jnp.max(scores, axis=0, keepdims=True))
            weights = shifted / jnp.sum(shifted, axis=0, keepdims=True)
            grad_weights = dot_tn(value, grad_mixed)
            row_dot = jnp.sum(weights * grad_weights, axis=0, keepdims=True)
            grad_scores = (weights * (grad_weights - row_dot)).astype(jnp.bfloat16)
            return (
                dot_nn(key, grad_scores)[0:72] * scale,
                dot_nt(query, grad_scores)[0:72] * scale,
                dot_nt(grad_mixed, weights.astype(jnp.bfloat16))[0:72],
            )

        def two_heads(pair_at, carry):
            @pl.when(pair_at < 7)
            def _():
                for copy in heads_load(pair_at + 1):
                    copy.start()

            for copy in heads_load(pair_at):
                copy.wait()
            first, second = one_head(pair_at, 0), one_head(pair_at, 1)
            for part in range(3):
                rows = pl.ds(pl.multiple_of(part * 1152 + pair_at * 144, 16), 144)
                all_t[rows, :] = jnp.concatenate([first[part], second[part]], axis=0).astype(
                    jnp.bfloat16
                )
            return carry

        lax.fori_loop(low, high, two_heads, 0)

    def sides():
        def side(step, _):
            mine = pl.ds(pl.multiple_of(core * 2304 + step * 144, 16), 144)
            theirs = pl.ds(pl.multiple_of((1 - core) * 2304 + step * 144, 16), 144)
            rows = pl.ds(pl.multiple_of(step * 144, 144), 144)
            rhs[rows, 0:256] = all_t[mine, :]
            leave[rows, :] = all_t[theirs, :].astype(jnp.float32)
            return _

        lax.fori_loop(0, 16, side, 0)

    def qkv_load(chunk):
        slot = lax.rem(chunk, 2)
        columns = pl.ds(pl.multiple_of(chunk * CHUNK, CHUNK), CHUNK)
        return pltpu.make_async_copy(w_qkv.at[:, columns], wb.at[slot], load_sem.at[1, slot])

    def last_columns(low, high):
        if low == 0:
            grad_t[...] = jnp.zeros((1152, 256), jnp.float32)
            token_load(0).start()

        def qkv_step(chunk, carry):
            @pl.when(chunk < 8)
            def _():
                qkv_load(chunk + 1).start()

            qkv_load(chunk).wait()
            rows = pl.ds(pl.multiple_of(chunk * CHUNK, CHUNK), CHUNK)
            grads = all_t[rows, :]
            grad_t[...] += dot_nn(wb[lax.rem(chunk, 2)], grads)
            bias_qv[:, rows] = dot_nt(ones, grads)[0:1]
            return carry

        lax.fori_loop(low, high, qkv_step, 0)

    def ada_load():
        return pltpu.make_async_copy(w_ada, wb.at[0, :, 0:256], load_sem.at[1, 0])

    def last_rows():
        ada_load().start()
        branch[...] = grad_t[...].T
        scale_attn = mods[1:2]

        def last_step(index, carry):
            rows = pl.ds(pl.multiple_of(index * ROWS, ROWS), ROWS)
            slot = lax.rem(index, 2)

            @pl.when(index < 256 // ROWS - 1)
            def _():
                token_load(index + 1).start()

            token_load(index).wait()

            @pl.when(index >= 2)
            def _():
                rows_out(1, index - 2).wait()

            normed, inverse = norm(rows_d[slot].astype(jnp.float32))
            grad_in = branch[rows, :]
            d_mod[0:1, :] += total(grad_in)
            d_mod[1:2, :] += total(grad_in * normed)
            back = norm_back(grad_in * (1.0 + scale_attn), normed, inverse)
            in_rows[slot] = (grad_resid[rows, :] + back).astype(jnp.bfloat16)
            rows_out(1, index).start()
            return carry

        lax.fori_loop(0, 256 // ROWS, last_step, 0)

    def share_to(hop):
        return pltpu.make_async_remote_copy(
            src_ref=shares.at[lax.rem(place + hop, 32)],
            dst_ref=got.at[place],
            send_sem=share_send.at[hop],
            recv_sem=share_recv.at[hop],
            device_id=dp_peer(hop),
            device_id_type=MESH,
        )

    def cond_to(hop):
        return pltpu.make_async_remote_copy(
            src_ref=conds.at[place],
            dst_ref=conds.at[place],
            send_sem=cond_send.at[hop],
            recv_sem=cond_recv.at[hop],
            device_id=dp_peer(hop),
            device_id_type=MESH,
        )

    def group_copies(hop):
        return [
            pltpu.make_async_remote_copy(
                src_ref=buffer.at[at["y"]],
                dst_ref=buffer.at[at["y"]],
                send_sem=group_send.at[side, hop],
                recv_sem=group_recv.at[side, hop],
                device_id=group_peer(hop),
                device_id_type=MESH,
            )
            for side, buffer in enumerate((packed, sums_all))
        ]

    def each(make, act):
        def one(hop, _):
            act(make(hop))
            return _

        lax.fori_loop(1, 32, one, 0)

    def tail_share():
        vectors = [d_mod[row : row + 1] for row in range(6)]
        vectors += [bias_qv[0:1, 0:1152], bias_qv[0:1, 2304:3456]]
        vectors += [bias_proj[...], bias_fc1[0:1, :], bias_fc2[...]]
        row = 0
        for vector in vectors:
            for column in range(vector.shape[1] // 128):
                flat[row] = vector[:, column * 128 : column * 128 + 128]
                row += 1
        flat[126] = jnp.zeros((1, 128), jnp.float32)
        flat[127] = jnp.zeros((1, 128), jnp.float32)

        def window(peer, _):
            into = 0
            for first, width, count in WINDOWS:
                start = first + lax.div(peer * width, 128)
                for offset in range(count):
                    shares[peer, into] = flat[start + offset]
                    into += 1
            return _

        lax.fori_loop(0, 32, window, 0)
        got[place] = shares[place]
        each(share_to, lambda copy: copy.start())

    def tail_cond():
        each(share_to, lambda copy: copy.wait())
        first, second = got[0], got[16]
        for source in range(1, 16):
            first = first + got[source]
            second = second + got[16 + source]

        def piece(rows, entry):
            begin = sum(count for _, _, count in WINDOWS[:entry])
            _, width, count = WINDOWS[entry]
            joined = jnp.concatenate([rows[begin + step] for step in range(count)], axis=1)
            joined = jnp.concatenate([joined] * 8, axis=0)
            shift = lax.rem(place * width, 128)
            moved = pltpu.roll(joined, lax.rem(count * 128 - shift, count * 128), 1)
            return moved[0:1]

        d_mod_own = jnp.concatenate([piece(first, 0), piece(second, 0)], axis=0)[:, 0:256]
        ada_load().wait()
        conds[place] = exact_dot(d_mod_own[:, 0:216], wb[0, :, 0:216], 1)
        each(cond_to, lambda copy: copy.start())
        for chunk in range(2):
            t2_load(chunk).start()
        both = first + second
        sums_all[at["y"], 0:1] = piece(both, 1)[:, 0:128]
        sums_all[at["y"], 1:2] = piece(both, 2)[:, 0:128]
        wide = piece(both, 3)
        sums_all[at["y"], 2:3] = wide[:, 0:128]
        sums_all[at["y"], 3:4] = wide[:, 128:256]
        sums_all[at["y"], 4:5] = piece(both, 4)[:, 0:128]
        sums_all[at["y"], 5:8] = jnp.zeros((3, 128), jnp.float32)
        packed[at["y"], :, 2304:3456] = silu(cond_in[...])
        packed[at["y"], :, 3456:4608] = silu(pre_in[...])
        packed[at["y"], :, 4608:4864] = d_mod_own
        packed[at["y"], :, 4864:5120] = feats[...]
        packed[at["y"], :, 5120:5248] = onehot[...]

    def t2_load(chunk):
        rows = pl.ds(chunk * CHUNK, CHUNK)
        return pltpu.make_async_copy(w_t2.at[rows], wa.at[chunk % 2], load_sem.at[0, chunk % 2])

    def tail_group():
        each(cond_to, lambda copy: copy.wait())
        total_cond = conds[0]
        for source in range(1, 32):
            total_cond = total_cond + conds[source]
        grad_cond = silu_back(cond_in[...], total_cond)
        packed[at["y"], :, 0:1152] = grad_cond
        for chunk in range(3):
            t2_load(chunk).wait()
            columns = exact_dot(grad_cond, wa[chunk % 2], 1)
            if chunk == 0:
                t2_load(2).start()
            begin = chunk * CHUNK
            packed[at["y"], :, 1152 + begin : 1152 + begin + CHUNK] = silu_back(
                pre_in[:, begin : begin + CHUNK], columns
            )
        for hop in (1, 2, 3):
            for copy in group_copies(hop):
                copy.start()

    def tail_end():
        for hop in (1, 2, 3):
            for copy in group_copies(hop):
                copy.wait()
        sums[...] = sums_all[0] + sums_all[1] + sums_all[2] + sums_all[3]

    swap_start(0)
    mlp_begin()
    for copy in heads_load(0):
        copy.start()
    lax.fori_loop(0, 16, clear, 0)
    swap_finish(0)
    products(0)
    mlp_backward(0, 4)
    mlp_backward(4, 8)
    mlp_backward(8, 12)
    swap_start(1)
    middle_begin()
    middle_rows(0, 4)
    receive(0, 0)
    middle_rows(4, 8)
    middle_end()
    swap_finish(1)
    products(1)
    qkv_load(0).start()
    attention_backward(0, 4)
    receive(0, 1)
    attention_backward(4, 8)
    sides()
    swap_start(2)
    last_columns(0, 5)
    last_columns(5, 9)
    receive(1, 0)
    swap_finish(2)
    receive(0, 2)
    products(2)
    last_rows()
    tail_share()
    receive(1, 1)
    receive(0, 3)
    tail_cond()
    receive(2, 0)
    receive(1, 2)
    receive(0, 4)
    tail_group()
    receive(2, 1)
    receive(1, 3)
    receive(0, 5)
    ring_start(0)
    receive(2, 2)
    receive(1, 4)
    ring_relay(0)
    receive(2, 3)
    receive(1, 5)
    ring_start(1)
    ring_finish(0)
    write(0)
    tail_end()
    receive(2, 4)
    ring_relay(1)
    receive(2, 5)
    ring_start(2)
    ring_finish(1)
    across(1).wait()
    write(1)
    ring_relay(2)
    drain(0)
    drain(1)
    ring_finish(2)
    across(2).wait()
    write(2)


def backward(operands):
    dma = pltpu.SemaphoreType.DMA
    regular = pltpu.SemaphoreType.REGULAR
    vmem = pl.BlockSpec(memory_space=pltpu.VMEM)
    anywhere = pl.BlockSpec(memory_space=pl.ANY)
    full = jnp.float32
    small = jnp.bfloat16
    return pl.pallas_call(
        backward_kernel,
        out_shape=(
            jax.ShapeDtypeStruct((36, 3456), full),
            jax.ShapeDtypeStruct((36, 1152), full),
            jax.ShapeDtypeStruct((36, 4608), full),
            jax.ShapeDtypeStruct((144, 1152), full),
            jax.ShapeDtypeStruct((256, 1152), small),
            jax.ShapeDtypeStruct((256, 1152), small),
            jax.ShapeDtypeStruct((4, 2, PACK), full),
            jax.ShapeDtypeStruct((8, 128), full),
        ),
        in_specs=[anywhere] * 11 + [vmem] + [anywhere] * 4 + [vmem] * 6 + [anywhere] * 6,
        out_specs=(vmem,) * 4 + (anywhere,) * 2 + (vmem,) * 2,
        scratch_shapes=[
            pltpu.VMEM((2, 6, 64, PIECE, 128), full),
            pltpu.VMEM((6, 63, PIECE, 128), full),
            pltpu.VMEM((16, 144, 512), small),
            pltpu.VMEM((2304, 512), small),
            pltpu.VMEM((16, 144, 256), full),
            pltpu.VMEM((2304, 256), full),
            pltpu.VMEM((2304, 256), full),
            pltpu.VMEM((3, 4, 6, PIECE, 128), full),
            pltpu.VMEM((4, 6, PIECE, 128), full),
            pltpu.VMEM((6, 8, PIECE, 128), full),
            pltpu.VMEM((8, 1152), full),
            pltpu.VMEM((1, 4608), full),
            pltpu.VMEM((1, 3456), full),
            pltpu.VMEM((1, 1152), full),
            pltpu.VMEM((1, 1152), full),
            pltpu.VMEM((128, 1, 128), full),
            pltpu.VMEM((32, 12, 1, 128), full),
            pltpu.VMEM((32, 12, 1, 128), full),
            pltpu.VMEM((32, 2, 1152), full),
            pltpu.VMEM((4, 8, 128), full),
            pltpu.VMEM((2, ROWS, 1152), small),
            pltpu.VMEM((2, ROWS, 1152), small),
            pltpu.VMEM((2, CHUNK, 1152), small),
            pltpu.VMEM((2, 1152, CHUNK), small),
            pltpu.VMEM((2, CHUNK, 256), small),
            pltpu.VMEM((2, CHUNK, 256), small),
            pltpu.VMEM((1152, 256), full),
            pltpu.VMEM((256, 1152), full),
            pltpu.VMEM((256, 1152), full),
            pltpu.VMEM((4608, 256), small),
            pltpu.VMEM((16, 80, 256), small),
            pltpu.VMEM((2, 3, 2, 80, 256), small),
            pltpu.VMEM((2, ROWS, 1152), full),
            pltpu.VMEM((2, ROWS, 1152), full),
            pltpu.VMEM((2, ROWS, 1152), full),
            pltpu.VMEM((2, ROWS, 1152), small),
            dma((6, 6)),
            dma((6, 6)),
            regular((6, 6)),
            dma((2,)),
            dma((2,)),
            regular,
            dma((2,)),
            dma((3, 4)),
            dma((3, 4)),
            dma((2,)),
            dma((2,)),
            dma((4, 2)),
            dma((4, 2)),
            dma((3, 2)),
            regular,
            dma((2, 2)),
            dma((32,)),
            dma((32,)),
            dma((32,)),
            dma((32,)),
            dma((2, 4)),
            dma((2, 4)),
        ],
        compiler_params=pltpu.CompilerParams(
            collective_id=1, has_side_effects=True, vmem_limit_bytes=255 * 2**18
        ),
    )(*operands)


def front_kernel(
    feats, w_t1, b_t1, w_t2, b_t2, rows_table, w_ada, b_ada, pre_out, cond_out, mods, mine, send, recv
):
    place = lax.axis_index("dp")
    barrier = pltpu.get_barrier_semaphore()

    def hello(hop, _):
        pl.semaphore_signal(barrier, inc=1, device_id=dp_peer(hop), device_id_type=MESH)
        return _

    lax.fori_loop(1, 32, hello, 0)
    pre_time = exact_dot(feats[...], w_t1[...]) + b_t1[...]
    condition = exact_dot(silu(pre_time), w_t2[...]) + b_t2[...] + rows_table[...]
    mod_part = exact_dot(silu(condition), w_ada[...]) + b_ada[...]
    pre_out[...] = pre_time
    cond_out[...] = condition
    for item in range(2):
        mine[item, :, 0:216] = mod_part[item : item + 1]
        mine[item, :, 216:256] = jnp.zeros((1, 40), jnp.float32)
    mods[place] = mine[lax.div(place, 16)]
    pl.semaphore_wait(barrier, 31)

    def copy_to(hop):
        target = lax.rem(place + hop, 32)
        return pltpu.make_async_remote_copy(
            src_ref=mine.at[lax.div(target, 16)],
            dst_ref=mods.at[place],
            send_sem=send.at[hop],
            recv_sem=recv.at[hop],
            device_id=dp_peer(hop),
            device_id_type=MESH,
        )

    def begin(hop, _):
        copy_to(hop).start()
        return _

    def finish(hop, _):
        copy_to(hop).wait()
        return _

    lax.fori_loop(1, 32, begin, 0)
    lax.fori_loop(1, 32, finish, 0)


def front(feats, w_t1, b_t1, w_t2, b_t2, rows_table, w_ada, b_ada):
    vmem = pl.BlockSpec(memory_space=pltpu.VMEM)
    width = w_t2.shape[0]
    return pl.pallas_call(
        front_kernel,
        out_shape=(
            jax.ShapeDtypeStruct((2, width), jnp.float32),
            jax.ShapeDtypeStruct((2, width), jnp.float32),
            jax.ShapeDtypeStruct((32, 1, 256), jnp.float32),
        ),
        in_specs=[vmem] * 8,
        out_specs=(vmem, vmem, vmem),
        scratch_shapes=[
            pltpu.VMEM((2, 1, 256), jnp.float32),
            pltpu.SemaphoreType.DMA((32,)),
            pltpu.SemaphoreType.DMA((32,)),
        ],
        compiler_params=pltpu.CompilerParams(
            collective_id=2, has_side_effects=True, vmem_limit_bytes=32 * 2**20
        ),
    )(feats, w_t1, b_t1[None], w_t2, b_t2[None], rows_table, w_ada, b_ada[None])


def on_device(
    tokens,
    out_grad,
    timesteps,
    labels,
    grid_ids,
    w_qkv,
    b_qv,
    w_proj,
    b_proj,
    w_fc1,
    b_fc1,
    w_fc2,
    b_fc2,
    w_ada,
    b_ada,
    w_t1,
    b_t1,
    w_t2,
    b_t2,
    table,
):
    dp_count = lax.axis_size("dp")
    dp_place = lax.axis_index("dp")
    row_count, model_width = tokens.shape
    frame_count = row_count // SLOTS
    head_count = HEADS
    head_dim = model_width // head_count
    score_scale = 1.0 / math.sqrt(head_dim)
    frame_shape = (frame_count, SLOTS, head_count, head_dim)
    time_feats = time_embed(timesteps, w_t1.shape[0] // 2)
    onehot = (labels[:, None] == jnp.arange(128, dtype=jnp.int32)[None, :]).astype(jnp.float32)
    pre_time, condition, mods = front(
        time_feats, w_t1, b_t1, w_t2, b_t2, table[labels], w_ada, b_ada
    )
    item_mod = mods.reshape(32, 256)[:, :216].reshape(6 * model_width)
    own_item = dp_place * frame_count // ITEM_FRAMES
    shift_attn, scale_attn, gate_attn, shift_mlp, scale_mlp, gate_mlp = jnp.split(item_mod, 6)
    grid_value = lax.dynamic_index_in_dim(grid_ids, own_item, 0, keepdims=False)
    first_live = jnp.where(grid_value == 2, SLOTS // 16, 0)
    end_live = jnp.where(grid_value == 1, SLOTS - SLOTS // 16, SLOTS)
    slot_pos = jnp.arange(SLOTS, dtype=jnp.int32)
    valid_keys = (slot_pos >= first_live) & (slot_pos < end_live)
    live_rows = jnp.tile(valid_keys, frame_count).astype(jnp.float32)[:, None]
    token_vals = tokens.astype(jnp.float32)
    normed_one, inv_one = norm_rows(token_vals)
    attn_in = (normed_one * (1.0 + scale_attn) + shift_attn).astype(jnp.bfloat16)
    qkv_rows = jnp.dot(attn_in, w_qkv, preferred_element_type=jnp.float32)
    queries = (
        (qkv_rows[:, :model_width] + b_qv[:model_width]).astype(jnp.bfloat16).reshape(frame_shape)
    )
    key_rows = qkv_rows[:, model_width : 2 * model_width].astype(jnp.bfloat16).reshape(frame_shape)
    values = (
        (qkv_rows[:, 2 * model_width :] + b_qv[model_width:])
        .astype(jnp.bfloat16)
        .reshape(frame_shape)
    )

    def masked_scores():
        raw = (
            jnp.einsum("fqhd,fkhd->fhqk", queries, key_rows, preferred_element_type=jnp.float32)
            * score_scale
        )
        return jnp.where(valid_keys[None, None, None, :], raw, NEG)

    scores = masked_scores()
    row_max = jnp.max(scores, axis=-1, keepdims=True)
    shifted = jnp.exp(scores - row_max)
    row_total = jnp.sum(shifted, axis=-1, keepdims=True)
    log_total = row_max + jnp.log(row_total)
    attn_weights = (shifted / row_total).astype(jnp.bfloat16)
    mixed = jnp.einsum("fhqk,fkhd->fqhd", attn_weights, values, preferred_element_type=jnp.float32)
    mixed_rows = mixed.reshape(row_count, model_width).astype(jnp.bfloat16)
    attn_out = jnp.dot(mixed_rows, w_proj, preferred_element_type=jnp.float32) + b_proj
    resid_one = token_vals + gate_attn * attn_out
    normed_two, inv_two = norm_rows(resid_one)
    mlp_in = (normed_two * (1.0 + scale_mlp) + shift_mlp).astype(jnp.bfloat16)
    hidden = jnp.dot(mlp_in, w_fc1, preferred_element_type=jnp.float32) + b_fc1
    gelu_vals, gelu_pull = jax.vjp(functools.partial(jax.nn.gelu, approximate=True), hidden)
    activated = gelu_vals.astype(jnp.bfloat16)
    slope = gelu_pull(jnp.ones_like(hidden))[0].astype(jnp.bfloat16)
    cotangent = out_grad.astype(jnp.float32) * live_rows
    grad_branch = (cotangent * gate_mlp).astype(jnp.bfloat16)
    act_t = activated.T
    act_split = act_t.reshape(16, 2, 144, row_count)
    gbr_t = grad_branch.T
    mlp_t = mlp_in.T.reshape(8, 144, row_count)
    two_t = jnp.stack([attn_in.T, mixed_rows.T]).reshape(16, 144, row_count)
    heads = jnp.stack([queries, key_rows, values])[:, 0].transpose(0, 2, 3, 1)
    wide = lambda array: array.astype(jnp.float32)
    bias_keys = jnp.broadcast_to(
        jnp.where(valid_keys, 0.0, NEG).astype(jnp.float32)[:, None], (SLOTS, 128)
    )
    mod_rows = jnp.pad(item_mod.reshape(6, model_width), ((0, 2), (0, 0)))
    (
        sum_qkv,
        sum_proj,
        sum_fc1,
        sum_fc2,
        block_out,
        input_grad,
        packs,
        sums,
    ) = backward(
        [
            act_split,
            wide(act_split),
            act_t,
            slope.T,
            gbr_t,
            wide(gbr_t),
            mlp_t,
            wide(mlp_t),
            two_t,
            wide(two_t),
            jnp.pad(heads.reshape(48, head_dim, SLOTS), ((0, 0), (0, 8), (0, 0))),
            bias_keys,
            cotangent,
            resid_one,
            attn_out,
            tokens,
            mod_rows,
            b_fc2[None],
            pre_time,
            condition,
            time_feats,
            onehot,
            jnp.pad(w_ada, ((0, 0), (0, 40))),
            w_t2,
            w_qkv,
            w_proj,
            w_fc1,
            w_fc2,
        ]
    )
    packs = packs.reshape(8, PACK)
    grad_cond, grad_pre = packs[:, 0:1152], packs[:, 1152:2304]
    act_cond, act_time = packs[:, 2304:3456], packs[:, 3456:4608]
    d_mod, feats_all = packs[:, 4608:4824], packs[:, 4864:5120]
    class_rows = packs[:, 5120 : 5120 + table.shape[0]]
    own_time = lax.dynamic_slice_in_dim(act_time, dp_place * 36, 36, 1)
    own_feats = lax.dynamic_slice_in_dim(feats_all, dp_place * 8, 8, 1)
    return (
        block_out,
        input_grad,
        sum_qkv,
        sums[0, 0:72],
        sum_proj,
        sums[1, 0:36],
        sum_fc1,
        sums[2:4].reshape(256)[0:144],
        sum_fc2,
        sums[4, 0:36],
        hdot_t(act_cond, d_mod),
        jnp.sum(d_mod, axis=0),
        hdot_t(own_feats, grad_pre),
        own_block(jnp.sum(grad_pre, axis=0), dp_place, dp_count),
        hdot_t(own_time, grad_cond),
        own_block(jnp.sum(grad_cond, axis=0), dp_place, dp_count),
        hdot_t(class_rows, grad_cond),
    )


def solution(mesh):
    placed = (
        P(("group", "dp"), None),
        P(("group", "dp"), None),
        P("group"),
        P("group"),
        P("group"),
        P(),
        P(),
        P(),
        P(),
        P(),
        P(),
        P(),
        P(),
        P(None, "dp"),
        P("dp"),
        P(),
        P(),
        P(),
        P(),
        P(),
    )
    return jax.shard_map(
        on_device,
        mesh=mesh,
        in_specs=placed,
        out_specs=(
            P(("group", "dp"), None),
            P(("group", "dp"), None),
            P("dp", None),
            P("dp"),
            P("dp", None),
            P("dp"),
            P("dp", None),
            P("dp"),
            P("dp", None),
            P("dp"),
            P(None, "dp"),
            P("dp"),
            P("dp", None),
            P("dp"),
            P("dp", None),
            P("dp"),
            P(),
        ),
        check_vma=False,
    )
```

time: 667 us -> 268 us (0.40)
  blocking collectives: 284 us -> 0 us
  matrix products: 90.6 us -> 30.7 us
  other arithmetic: 33.4 us -> 14.4 us
  between operations: 16.9 us -> 2.52 us
  local copies, waits for them, and re-layouts: 43.8 us -> 32.4 us
  Pallas kernels: 194 us -> 187 us
    psum x2 -> x0, blocking collectives: 136 us -> none  [the longest x1 124 us: on_device(): lax.psum((cond_part, bias_qv, bias_proj, bias_fc1, bias_fc2), 'dp')]
    unnamed x1 -> x0, blocking collectives: 121 us -> none
    dot_general x16 -> x0, matrix products: 62 us -> none  [the longest x1 18.3 us: on_device(): grad_act = jnp.dot(grad_branch, w_fc2.T, preferred_element_type=jnp.float32)]
    all_gather x1 -> x0, blocking collectives: 26.9 us -> none  [on_device(): mod_all = lax.all_gather(mod_part, 'dp', axis=1, tiled=True)]
    convert_element_type x3 -> x1, other arithmetic: 8.91 us -> 0.63 us  [on_device(): (labels[:, None] == jnp.arange(128, dtype=jnp.int32)[None, :]).astype(jnp...]
    convert_element_type x6 -> x3, other arithmetic: 13.7 us -> 5.67 us  [on_device(): wide = lambda array: array.astype(jnp.float32)]
    reshape x4 -> x3, local copies, waits for them, and re-layouts: 9.42 us -> 1.76 us  [the longest x1 1.09 us: on_device(): packs = packs.reshape(8, PACK)]
    pallas_call x1 -> x2, Pallas kernels: 194 us -> 187 us  [the longest x1 174 us: backward(): pl.pallas_call(backward_kernel, out_shape=(jax.ShapeDtypeStruct((36, 3456...]
  transfers between devices with their start and end apart: 1 -> 0, of which waited for: 0 -> 0; matrix products, arithmetic and copies ran while one was open for 7% -> 0% of each run, Pallas kernels for 29% -> 0%
where the time goes in v2:
time: 268 us; the launch traced here: 267 us
  Pallas kernels  187 us (70%)
  local copies, waits for them, and re-layouts  32.4 us (12%)
  matrix products  30.7 us (11%)
  other arithmetic  14.4 us (5%)
    pallas_call x1, Pallas kernels, backward(): pl.pallas_call(backward_kernel, out_shape=(jax.ShapeDtypeStruct((36, 3456...  174 us
    pallas_call x1, Pallas kernels, front(): pl.pallas_call(front_kernel, out_shape=(jax.ShapeDtypeStruct((2, width),...  12.3 us
    unnamed x102, local copies, waits for them, and re-layouts  12 us
    dot_general x1, matrix products, on_device(): hidden = jnp.dot(mlp_in, w_fc1, preferred_element_type=jnp.float32) + b_fc1  11 us
    dot_general x1, matrix products, on_device(): qkv_rows = jnp.dot(attn_in, w_qkv, preferred_element_type=jnp.float32)  6 us
    convert_element_type x3, other arithmetic, on_device(): wide = lambda array: array.astype(jnp.float32)  5.67 us
    dot_general x4, matrix products, hdot_t(): lax.dot_general(left_op, right_op, (((0,), (0,)), ((), ())), precision=la...  5.44 us

profile of v2, /device:TPU:1, one launch (start us, length us, event | category | flops | bytes accessed | tf_op | source)
XLA Modules:
  0.0 266.6 jit_solution(14310044923503384559)
XLA Ops:
  0.7 1.3 dynamic_slice.16
  3.8 0.7 convert_element_type.78
  4.6 1.3 copy.52.w_ada
  5.9 0.7 compare_select_fusion
  6.6 1.6 gather_fusion
  8.3 1.7 copy-done
  10.0 12.3 %shard_map.323 = (f32[2,1152]{1,0:T(2,128)S(1)}, f32[2,1152]{1,0:T(2,128)S(1)}, f32[32,1,256]{2,1,0:T(1,128)S(1)}) custom-call(f32[2,256]{1,0:T(2,128)S(1)} %pad_maximum_fusion.2.feats, bf16[256,1152]{1,0:T(8,128)(2,1)S(1)} %copy-done.1, f32[1,1152]{1,0:T(1,128)S(1)} %broadcast_in_dim.30.b_t1, bf16[1152,1152]{1,0:T(8,128)(2,1)S(1)} %copy-done, ...), custom_call_target="tpu_custom_call" | custom-call | tf_op jit(solution)/shard_map/pallas_call | solution.py:1210
  22.3 0.6 copy-done.3
  23.0 0.6 fusion.47
  24.7 6.0 %fusion.43 = f32[256,3456]{1,0:T(8,128)S(1)} fusion(bf16[1152,3456]{1,0:T(8,128)(2,1)} %w_qkv.1, bf16[256,1152]{1,0:T(8,128)(2,1)S(1)} %copy-done.9, f32[1152]{0:T(1024)S(1)} %get-tuple-element.56, f32[1152]{0:T(1024)S(1)} %get-tuple-element.57, f32[256]{0:T(256)S(1)} %add_rsqrt_fusion.1, f32[256]{0:T(256)S(1)} %broadcast_multiply_fusion.1), kind=kOutput, calls=%fused_computation.86 | convolution fusion | flops 2040201216 | bytes 12102656 | tf_op jit(solution)/shard_map/dot_general | solution.py:1277
  30.9 1.5 copy-done.13
  32.7 1.3 slice.112
  34.3 4.3 %fusion.49 = (f32[16,256]{1,0:T(8,128)S(1)}, f32[16,256,256]{1,2,0:T(8,128)}) fusion(pred[256]{0:T(512)(128)(4,1)} %get-tuple-element.42, bf16[256,16,72]{0,2,1:T(8,128)(2,1)S(1)} %bitcast.65, bf16[256,16,72]{0,2,1:T(8,128)(2,1)S(1)} %bitcast.67), kind=kOutput, calls=%fused_computation.91 | convolution fusion | flops 155189504 | bytes 5390592 | tf_op jit(solution)/shard_map/sub | solution.py:1297
  39.0 2.9 %fusion.16 = bf16[16,72,256]{2,1,0:T(8,128)(2,1)S(1)} fusion(bf16[256,16,72]{0,2,1:T(8,128)(2,1)S(1)} %bitcast.69, f32[16,256,256]{1,2,0:T(8,128)} %get-tuple-element.66, f32[16,256]{1,0:T(8,128)S(1)} %get-tuple-element.65), kind=kOutput, calls=%fused_computation.29 | convolution fusion | flops 153387008 | bytes 5390336 | tf_op jit(solution)/shard_map/fhqk,fkhd->fqhd/dot_general | solution.py:1301
  42.2 1.0 convolution_add_fusion.1.attn_out
  43.3 1.1 fusion.46
  44.4 1.8 copy.59
  46.2 1.2 pad_maximum_fusion.1
  47.3 1.6 copy.60
  48.9 1.7 convert_element_type.96.two_wide
  51.7 1.6 convert_multiply_fusion
  53.4 1.3 copy.58
  54.7 1.2 convert_element_type.95.mlp_wide
  55.9 1.3 copy.66.gbr_wide
  57.2 1.1 copy.65.gbr_own
  58.2 11.0 %fusion.8 = (bf16[4608,256]{1,0:T(8,128)(2,1)}, bf16[4608,256]{1,0:T(8,128)(2,1)S(1)}) fusion(f32[4608]{0:T(1024)} %param.30, bf16[1152,4608]{1,0:T(8,128)(2,1)} %w_fc1.1, f32[256,1152]{1,0:T(8,128)S(1)} %get-tuple-element.44.resid, f32[1152]{0:T(1024)S(1)} %get-tuple-element.54, f32[1152]{0:T(1024)} %get-tuple-element.55, f32[256]{0:T(256)} %copy-done.42, ...), kind=kOutput, calls=%fused_computation.12 | convolution fusion | flops 2744156160 | bytes 16544768 | tf_op jit(solution)/shard_map/dot_general | solution.py:1307
  69.2 2.7 %convert_element_type.89.act_wide = f32[16,2,144,256]{3,2,1,0:T(8,128)} convert(bf16[16,2,144,256]{3,2,1,0:T(8,128)(2,1)S(1)} %bitcast.58) | non-fusion elementwise | flops 1179648 | bytes 7077888 | tf_op jit(solution)/shard_map/convert_element_type | solution.py:1319
  72.2 0.8 broadcast_in_dim.40.bias_keys
  73.2 1.5 pad.12.heads
  74.8 0.6 pad.13.mods
  75.4 0.9 pad.14.w_ada
  76.3 0.6 broadcast_in_dim.41.b_fc2
  76.9 0.6 compare_convert_fusion.onehot
  77.5 174.3 %shard_map.324 = (f32[36,3456]{1,0:T(8,128)}, f32[36,1152]{1,0:T(8,128)}, f32[36,4608]{1,0:T(8,128)}, f32[144,1152]{1,0:T(8,128)}, bf16[256,1152]{1,0:T(8,128)(2...) custom-call(bf16[16,2,144,256]{3,2,1,0:T(8,128)(2,1)} %bitcast.59, ...), custom_call_target="tpu_custom_call" | custom-call | tf_op jit(solution)/shard_map/pallas_call | solution.py:1082
  251.9 1.1 reshape.177
  253.0 1.1 fusion.32
  254.1 0.9 fusion.28
  255.0 2.0 fusion.26
  257.1 1.4 fusion.30
  258.5 0.6 dynamic_slice.18
  259.0 0.6 dynamic_slice.20
  259.6 0.6 slice_reduce_fusion.2
  261.8 0.8 copy.78
  262.6 0.8 copy.79
  263.4 0.8 copy.80
  264.3 0.7 copy.81
  264.9 0.9 copy.82
  265.8 0.8 copy.83
  (120 shorter events, 6.4 us)
Async XLA Ops:
  0.7 7.5 %copy-start.36 = (f32[1152]{0:T(1024)S(1)}, f32[1152]{0:T(1024)}, u32[]{:S(2)}) copy-start(f32[1152]{0:T(1024)} %param.36) | copy-start | bytes 13828
  0.7 7.5 %copy-start.37 = (f32[1152]{0:T(1024)S(1)}, f32[1152]{0:T(1024)}, u32[]{:S(2)}) copy-start(f32[1152]{0:T(1024)} %param.38) | copy-start | bytes 13828
  0.7 7.5 %copy-start.5 = (f32[216]{0:T(256)S(1)}, f32[216]{0:T(256)}, u32[]{:S(2)}) copy-start(f32[216]{0:T(256)} %param.34) | copy-start | bytes 2596
  0.7 7.5 %copy-start.1 = (bf16[256,1152]{1,0:T(8,128)(2,1)S(1)}, bf16[256,1152]{1,0:T(8,128)(2,1)}, u32[]{:S(2)}) copy-start(bf16[256,1152]{1,0:T(8,128)(2,1)} %w_t1.1) | copy-start | bytes 1769476
  4.6 17.7 %copy-start.2 = (f32[2,256]{1,0:T(2,128)}, f32[2,256]{1,0:T(2,128)S(1)}, u32[]{:S(2)}) copy-start(f32[2,256]{1,0:T(2,128)S(1)} %pad_maximum_fusion.2.feats) | copy-start | bytes 6148
  8.2 1.8 copy-start
  10.0 13.6 %copy-start.9 = (bf16[256,1152]{1,0:T(8,128)(2,1)S(1)}, bf16[256,1152]{1,0:T(8,128)(2,1)}, u32[]{:S(2)}) copy-start(bf16[256,1152]{1,0:T(8,128)(2,1)} %tokens.1) | copy-start | bytes 1769476
  22.3 0.6 copy-start.3
  22.3 0.6 copy-start.4
  22.9 7.8 %copy-start.25 = (f32[32,1,256]{2,0,1:T(8,128)}, f32[32,1,256]{2,0,1:T(8,128)S(1)}, u32[]{:S(2)}) copy-start(f32[32,1,256]{2,0,1:T(8,128)S(1)} %copy.71) | copy-start | bytes 98308
  23.6 7.1 %copy-start.30 = (f32[1152]{0:T(1024)}, f32[1152]{0:T(1024)S(1)}, u32[]{:S(2)}) copy-start(f32[1152]{0:T(1024)S(1)} %get-tuple-element.56) | copy-start | bytes 13828
  23.6 7.1 %copy-start.32 = (f32[1152]{0:T(1024)}, f32[1152]{0:T(1024)S(1)}, u32[]{:S(2)}) copy-start(f32[1152]{0:T(1024)S(1)} %get-tuple-element.57) | copy-start | bytes 13828
  24.1 0.6 copy-start.39
  24.7 6.0 %copy-start.35 = (f32[2304]{0:T(1024)S(1)}, f32[2304]{0:T(1024)}, u32[]{:S(2)}) copy-start(f32[2304]{0:T(1024)} %param.26) | copy-start | bytes 27652
  30.7 1.7 copy-start.13
  34.3 4.4 %copy-start.14 = (bf16[256,1152]{0,1:T(8,128)(2,1)}, bf16[256,1152]{0,1:T(8,128)(2,1)S(1)}, u32[]{:S(2)}) copy-start(bf16[256,1152]{0,1:T(8,128)(2,1)S(1)} %copy.55) | copy-start | bytes 1769476
  38.9 3.0 %copy-start.16 = (bf16[256,1152]{0,1:T(8,128)(2,1)}, bf16[256,1152]{0,1:T(8,128)(2,1)S(1)}, u32[]{:S(2)}) copy-start(bf16[256,1152]{0,1:T(8,128)(2,1)S(1)} %copy.53) | copy-start | bytes 1769476
  39.0 3.2 %copy-start.12 = (bf16[1152,1152]{1,0:T(8,128)(2,1)S(1)}, bf16[1152,1152]{1,0:T(8,128)(2,1)}, u32[]{:S(2)}) copy-start(bf16[1152,1152]{1,0:T(8,128)(2,1)} %w_proj.1) | copy-start | bytes 7962628
  39.0 3.2 %copy-start.45 = (f32[1152]{0:T(1024)S(1)}, f32[1152]{0:T(1024)}, u32[]{:S(2)}) copy-start(f32[1152]{0:T(1024)} %param.28) | copy-start | bytes 13828
  41.9 1.3 copy-start.22
  42.2 1.1 copy-start.31
  42.2 1.1 copy-start.33
  42.2 1.1 copy-start.34
  42.2 1.1 copy-start.40
  43.3 1.1 copy-start.11
  44.4 13.8 %copy-start.7 = (f32[256,1152]{1,0:T(8,128)}, f32[256,1152]{1,0:T(8,128)S(1)}, u32[]{:S(2)}) copy-start(f32[256,1152]{1,0:T(8,128)S(1)} %get-tuple-element.44.resid) | copy-start | bytes 3538948
  48.9 1.8 copy-start.8
  48.9 1.8 copy-start.41
  50.7 0.7 copy-start.44
  50.7 1.1 copy-start.23
  50.7 1.1 copy-start.28
  50.7 1.1 copy-start.29
  51.3 2.0 copy-start.42
  54.7 2.5 copy-start.10
  69.2 3.0 %copy-start.6 = (bf16[4608,256]{1,0:T(8,128)(2,1)}, bf16[4608,256]{1,0:T(8,128)(2,1)S(1)}, u32[]{:S(2)}) copy-start(bf16[4608,256]{1,0:T(8,128)(2,1)S(1)} %get-tuple-element.46.act_flat) | copy-start | bytes 7077892
  69.2 3.8 %copy-start.15 = (bf16[256,1152]{0,1:T(8,128)(2,1)S(1)}, bf16[256,1152]{0,1:T(8,128)(2,1)}, u32[]{:S(2)}) copy-start(bf16[256,1152]{0,1:T(8,128)(2,1)} %copy-done.14) | copy-start | bytes 1769476
  69.2 3.8 %copy-start.17 = (bf16[256,1152]{0,1:T(8,128)(2,1)S(1)}, bf16[256,1152]{0,1:T(8,128)(2,1)}, u32[]{:S(2)}) copy-start(bf16[256,1152]{0,1:T(8,128)(2,1)} %copy-done.16) | copy-start | bytes 1769476
  73.2 1.5 copy-start.26
  74.7 1.6 copy-start.38
  74.7 2.2 copy-start.46
  251.9 8.4 %copy-start.43 = (f32[8,128]{1,0:T(8,128)S(1)}, f32[8,128]{1,0:T(8,128)}, u32[]{:S(2)}) copy-start(f32[8,128]{1,0:T(8,128)} %get-tuple-element.34) | copy-start | bytes 12292
  251.9 9.9 %copy-start.21 = (bf16[256,1152]{1,0:T(8,128)(2,1)S(1)}, bf16[256,1152]{1,0:T(8,128)(2,1)}, u32[]{:S(2)}) copy-start(bf16[256,1152]{1,0:T(8,128)(2,1)} %get-tuple-element.85) | copy-start | bytes 1769476
  255.0 7.6 %copy-start.20 = (bf16[256,1152]{1,0:T(8,128)(2,1)S(1)}, bf16[256,1152]{1,0:T(8,128)(2,1)}, u32[]{:S(2)}) copy-start(bf16[256,1152]{1,0:T(8,128)(2,1)} %get-tuple-element.86) | copy-start | bytes 1769476
  261.8 1.6 copy-start.24
  262.6 1.6 copy-start.27
  262.6 2.3 copy-start.18
  264.2 1.5 copy-start.19

commit v3 on v2

--- a/solution.py
+++ b/solution.py
@@ -1,4 +1,3 @@
-import functools
 import math
 
 import jax
@@ -8,19 +7,12 @@
 from jax.experimental.pallas import tpu as pltpu
 from jax.sharding import PartitionSpec as P
 
-HEADS = 16
 SLOTS = 256
 ITEM_FRAMES = 16
 
 
 EPS = 1e-06
 NEG = -1e30
-
-
-def hdot(left_op, right_op):
-    return jnp.dot(
-        left_op, right_op, precision=lax.Precision.HIGHEST, preferred_element_type=jnp.float32
-    )
 
 
 def hdot_t(left_op, right_op):
@@ -31,19 +23,6 @@
         precision=lax.Precision.HIGHEST,
         preferred_element_type=jnp.float32,
     )
-
-
-def weight_term(left_op, right_op):
-    return lax.dot_general(
-        left_op, right_op, (((0,), (0,)), ((), ())), preferred_element_type=jnp.float32
-    )
-
-
-def norm_rows(matrix):
-    row_mean = jnp.mean(matrix, axis=-1, keepdims=True)
-    centered = matrix - row_mean
-    inv_std = lax.rsqrt(jnp.mean(centered * centered, axis=-1, keepdims=True) + EPS)
-    return (centered * inv_std, inv_std)
 
 
 def norm_back(grad_in, normed, inv_std):
@@ -168,16 +147,12 @@
 
 
 def backward_kernel(
-    act_split,
-    act_wide,
+    lhs_zero,
+    lhs_one,
+    lhs_two,
+    rhs_zero,
     act_flat,
     slope,
-    gbr_own,
-    gbr_wide,
-    mlp_own,
-    mlp_wide,
-    two_own,
-    two_wide,
     heads,
     bias_keys,
     cot,
@@ -208,7 +183,6 @@
     landed,
     lhs,
     rhs,
-    stage_lhs,
     stage_rhs,
     leave,
     final,
@@ -279,73 +253,42 @@
     lax.fori_loop(1, 32, hello, 0)
     for hop in (1, 2, 3):
         pl.semaphore_signal(barrier, inc=1, device_id=group_peer(hop), device_id_type=MESH)
-    pl.semaphore_wait(barrier, 34)
-
-    def swap(phase):
-        if phase == 0:
-            pairs = [
-                (act_wide.at[:, 1 - core], stage_lhs),
-                (gbr_wide, stage_rhs.at[0:1152]),
-            ]
-        elif phase == 1:
-            pairs = [(mlp_wide, stage_lhs.at[0:8]), (leave, stage_rhs)]
-        else:
-            pairs = [(two_wide, stage_lhs), (leave, stage_rhs)]
-        return [
-            pltpu.make_async_remote_copy(
-                src_ref=source,
-                dst_ref=target,
-                send_sem=swap_send.at[place],
-                recv_sem=swap_recv.at[place],
-                device_id=sibling,
-                device_id_type=MESH,
-            )
-            for place, (source, target) in enumerate(pairs)
-        ]
-
-    def own_loads(phase):
-        if phase == 0:
-            pairs = [
-                (act_split.at[:, core], lhs.at[:, :, 0:256]),
-                (gbr_own, rhs.at[0:1152, 0:256]),
-            ]
-        elif phase == 1:
-            pairs = [(mlp_own, lhs.at[0:8, :, 0:256])]
-        else:
-            pairs = [(two_own, lhs.at[:, :, 0:256])]
-        return [
-            pltpu.make_async_copy(source, target, own_sem.at[place])
-            for place, (source, target) in enumerate(pairs)
-        ]
+    def swap():
+        return pltpu.make_async_remote_copy(
+            src_ref=leave,
+            dst_ref=stage_rhs,
+            send_sem=swap_send,
+            recv_sem=swap_recv,
+            device_id=sibling,
+            device_id_type=MESH,
+        )
+
+    def lhs_load(phase):
+        source = (lhs_zero, lhs_one, lhs_two)[phase]
+        target = lhs.at[0:8] if phase == 1 else lhs
+        return pltpu.make_async_copy(source, target, own_sem.at[0])
+
+    def rhs_load():
+        return pltpu.make_async_copy(rhs_zero, rhs.at[0:1152], own_sem.at[1])
 
     def swap_start(phase):
-        if phase:
+        lhs_load(phase).start()
+        if phase == 2:
             pl.semaphore_wait(swap_credit, 1)
-        for copy in swap(phase):
-            copy.start()
+        swap().start()
 
     def swap_finish(phase):
-        for copy in own_loads(phase):
-            copy.start()
-        for copy in swap(phase):
-            copy.wait()
-
-        def narrow_lhs(step, _):
-            lhs[step, :, 256:512] = stage_lhs[step].astype(jnp.bfloat16)
-            return _
-
-        lax.fori_loop(0, 8 if phase == 1 else 16, narrow_lhs, 0)
+        swap().wait()
 
         def narrow_rhs(step, _):
             rows = pl.ds(pl.multiple_of(step * 144, 144), 144)
             rhs[rows, 256:512] = stage_rhs[rows, :].astype(jnp.bfloat16)
             return _
 
-        lax.fori_loop(0, 8 if phase == 0 else 16, narrow_rhs, 0)
-        if phase < 2:
+        lax.fori_loop(0, 16, narrow_rhs, 0)
+        if phase == 1:
             pl.semaphore_signal(swap_credit, inc=1, device_id=sibling, device_id_type=MESH)
-        for copy in own_loads(phase):
-            copy.wait()
+        lhs_load(phase).wait()
 
     def base_of(phase, stream, z_place, x_place, y_slot):
         order, pairing = STREAMS[phase][stream]
@@ -599,8 +542,38 @@
             pltpu.make_async_copy(w_fc2.at[rows], wa.at[slot], load_sem.at[0, slot]),
             pltpu.make_async_copy(w_fc1.at[:, rows], wb.at[slot], load_sem.at[1, slot]),
             pltpu.make_async_copy(slope.at[rows], slope_in.at[slot], load_sem.at[2, slot]),
+        ]
+
+    def branch_loads(chunk):
+        slot = lax.rem(chunk, 2)
+        rows = pl.ds(pl.multiple_of(chunk * CHUNK, CHUNK), CHUNK)
+        return [
+            pltpu.make_async_copy(w_fc2.at[rows], wa.at[slot], load_sem.at[0, slot]),
             pltpu.make_async_copy(act_flat.at[rows], act_in.at[slot], load_sem.at[3, slot]),
         ]
+
+    def branch_begin():
+        for copy in branch_loads(0):
+            copy.start()
+
+    def branch_forward(low, high):
+        if low == 0:
+            branch[...] = jnp.zeros((256, 1152), jnp.float32)
+
+        def branch_step(chunk, carry):
+            slot = lax.rem(chunk, 2)
+
+            @pl.when(chunk < 11)
+            def _():
+                for copy in branch_loads(chunk + 1):
+                    copy.start()
+
+            for copy in branch_loads(chunk):
+                copy.wait()
+            branch[...] += dot_tn(act_in[slot], wa[slot])
+            return carry
+
+        lax.fori_loop(low, high, branch_step, 0)
 
     def mlp_begin():
         for copy in mlp_loads(0):
@@ -610,7 +583,6 @@
         if low == 0:
             rhs[0:1152, 256:512] = rhs[0:1152, 0:256]
             grad_t[...] = jnp.zeros((1152, 256), jnp.float32)
-            branch[...] = jnp.zeros((256, 1152), jnp.float32)
 
         def chunk_step(chunk, carry):
             slot = lax.rem(chunk, 2)
@@ -638,7 +610,6 @@
             columns = pl.ds(pl.multiple_of(chunk * CHUNK, CHUNK), CHUNK)
             bias_fc1[:, columns] = dot_nt(ones, grad_hidden)[0:1]
             grad_t[...] += dot_nn(wb[slot], grad_hidden)
-            branch[...] += dot_tn(act_in[slot], wa[slot])
             return carry
 
         lax.fori_loop(low, high, chunk_step, 0)
@@ -697,8 +668,7 @@
         grad_resid[...] = grad_t[...].T
 
     def middle_rows(low, high):
-        scale_mlp, gate_mlp = mods[4:5], mods[5:6]
-        gate_attn = mods[2:3]
+        scale_mlp, gate_attn = mods[4:5], mods[2:3]
 
         def rows_step(index, carry):
             rows = pl.ds(pl.multiple_of(index * ROWS, ROWS), ROWS)
@@ -712,18 +682,7 @@
             for copy in middle_loads(index):
                 copy.wait()
 
-            @pl.when(index >= 2)
-            def _():
-                rows_out(0, index - 2).wait()
-
             cotangent, stream_rows = rows_a[slot], rows_b[slot]
-            branch_rows = branch[rows, :] + b_fc2[...]
-            out_rows[slot] = (stream_rows + gate_mlp * branch_rows).astype(jnp.bfloat16)
-            rows_out(0, index).start()
-            d_mod[5:6, :] += total(cotangent * branch_rows)
-            bias_fc2[...] += total(
-                (cotangent * gate_mlp).astype(jnp.bfloat16).astype(jnp.float32)
-            )
             normed, inverse = norm(stream_rows)
             grad_in = grad_resid[rows, :]
             d_mod[3:4, :] += total(grad_in)
@@ -738,6 +697,41 @@
             return carry
 
         lax.fori_loop(low, high, rows_step, 0)
+
+    def finish_begin():
+        for copy in middle_loads(0)[0:2]:
+            copy.start()
+
+    def finish_rows():
+        gate_mlp = mods[5:6]
+
+        def finish_step(index, carry):
+            rows = pl.ds(pl.multiple_of(index * ROWS, ROWS), ROWS)
+            slot = lax.rem(index, 2)
+
+            @pl.when(index < 256 // ROWS - 1)
+            def _():
+                for copy in middle_loads(index + 1)[0:2]:
+                    copy.start()
+
+            for copy in middle_loads(index)[0:2]:
+                copy.wait()
+
+            @pl.when(index >= 2)
+            def _():
+                rows_out(0, index - 2).wait()
+
+            cotangent, stream_rows = rows_a[slot], rows_b[slot]
+            branch_rows = branch[rows, :] + b_fc2[...].reshape(1, 1152)
+            out_rows[slot] = (stream_rows + gate_mlp * branch_rows).astype(jnp.bfloat16)
+            rows_out(0, index).start()
+            d_mod[5:6, :] += total(cotangent * branch_rows)
+            bias_fc2[...] += total(
+                (cotangent * gate_mlp).astype(jnp.bfloat16).astype(jnp.float32)
+            )
+            return carry
+
+        lax.fori_loop(0, 256 // ROWS, finish_step, 0)
 
     def middle_end():
         all_t[3456:4608, :] = branch[...].T.astype(jnp.bfloat16)
@@ -842,10 +836,9 @@
         lax.fori_loop(low, high, qkv_step, 0)
 
     def ada_load():
-        return pltpu.make_async_copy(w_ada, wb.at[0, :, 0:256], load_sem.at[1, 0])
+        return pltpu.make_async_copy(w_ada, wa.at[0, 0:256], load_sem.at[0, 0])
 
     def last_rows():
-        ada_load().start()
         branch[...] = grad_t[...].T
         scale_attn = mods[1:2]
 
@@ -915,6 +908,7 @@
         lax.fori_loop(1, 32, one, 0)
 
     def tail_share():
+        ada_load().start()
         vectors = [d_mod[row : row + 1] for row in range(6)]
         vectors += [bias_qv[0:1, 0:1152], bias_qv[0:1, 2304:3456]]
         vectors += [bias_proj[...], bias_fc1[0:1, :], bias_fc2[...]]
@@ -946,6 +940,8 @@
             first = first + got[source]
             second = second + got[16 + source]
 
+        lanes = lax.broadcasted_iota(jnp.int32, (1, 256), 1)
+
         def piece(rows, entry):
             begin = sum(count for _, _, count in WINDOWS[:entry])
             _, width, count = WINDOWS[entry]
@@ -955,9 +951,12 @@
             moved = pltpu.roll(joined, lax.rem(count * 128 - shift, count * 128), 1)
             return moved[0:1]
 
-        d_mod_own = jnp.concatenate([piece(first, 0), piece(second, 0)], axis=0)[:, 0:256]
+        d_mod_own = jnp.concatenate(
+            [jnp.where(lanes < 216, piece(rows, 0)[:, 0:256], 0.0) for rows in (first, second)],
+            axis=0,
+        )
         ada_load().wait()
-        conds[place] = exact_dot(d_mod_own[:, 0:216], wb[0, :, 0:216], 1)
+        conds[place] = exact_dot(d_mod_own, wa[0, 0:256])
         each(cond_to, lambda copy: copy.start())
         for chunk in range(2):
             t2_load(chunk).start()
@@ -1005,12 +1004,15 @@
                 copy.wait()
         sums[...] = sums_all[0] + sums_all[1] + sums_all[2] + sums_all[3]
 
-    swap_start(0)
+    lhs_load(0).start()
+    rhs_load().start()
     mlp_begin()
     for copy in heads_load(0):
         copy.start()
     lax.fori_loop(0, 16, clear, 0)
-    swap_finish(0)
+    lhs_load(0).wait()
+    rhs_load().wait()
+    pl.semaphore_wait(barrier, 34)
     products(0)
     mlp_backward(0, 4)
     mlp_backward(4, 8)
@@ -1035,19 +1037,24 @@
     swap_finish(2)
     receive(0, 2)
     products(2)
+    branch_begin()
+    finish_begin()
     last_rows()
-    tail_share()
     receive(1, 1)
     receive(0, 3)
+    branch_forward(0, 6)
+    branch_forward(6, 12)
+    receive(1, 2)
+    finish_rows()
+    tail_share()
+    receive(2, 0)
+    receive(0, 4)
     tail_cond()
-    receive(2, 0)
-    receive(1, 2)
-    receive(0, 4)
-    tail_group()
     receive(2, 1)
     receive(1, 3)
     receive(0, 5)
     ring_start(0)
+    tail_group()
     receive(2, 2)
     receive(1, 4)
     ring_relay(0)
@@ -1091,14 +1098,13 @@
             jax.ShapeDtypeStruct((4, 2, PACK), full),
             jax.ShapeDtypeStruct((8, 128), full),
         ),
-        in_specs=[anywhere] * 11 + [vmem] + [anywhere] * 4 + [vmem] * 6 + [anywhere] * 6,
+        in_specs=[anywhere] * 7 + [vmem] + [anywhere] * 4 + [vmem] * 6 + [anywhere] * 6,
         out_specs=(vmem,) * 4 + (anywhere,) * 2 + (vmem,) * 2,
         scratch_shapes=[
             pltpu.VMEM((2, 6, 64, PIECE, 128), full),
             pltpu.VMEM((6, 63, PIECE, 128), full),
             pltpu.VMEM((16, 144, 512), small),
             pltpu.VMEM((2304, 512), small),
-            pltpu.VMEM((16, 144, 256), full),
             pltpu.VMEM((2304, 256), full),
             pltpu.VMEM((2304, 256), full),
             pltpu.VMEM((3, 4, 6, PIECE, 128), full),
@@ -1133,8 +1139,8 @@
             dma((6, 6)),
             dma((6, 6)),
             regular((6, 6)),
-            dma((2,)),
-            dma((2,)),
+            dma,
+            dma,
             regular,
             dma((2,)),
             dma((3, 4)),
@@ -1159,10 +1165,93 @@
     )(*operands)
 
 
-def front_kernel(
-    feats, w_t1, b_t1, w_t2, b_t2, rows_table, w_ada, b_ada, pre_out, cond_out, mods, mine, send, recv
+def as_row(ref):
+    return ref[...].reshape(1, ref.shape[0])
+
+
+def forward_kernel(
+    tokens,
+    out_grad,
+    feats,
+    labels,
+    grid_ids,
+    table,
+    w_t1,
+    b_t1,
+    w_t2,
+    b_t2,
+    w_ada,
+    b_ada,
+    w_qkv,
+    b_qv,
+    w_proj,
+    b_proj,
+    w_fc1,
+    b_fc1,
+    pre_out,
+    cond_out,
+    mods,
+    lhs_two,
+    lhs_one,
+    lhs_zero,
+    rhs_zero,
+    act_out,
+    slope_out,
+    heads,
+    cot,
+    resid,
+    attn_out,
+    ada_wide,
+    bias_keys,
+    onehot,
+    mine,
+    gathered,
+    flat,
+    normed,
+    qkv_t,
+    w_q,
+    w_p,
+    w_f,
+    w_1,
+    w_2,
+    keys_off,
+    live_rows,
+    send_a,
+    send_b,
+    send_c,
+    send_d,
+    send_e,
+    got_a,
+    got_b,
+    got_c,
+    got_d,
+    got_e,
+    send,
+    recv,
+    load_sem,
+    pair_send,
+    pair_recv,
+    fc_sem,
 ):
+    at = coords()
+    core = at["core"]
+    sibling = sibling_of(at)
     place = lax.axis_index("dp")
+    loads = [
+        pltpu.make_async_copy(source, target, load_sem.at[index])
+        for index, (source, target) in enumerate(
+            ((w_t1, w_1), (w_t2, w_2), (w_qkv, w_q), (w_proj, w_p))
+        )
+    ]
+    for copy in loads:
+        copy.start()
+
+    def fc_load(part):
+        columns = pl.ds(part * 1152, 1152)
+        return pltpu.make_async_copy(w_fc1.at[:, columns], w_f.at[part % 2], fc_sem.at[part % 2])
+
+    fc_load(0).start()
+    fc_load(1).start()
     barrier = pltpu.get_barrier_semaphore()
 
     def hello(hop, _):
@@ -1170,22 +1259,27 @@
         return _
 
     lax.fori_loop(1, 32, hello, 0)
-    pre_time = exact_dot(feats[...], w_t1[...]) + b_t1[...]
-    condition = exact_dot(silu(pre_time), w_t2[...]) + b_t2[...] + rows_table[...]
-    mod_part = exact_dot(silu(condition), w_ada[...]) + b_ada[...]
+    rows_table = jnp.concatenate(
+        [table[pl.ds(labels[0], 1), :], table[pl.ds(labels[1], 1), :]], axis=0
+    )
+    loads[0].wait()
+    pre_time = exact_dot(feats[...], w_1[...]) + as_row(b_t1)
+    loads[1].wait()
+    condition = exact_dot(silu(pre_time), w_2[...]) + as_row(b_t2) + rows_table
+    mod_part = exact_dot(silu(condition), w_ada[...], 1) + as_row(b_ada)
     pre_out[...] = pre_time
     cond_out[...] = condition
     for item in range(2):
         mine[item, :, 0:216] = mod_part[item : item + 1]
         mine[item, :, 216:256] = jnp.zeros((1, 40), jnp.float32)
-    mods[place] = mine[lax.div(place, 16)]
+    gathered[place] = mine[lax.div(place, 16)]
     pl.semaphore_wait(barrier, 31)
 
     def copy_to(hop):
         target = lax.rem(place + hop, 32)
         return pltpu.make_async_remote_copy(
             src_ref=mine.at[lax.div(target, 16)],
-            dst_ref=mods.at[place],
+            dst_ref=gathered.at[place],
             send_sem=send.at[hop],
             recv_sem=recv.at[hop],
             device_id=dp_peer(hop),
@@ -1200,31 +1294,263 @@
         copy_to(hop).wait()
         return _
 
+    def norm(values):
+        mean = jnp.mean(values, axis=-1, keepdims=True)
+        centered = values - mean
+        inverse = lax.rsqrt(jnp.mean(centered * centered, axis=-1, keepdims=True) + EPS)
+        return centered * inverse
+
+    def row_range(index):
+        return pl.ds(pl.multiple_of(index * 64, 64), 64)
+
     lax.fori_loop(1, 32, begin, 0)
+    ada_rows = jnp.concatenate([w_ada[...].astype(jnp.float32), jnp.zeros((40, 1152))], axis=0)
+    ada_wide[...] = ada_rows.astype(jnp.bfloat16)
+    grid_value = grid_ids[lax.div(place, 16)]
+    first_live = jnp.where(grid_value == 2, 16, 0)
+    end_live = jnp.where(grid_value == 1, 240, 256)
+    slots = lax.broadcasted_iota(jnp.int32, (256, 128), 0)
+    live = (slots >= first_live) & (slots < end_live)
+    keys_off[...] = jnp.where(live, 0.0, NEG)
+    live_rows[...] = jnp.where(live, 1.0, 0.0)
+    bias_keys[...] = keys_off[...]
+    for item in range(2):
+        classes = lax.broadcasted_iota(jnp.int32, (1, 128), 1)
+        onehot[item : item + 1, :] = jnp.where(classes == labels[item], 1.0, 0.0)
+
+    def first_norm(index, _):
+        rows = row_range(index)
+        normed[rows, :] = norm(tokens[rows, :].astype(jnp.float32))
+        cot[rows, :] = out_grad[rows, :].astype(jnp.float32) * live_rows[rows, 0:1]
+        return _
+
+    lax.fori_loop(0, 4, first_norm, 0)
+
+    def blank(row, _):
+        flat[row] = jnp.zeros((1, 128), jnp.float32)
+        return _
+
+    lax.fori_loop(0, 56, blank, 0)
     lax.fori_loop(1, 32, finish, 0)
-
-
-def front(feats, w_t1, b_t1, w_t2, b_t2, rows_table, w_ada, b_ada):
+    for piece in range(32):
+        row, shift = piece * 216 // 128, piece * 216 % 128
+        wide = jnp.concatenate([gathered[piece], jnp.zeros((1, 128), jnp.float32)], axis=1)
+        wide = pltpu.roll(jnp.concatenate([wide] * 8, axis=0), shift, 1)[0:1]
+        for step in range(3):
+            flat[row + step] += wide[:, step * 128 : step * 128 + 128]
+    for row in range(6):
+        for column in range(9):
+            mods[row : row + 1, column * 128 : column * 128 + 128] = flat[row * 9 + column]
+    mods[6:8, :] = jnp.zeros((2, 1152), jnp.float32)
+
+    def to_sibling(index, source, target):
+        return pltpu.make_async_remote_copy(
+            src_ref=source,
+            dst_ref=target,
+            send_sem=pair_send.at[index],
+            recv_sem=pair_recv.at[index],
+            device_id=sibling,
+            device_id_type=MESH,
+        )
+
+    def modulate(index, _):
+        rows = row_range(index)
+        normed[rows, :] = normed[rows, :] * (1.0 + mods[1:2]) + mods[0:1]
+        return _
+
+    lax.fori_loop(0, 4, modulate, 0)
+    send_a[...] = normed[...].T
+    pair_a = to_sibling(0, send_a, got_a)
+    pair_a.start()
+    for part in range(8):
+        lhs_two[part, :, 0:256] = send_a[part * 144 : part * 144 + 144].astype(jnp.bfloat16)
+    loads[2].wait()
+    for part in range(3):
+        block = dot_nn(
+            normed[...].astype(jnp.bfloat16), w_q[:, part * 1152 : part * 1152 + 1152]
+        )
+        if part == 0:
+            block = block + as_row(b_qv)[:, 0:1152]
+        if part == 2:
+            block = block + as_row(b_qv)[:, 1152:2304]
+        qkv_t[part * 1152 : part * 1152 + 1152, :] = block.T
+
+    def branch_grad(index, _):
+        rows = row_range(index)
+        normed[rows, :] = cot[rows, :] * mods[5:6]
+        return _
+
+    scale = 1.0 / math.sqrt(72)
+
+    def one_head(head, _):
+        parts = []
+        for part in range(3):
+            rows = pl.ds(pl.multiple_of(part * 1152 + head * 72, 8), 72)
+            padded = jnp.concatenate([qkv_t[rows, :], jnp.zeros((8, 256), jnp.float32)], axis=0)
+            parts.append(padded.astype(jnp.bfloat16))
+            heads[head + part * 16] = parts[-1]
+        query, key, value = parts
+        scores = dot_tn(key, query) * scale + jnp.concatenate([keys_off[...]] * 2, axis=1)
+        shifted = jnp.exp(scores - jnp.max(scores, axis=0, keepdims=True))
+        weights = (shifted / jnp.sum(shifted, axis=0, keepdims=True)).astype(jnp.bfloat16)
+        rows = pl.ds(pl.multiple_of(head * 72, 8), 72)
+        send_b[rows, :] = dot_nn(value, weights)[0:72]
+        return _
+
+    lax.fori_loop(0, 16, one_head, 0, unroll=4)
+    pair_b = to_sibling(1, send_b, got_b)
+    pair_b.start()
+    for part in range(8):
+        lhs_two[part + 8, :, 0:256] = send_b[part * 144 : part * 144 + 144].astype(jnp.bfloat16)
+    lax.fori_loop(0, 4, branch_grad, 0)
+    send_c[...] = normed[...].T
+    pair_c = to_sibling(2, send_c, got_c)
+    pair_c.start()
+    rhs_zero[:, 0:256] = send_c[...].astype(jnp.bfloat16)
+    loads[3].wait()
+    attn_out[...] = dot_tn(send_b[...].astype(jnp.bfloat16), w_p[...]) + as_row(b_proj)
+
+    def second_norm(index, _):
+        rows = row_range(index)
+        stream = tokens[rows, :].astype(jnp.float32) + mods[2:3] * attn_out[rows, :]
+        resid[rows, :] = stream
+        normed[rows, :] = norm(stream) * (1.0 + mods[4:5]) + mods[3:4]
+        return _
+
+    lax.fori_loop(0, 4, second_norm, 0)
+    send_d[...] = normed[...].T
+    pair_d = to_sibling(3, send_d, got_d)
+    pair_d.start()
+    for part in range(8):
+        lhs_one[part, :, 0:256] = send_d[part * 144 : part * 144 + 144].astype(jnp.bfloat16)
+    pair_a.wait()
+    for part in range(8):
+        lhs_two[part, :, 256:512] = got_a[part * 144 : part * 144 + 144].astype(jnp.bfloat16)
+    inner = math.sqrt(2.0 / math.pi)
+    pair_e = []
+    for part in range(4):
+        fc_load(part).wait()
+        columns = slice(part * 1152, part * 1152 + 1152)
+        hidden = dot_nn(normed[...].astype(jnp.bfloat16), w_f[part % 2]) + as_row(b_fc1)[:, columns]
+        qkv_t[0:1152, :] = hidden.T
+        if part < 2:
+            fc_load(part + 2).start()
+
+        def gelu(index, _, part=part):
+            rows = pl.ds(pl.multiple_of(index * 144, 144), 144)
+            values = qkv_t[rows, :]
+            square = values * values
+            bend = jnp.tanh(inner * values * (1.0 + 0.044715 * square))
+            half = 0.5 * (1.0 + bend)
+            active = values * half
+            steep = half + 0.5 * values * (1.0 - bend * bend) * inner * (
+                1.0 + 3.0 * 0.044715 * square
+            )
+            into = pl.ds(pl.multiple_of(part * 1152 + index * 144, 144), 144)
+            act_out[into, :] = active.astype(jnp.bfloat16)
+            slope_out[into, :] = steep.astype(jnp.bfloat16)
+            chip = part * 4 + lax.div(index, 2)
+
+            @pl.when(lax.rem(index, 2) == core)
+            def _():
+                lhs_zero[chip, :, 0:256] = active.astype(jnp.bfloat16)
+
+            @pl.when(lax.rem(index, 2) != core)
+            def _():
+                send_e[chip] = active
+
+            return 0
+
+        lax.fori_loop(0, 8, gelu, 0)
+        some = pl.ds(part * 4, 4)
+        pair_e.append(to_sibling(4 + part, send_e.at[some], got_e.at[some]))
+        pair_e[-1].start()
+        if part == 0:
+            pair_b.wait()
+            for chip in range(8):
+                rows = got_b[chip * 144 : chip * 144 + 144]
+                lhs_two[chip + 8, :, 256:512] = rows.astype(jnp.bfloat16)
+        if part == 1:
+            pair_c.wait()
+            rhs_zero[:, 256:512] = got_c[...].astype(jnp.bfloat16)
+        if part == 2:
+            pair_d.wait()
+            for chip in range(8):
+                rows = got_d[chip * 144 : chip * 144 + 144]
+                lhs_one[chip, :, 256:512] = rows.astype(jnp.bfloat16)
+    for part in range(4):
+        pair_e[part].wait()
+        for chip in range(part * 4, part * 4 + 4):
+            lhs_zero[chip, :, 256:512] = got_e[chip].astype(jnp.bfloat16)
+
+
+def forward(operands):
+    dma = pltpu.SemaphoreType.DMA
     vmem = pl.BlockSpec(memory_space=pltpu.VMEM)
-    width = w_t2.shape[0]
+    smem = pl.BlockSpec(memory_space=pltpu.SMEM)
+    anywhere = pl.BlockSpec(memory_space=pl.ANY)
+    full, small = jnp.float32, jnp.bfloat16
+    out = jax.ShapeDtypeStruct
     return pl.pallas_call(
-        front_kernel,
+        forward_kernel,
         out_shape=(
-            jax.ShapeDtypeStruct((2, width), jnp.float32),
-            jax.ShapeDtypeStruct((2, width), jnp.float32),
-            jax.ShapeDtypeStruct((32, 1, 256), jnp.float32),
+            out((2, 1152), full),
+            out((2, 1152), full),
+            out((8, 1152), full),
+            out((16, 144, 512), small),
+            out((8, 144, 512), small),
+            out((16, 144, 512), small),
+            out((1152, 512), small),
+            out((4608, 256), small),
+            out((4608, 256), small),
+            out((48, 80, 256), small),
+            out((256, 1152), full),
+            out((256, 1152), full),
+            out((256, 1152), full),
+            out((256, 1152), small),
+            out((256, 128), full),
+            out((2, 128), full),
         ),
-        in_specs=[vmem] * 8,
-        out_specs=(vmem, vmem, vmem),
+        in_specs=[vmem] * 3
+        + [smem, smem, vmem]
+        + [anywhere, vmem] * 2
+        + [vmem, vmem]
+        + [anywhere, vmem] * 3,
+        out_specs=(vmem,) * 16,
         scratch_shapes=[
-            pltpu.VMEM((2, 1, 256), jnp.float32),
-            pltpu.SemaphoreType.DMA((32,)),
-            pltpu.SemaphoreType.DMA((32,)),
+            pltpu.VMEM((2, 1, 256), full),
+            pltpu.VMEM((32, 1, 256), full),
+            pltpu.VMEM((56, 1, 128), full),
+            pltpu.VMEM((256, 1152), full),
+            pltpu.VMEM((3456, 256), full),
+            pltpu.VMEM((1152, 3456), small),
+            pltpu.VMEM((1152, 1152), small),
+            pltpu.VMEM((2, 1152, 1152), small),
+            pltpu.VMEM((256, 1152), small),
+            pltpu.VMEM((1152, 1152), small),
+            pltpu.VMEM((256, 128), full),
+            pltpu.VMEM((256, 128), full),
+            pltpu.VMEM((1152, 256), full),
+            pltpu.VMEM((1152, 256), full),
+            pltpu.VMEM((1152, 256), full),
+            pltpu.VMEM((1152, 256), full),
+            pltpu.VMEM((16, 144, 256), full),
+            pltpu.VMEM((1152, 256), full),
+            pltpu.VMEM((1152, 256), full),
+            pltpu.VMEM((1152, 256), full),
+            pltpu.VMEM((1152, 256), full),
+            pltpu.VMEM((16, 144, 256), full),
+            dma((32,)),
+            dma((32,)),
+            dma((4,)),
+            dma((8,)),
+            dma((8,)),
+            dma((2,)),
         ],
         compiler_params=pltpu.CompilerParams(
-            collective_id=2, has_side_effects=True, vmem_limit_bytes=32 * 2**20
+            collective_id=2, has_side_effects=True, vmem_limit_bytes=255 * 2**18
         ),
-    )(feats, w_t1, b_t1[None], w_t2, b_t2[None], rows_table, w_ada, b_ada[None])
+    )(*operands)
 
 
 def on_device(
@@ -1251,76 +1577,47 @@
 ):
     dp_count = lax.axis_size("dp")
     dp_place = lax.axis_index("dp")
-    row_count, model_width = tokens.shape
-    frame_count = row_count // SLOTS
-    head_count = HEADS
-    head_dim = model_width // head_count
-    score_scale = 1.0 / math.sqrt(head_dim)
-    frame_shape = (frame_count, SLOTS, head_count, head_dim)
+    model_width = tokens.shape[1]
     time_feats = time_embed(timesteps, w_t1.shape[0] // 2)
-    onehot = (labels[:, None] == jnp.arange(128, dtype=jnp.int32)[None, :]).astype(jnp.float32)
-    pre_time, condition, mods = front(
-        time_feats, w_t1, b_t1, w_t2, b_t2, table[labels], w_ada, b_ada
+    (
+        pre_time,
+        condition,
+        mods,
+        lhs_two,
+        lhs_one,
+        lhs_zero,
+        rhs_zero,
+        act_t,
+        slope_t,
+        heads,
+        cotangent,
+        resid_one,
+        attn_out,
+        ada_wide,
+        bias_keys,
+        onehot,
+    ) = forward(
+        [
+            tokens,
+            out_grad,
+            time_feats,
+            labels,
+            grid_ids,
+            table,
+            w_t1,
+            b_t1,
+            w_t2,
+            b_t2,
+            w_ada.T,
+            b_ada,
+            w_qkv,
+            b_qv,
+            w_proj,
+            b_proj,
+            w_fc1,
+            b_fc1,
+        ]
     )
-    item_mod = mods.reshape(32, 256)[:, :216].reshape(6 * model_width)
-    own_item = dp_place * frame_count // ITEM_FRAMES
-    shift_attn, scale_attn, gate_attn, shift_mlp, scale_mlp, gate_mlp = jnp.split(item_mod, 6)
-    grid_value = lax.dynamic_index_in_dim(grid_ids, own_item, 0, keepdims=False)
-    first_live = jnp.where(grid_value == 2, SLOTS // 16, 0)
-    end_live = jnp.where(grid_value == 1, SLOTS - SLOTS // 16, SLOTS)
-    slot_pos = jnp.arange(SLOTS, dtype=jnp.int32)
-    valid_keys = (slot_pos >= first_live) & (slot_pos < end_live)
-    live_rows = jnp.tile(valid_keys, frame_count).astype(jnp.float32)[:, None]
-    token_vals = tokens.astype(jnp.float32)
-    normed_one, inv_one = norm_rows(token_vals)
-    attn_in = (normed_one * (1.0 + scale_attn) + shift_attn).astype(jnp.bfloat16)
-    qkv_rows = jnp.dot(attn_in, w_qkv, preferred_element_type=jnp.float32)
-    queries = (
-        (qkv_rows[:, :model_width] + b_qv[:model_width]).astype(jnp.bfloat16).reshape(frame_shape)
-    )
-    key_rows = qkv_rows[:, model_width : 2 * model_width].astype(jnp.bfloat16).reshape(frame_shape)
-    values = (
-        (qkv_rows[:, 2 * model_width :] + b_qv[model_width:])
-        .astype(jnp.bfloat16)
-        .reshape(frame_shape)
-    )
-
-    def masked_scores():
-        raw = (
-            jnp.einsum("fqhd,fkhd->fhqk", queries, key_rows, preferred_element_type=jnp.float32)
-            * score_scale
-        )
-        return jnp.where(valid_keys[None, None, None, :], raw, NEG)
-
-    scores = masked_scores()
-    row_max = jnp.max(scores, axis=-1, keepdims=True)
-    shifted = jnp.exp(scores - row_max)
-    row_total = jnp.sum(shifted, axis=-1, keepdims=True)
-    log_total = row_max + jnp.log(row_total)
-    attn_weights = (shifted / row_total).astype(jnp.bfloat16)
-    mixed = jnp.einsum("fhqk,fkhd->fqhd", attn_weights, values, preferred_element_type=jnp.float32)
-    mixed_rows = mixed.reshape(row_count, model_width).astype(jnp.bfloat16)
-    attn_out = jnp.dot(mixed_rows, w_proj, preferred_element_type=jnp.float32) + b_proj
-    resid_one = token_vals + gate_attn * attn_out
-    normed_two, inv_two = norm_rows(resid_one)
-    mlp_in = (normed_two * (1.0 + scale_mlp) + shift_mlp).astype(jnp.bfloat16)
-    hidden = jnp.dot(mlp_in, w_fc1, preferred_element_type=jnp.float32) + b_fc1
-    gelu_vals, gelu_pull = jax.vjp(functools.partial(jax.nn.gelu, approximate=True), hidden)
-    activated = gelu_vals.astype(jnp.bfloat16)
-    slope = gelu_pull(jnp.ones_like(hidden))[0].astype(jnp.bfloat16)
-    cotangent = out_grad.astype(jnp.float32) * live_rows
-    grad_branch = (cotangent * gate_mlp).astype(jnp.bfloat16)
-    act_t = activated.T
-    act_split = act_t.reshape(16, 2, 144, row_count)
-    gbr_t = grad_branch.T
-    mlp_t = mlp_in.T.reshape(8, 144, row_count)
-    two_t = jnp.stack([attn_in.T, mixed_rows.T]).reshape(16, 144, row_count)
-    heads = jnp.stack([queries, key_rows, values])[:, 0].transpose(0, 2, 3, 1)
-    wide = lambda array: array.astype(jnp.float32)
-    bias_keys = jnp.broadcast_to(
-        jnp.where(valid_keys, 0.0, NEG).astype(jnp.float32)[:, None], (SLOTS, 128)
-    )
-    mod_rows = jnp.pad(item_mod.reshape(6, model_width), ((0, 2), (0, 0)))
     (
         sum_qkv,
         sum_proj,
@@ -1332,29 +1629,25 @@
         sums,
     ) = backward(
         [
-            act_split,
-            wide(act_split),
+            lhs_zero,
+            lhs_one,
+            lhs_two,
+            rhs_zero,
             act_t,
-            slope.T,
-            gbr_t,
-            wide(gbr_t),
-            mlp_t,
-            wide(mlp_t),
-            two_t,
-            wide(two_t),
-            jnp.pad(heads.reshape(48, head_dim, SLOTS), ((0, 0), (0, 8), (0, 0))),
+            slope_t,
+            heads,
             bias_keys,
             cotangent,
             resid_one,
             attn_out,
             tokens,
-            mod_rows,
-            b_fc2[None],
+            mods,
+            b_fc2,
             pre_time,
             condition,
             time_feats,
             onehot,
-            jnp.pad(w_ada, ((0, 0), (0, 40))),
+            ada_wide,
             w_t2,
             w_qkv,
             w_proj,

time: 268 us -> 230 us (0.86)
  matrix products: 30.7 us -> 5.44 us
  Pallas kernels: 187 us -> 212 us
  local copies, waits for them, and re-layouts: 32.4 us -> 8.75 us
  other arithmetic: 14.4 us -> 1.97 us
    pallas_call x1, Pallas kernels: 12.3 us -> 43.4 us  [forward(): pl.pallas_call(forward_kernel, out_shape=(out((2, 1152), full), out((2, 1...]
    dot_general x4 -> x0, matrix products: 20.9 us -> none  [the longest x1 11 us: on_device(): hidden = jnp.dot(mlp_in, w_fc1, preferred_element_type=jnp.float32) + b_fc1]
    unnamed x102 -> x20, local copies, waits for them, and re-layouts: 12 us -> 4.84 us
    convert_element_type x6 -> x0, other arithmetic: 6.47 us -> none  [the longest x3 5.67 us: on_device(): wide = lambda array: array.astype(jnp.float32)]
    pallas_call x1, Pallas kernels: 174 us -> 169 us  [backward(): pl.pallas_call(backward_kernel, out_shape=(jax.ShapeDtypeStruct((36, 3456...]
    sub x1 -> x0, matrix products: 4.34 us -> none  [on_device(): shifted = jnp.exp(scores - row_max)]
    convert_element_type x4 -> x0, local copies, waits for them, and re-layouts: 3.57 us -> none  [the longest x1 1.76 us: on_device(): mixed_rows = mixed.reshape(row_count, model_width).astype(jnp.bfloat16)]
    pad x3 -> x0, local copies, waits for them, and re-layouts: 3 us -> none  [the longest x1 1.47 us: on_device(): jnp.pad(heads.reshape(48, head_dim, SLOTS), ((0, 0), (0, 8), (0, 0)))]
where the time goes in v3:
time: 230 us; the launch traced here: 229 us
  Pallas kernels  212 us (92%)
  local copies, waits for them, and re-layouts  8.75 us (4%)
  matrix products  5.44 us (2%)
    pallas_call x1, Pallas kernels, backward(): pl.pallas_call(backward_kernel, out_shape=(jax.ShapeDtypeStruct((36, 3456...  169 us
    pallas_call x1, Pallas kernels, forward(): pl.pallas_call(forward_kernel, out_shape=(out((2, 1152), full), out((2, 1...  43.4 us
    dot_general x4, matrix products, hdot_t(): lax.dot_general(left_op, right_op, (((0,), (0,)), ((), ())), precision=la...  5.44 us
    unnamed x20, local copies, waits for them, and re-layouts  4.84 us

profile of v3, /device:TPU:1, one launch (start us, length us, event | category | flops | bytes accessed | tf_op | source)
XLA Modules:
  0.0 228.8 jit_solution(16876132969953266567)
XLA Ops:
  0.7 0.7 convert_element_type.3
  1.3 0.1 multiply_cosine_fusion
  1.4 0.6 pad_maximum_fusion.feats
  2.0 43.4 %shard_map.323 = (f32[2,1152]{1,0:T(2,128)}, f32[2,1152]{1,0:T(2,128)}, f32[8,1152]{1,0:T(8,128)}, bf16[16,144,512]{2,1,0:T(8,128)(2,1)}, bf16[8,144,512]{2,1,0:...) custom-call(bf16[256,1152]{1,0:T(8,128)(2,1)} %tokens.3, ...), custom_call_target="tpu_custom_call" | custom-call | tf_op jit(solution)/shard_map/pallas_call | solution.py:1494
  45.5 168.5 %shard_map.324 = (f32[36,3456]{1,0:T(8,128)}, f32[36,1152]{1,0:T(8,128)}, f32[36,4608]{1,0:T(8,128)}, f32[144,1152]{1,0:T(8,128)}, bf16[256,1152]{1,0:T(8,128)(2...) custom-call(bf16[16,144,512]{2,1,0:T(8,128)(2,1)} %get-tuple-element.41.lhs_zero, ...), custom_call_target="tpu_custom_call" | custom-call | tf_op jit(solution)/shard_map/pallas_call | solution.py:1089
  214.0 0.0 copy-start.6
  214.0 0.0 copy-start.3
  214.0 0.0 copy-start.2
  214.0 0.0 copy-start.4
  214.0 1.2 reshape.47
  215.2 1.1 fusion.6
  216.3 0.9 fusion.2
  217.2 0.0 copy-start.5
  217.2 2.0 fusion
  219.3 0.0 copy-start
  219.3 1.4 fusion.4
  220.7 0.6 dynamic_slice.13
  221.2 0.6 dynamic_slice.15
  221.8 0.6 slice_reduce_fusion.2
  222.4 0.0 copy-done.6
  222.4 0.5 slice_bitcast_fusion.1
  222.9 0.6 slice_bitcast_fusion
  223.5 0.5 slice_bitcast_fusion.3
  224.0 0.0 copy-done.3
  224.0 0.8 copy.43
  224.8 0.0 copy-done.2
  224.8 0.0 copy-start.1
  224.8 0.8 copy.44
  225.6 0.0 copy-done.4
  225.6 0.8 copy.45
  226.4 0.0 copy-done.5
  226.4 0.7 copy.46
  227.1 0.0 copy-done
  227.1 0.9 copy.47
  228.0 0.0 copy-done.1
  228.0 0.8 copy.48
  (3 shorter events, 0.0 us)
Async XLA Ops:
  214.0 8.4 %copy-start.6 = (f32[8,128]{1,0:T(8,128)S(1)}, f32[8,128]{1,0:T(8,128)}, u32[]{:S(2)}) copy-start(f32[8,128]{1,0:T(8,128)} %get-tuple-element.60) | copy-start | bytes 12292
  214.0 10.0 %copy-start.3 = (bf16[256,1152]{1,0:T(8,128)(2,1)S(1)}, bf16[256,1152]{1,0:T(8,128)(2,1)}, u32[]{:S(2)}) copy-start(bf16[256,1152]{1,0:T(8,128)(2,1)} %get-tuple-element.89) | copy-start | bytes 1769476
  214.0 10.8 %copy-start.2 = (bf16[256,1152]{1,0:T(8,128)(2,1)S(1)}, bf16[256,1152]{1,0:T(8,128)(2,1)}, u32[]{:S(2)}) copy-start(bf16[256,1152]{1,0:T(8,128)(2,1)} %get-tuple-element.90) | copy-start | bytes 1769476
  214.0 11.6 %copy-start.4 = (f32[36,3456]{1,0:T(8,128)S(1)}, f32[36,3456]{1,0:T(8,128)}, u32[]{:S(2)}) copy-start(f32[36,3456]{1,0:T(8,128)} %get-tuple-element.91) | copy-start | bytes 1492996
  217.2 9.2 %copy-start.5 = (f32[36,1152]{1,0:T(8,128)S(1)}, f32[36,1152]{1,0:T(8,128)}, u32[]{:S(2)}) copy-start(f32[36,1152]{1,0:T(8,128)} %get-tuple-element.93) | copy-start | bytes 497668
  219.3 7.9 %copy-start = (f32[36,4608]{1,0:T(8,128)S(1)}, f32[36,4608]{1,0:T(8,128)}, u32[]{:S(2)}) copy-start(f32[36,4608]{1,0:T(8,128)} %get-tuple-element.95) | copy-start | bytes 1990660
  224.8 3.2 %copy-start.1 = (f32[144,1152]{1,0:T(8,128)S(1)}, f32[144,1152]{1,0:T(8,128)}, u32[]{:S(2)}) copy-start(f32[144,1152]{1,0:T(8,128)} %get-tuple-element.97) | copy-start | bytes 1990660

commit v4 on v3

--- a/solution.py
+++ b/solution.py
@@ -15,16 +15,6 @@
 NEG = -1e30
 
 
-def hdot_t(left_op, right_op):
-    return lax.dot_general(
-        left_op,
-        right_op,
-        (((0,), (0,)), ((), ())),
-        precision=lax.Precision.HIGHEST,
-        preferred_element_type=jnp.float32,
-    )
-
-
 def norm_back(grad_in, normed, inv_std):
     return inv_std * (
         grad_in
@@ -44,11 +34,6 @@
     )
     angles = step_ids.astype(jnp.float32)[:, None] * frequency[None, :]
     return jnp.concatenate([jnp.cos(angles), jnp.sin(angles)], axis=1)
-
-
-def own_block(vector, dp_place, dp_count):
-    block_rows = vector.shape[0] // dp_count
-    return lax.dynamic_slice_in_dim(vector, dp_place * block_rows, block_rows, 0)
 
 
 def split_three(values):
@@ -1553,6 +1538,126 @@
     )(*operands)
 
 
+def split_parts(values):
+    high = values.astype(jnp.bfloat16)
+    rest = values - high.astype(jnp.float32)
+    middle = rest.astype(jnp.bfloat16)
+    low = (rest - middle.astype(jnp.float32)).astype(jnp.bfloat16)
+    return high, middle, low
+
+
+def outer_sum(left, right):
+    left_high, left_middle, left_low = split_parts(left)
+    right_high, right_middle, right_low = split_parts(right)
+    lefts = [left_high, left_high, left_middle, left_middle, left_high, left_low]
+    rights = [right_high, right_middle, right_high, right_middle, right_low, right_high]
+    return dot_tn(jnp.concatenate(lefts, axis=0), jnp.concatenate(rights, axis=0))
+
+
+def finish_kernel(
+    packs,
+    sums,
+    in_qkv,
+    in_proj,
+    in_fc1,
+    in_fc2,
+    in_block,
+    in_grad,
+    out_qkv,
+    out_proj,
+    out_fc1,
+    out_fc2,
+    out_block,
+    out_grad,
+    d_ada,
+    b_ada,
+    d_t1,
+    b_t1,
+    d_t2,
+    b_t2,
+    d_table,
+    b_qv,
+    b_proj,
+    b_fc1,
+    b_fc2,
+    copy_sem,
+):
+    place = lax.axis_index("dp")
+    copies = [
+        pltpu.make_async_copy(source, target, copy_sem.at[index])
+        for index, (source, target) in enumerate(
+            (
+                (in_qkv, out_qkv),
+                (in_proj, out_proj),
+                (in_fc1, out_fc1),
+                (in_fc2, out_fc2),
+                (in_block, out_block),
+                (in_grad, out_grad),
+            )
+        )
+    ]
+    for copy in copies:
+        copy.start()
+
+    def eight(begin, end):
+        return jnp.concatenate([packs[group, :, begin:end] for group in range(4)], axis=0)
+
+    def own(rows, width):
+        count = rows.shape[1]
+        return pltpu.roll(rows, lax.rem(count - place * width, count), 1)
+
+    grad_cond, grad_pre = eight(0, 1152), eight(1152, 2304)
+    d_mod = eight(4608, 4864)
+    d_ada[...] = outer_sum(d_mod, eight(2304, 3456))[0:216]
+    b_ada[...] = jnp.sum(d_mod, axis=0, keepdims=True)[:, 0:216].reshape(216)
+    d_t1[...] = outer_sum(own(eight(4864, 5120), 8)[:, 0:128], grad_pre)[0:8]
+    d_t2[...] = outer_sum(own(eight(3456, 4608), 36)[:, 0:128], grad_cond)[0:36]
+    d_table[...] = outer_sum(eight(5120, 5248), grad_cond)[0:101]
+    total_pre = jnp.concatenate([jnp.sum(grad_pre, axis=0, keepdims=True)] * 8, axis=0)
+    total_cond = jnp.concatenate([jnp.sum(grad_cond, axis=0, keepdims=True)] * 8, axis=0)
+    b_t1[...] = own(total_pre, 36)[0:1, 0:36].reshape(36)
+    b_t2[...] = own(total_cond, 36)[0:1, 0:36].reshape(36)
+    b_qv[...] = sums[0:1, 0:72].reshape(72)
+    b_proj[...] = sums[1:2, 0:36].reshape(36)
+    b_fc1[...] = jnp.concatenate([sums[2:3, :], sums[3:4, :]], axis=1)[:, 0:144].reshape(144)
+    b_fc2[...] = sums[4:5, 0:36].reshape(36)
+    for copy in copies:
+        copy.wait()
+
+
+def finish(operands):
+    vmem = pl.BlockSpec(memory_space=pltpu.VMEM)
+    anywhere = pl.BlockSpec(memory_space=pl.ANY)
+    full, small = jnp.float32, jnp.bfloat16
+    out = jax.ShapeDtypeStruct
+    return pl.pallas_call(
+        finish_kernel,
+        out_shape=(
+            out((36, 3456), full),
+            out((36, 1152), full),
+            out((36, 4608), full),
+            out((144, 1152), full),
+            out((256, 1152), small),
+            out((256, 1152), small),
+            out((216, 1152), full),
+            out((216,), full),
+            out((8, 1152), full),
+            out((36,), full),
+            out((36, 1152), full),
+            out((36,), full),
+            out((101, 1152), full),
+            out((72,), full),
+            out((36,), full),
+            out((144,), full),
+            out((36,), full),
+        ),
+        in_specs=[vmem, vmem] + [anywhere] * 6,
+        out_specs=(anywhere,) * 6 + (vmem,) * 11,
+        scratch_shapes=[pltpu.SemaphoreType.DMA((6,))],
+        compiler_params=pltpu.CompilerParams(vmem_limit_bytes=255 * 2**18),
+    )(*operands)
+
+
 def on_device(
     tokens,
     out_grad,
@@ -1575,7 +1680,6 @@
     b_t2,
     table,
 ):
-    dp_count = lax.axis_size("dp")
     dp_place = lax.axis_index("dp")
     model_width = tokens.shape[1]
     time_feats = time_embed(timesteps, w_t1.shape[0] // 2)
@@ -1655,31 +1759,43 @@
             w_fc2,
         ]
     )
-    packs = packs.reshape(8, PACK)
-    grad_cond, grad_pre = packs[:, 0:1152], packs[:, 1152:2304]
-    act_cond, act_time = packs[:, 2304:3456], packs[:, 3456:4608]
-    d_mod, feats_all = packs[:, 4608:4824], packs[:, 4864:5120]
-    class_rows = packs[:, 5120 : 5120 + table.shape[0]]
-    own_time = lax.dynamic_slice_in_dim(act_time, dp_place * 36, 36, 1)
-    own_feats = lax.dynamic_slice_in_dim(feats_all, dp_place * 8, 8, 1)
+    (
+        sum_qkv,
+        sum_proj,
+        sum_fc1,
+        sum_fc2,
+        block_out,
+        input_grad,
+        d_ada,
+        b_ada,
+        d_t1,
+        b_t1,
+        d_t2,
+        b_t2,
+        d_table,
+        d_qv,
+        d_proj,
+        d_fc1,
+        d_fc2,
+    ) = finish([packs, sums, sum_qkv, sum_proj, sum_fc1, sum_fc2, block_out, input_grad])
     return (
         block_out,
         input_grad,
         sum_qkv,
-        sums[0, 0:72],
+        d_qv,
         sum_proj,
-        sums[1, 0:36],
+        d_proj,
         sum_fc1,
-        sums[2:4].reshape(256)[0:144],
+        d_fc1,
         sum_fc2,
-        sums[4, 0:36],
-        hdot_t(act_cond, d_mod),
-        jnp.sum(d_mod, axis=0),
-        hdot_t(own_feats, grad_pre),
-        own_block(jnp.sum(grad_pre, axis=0), dp_place, dp_count),
-        hdot_t(own_time, grad_cond),
-        own_block(jnp.sum(grad_cond, axis=0), dp_place, dp_count),
-        hdot_t(class_rows, grad_cond),
+        d_fc2,
+        d_ada.T,
+        b_ada,
+        d_t1,
+        b_t1,
+        d_t2,
+        b_t2,
+        d_table,
     )
 
 

time: 230 us -> 319 us (1.39)
  Pallas kernels: 212 us -> 316 us
  local copies, waits for them, and re-layouts: 8.75 us -> 0 us
  matrix products: 5.44 us -> 0 us
    pallas_call x0 -> x1, Pallas kernels: none -> 104 us  [finish(): pl.pallas_call(finish_kernel, out_shape=(out((36, 3456), full), out((36,...]
    dot_general x4 -> x0, matrix products: 5.44 us -> none  [hdot_t(): lax.dot_general(left_op, right_op, (((0,), (0,)), ((), ())), precision=la...]
    unnamed x20 -> x0, local copies, waits for them, and re-layouts: 4.84 us -> none
where the time goes in v4:
time: 319 us; the launch traced here: 318 us
  Pallas kernels  316 us (99%)
    pallas_call x1, Pallas kernels, backward(): pl.pallas_call(backward_kernel, out_shape=(jax.ShapeDtypeStruct((36, 3456...  169 us
    pallas_call x1, Pallas kernels, finish(): pl.pallas_call(finish_kernel, out_shape=(out((36, 3456), full), out((36,...  104 us
    pallas_call x1, Pallas kernels, forward(): pl.pallas_call(forward_kernel, out_shape=(out((2, 1152), full), out((2, 1...  43.4 us

profile of v4, /device:TPU:1, one launch (start us, length us, event | category | flops | bytes accessed | tf_op | source)
XLA Modules:
  0.0 317.9 jit_solution(15735241875855348366)
XLA Ops:
  0.7 0.7 convert_element_type.3
  1.3 0.1 multiply_cosine_fusion
  1.4 0.6 pad_maximum_fusion.feats
  2.0 43.4 %shard_map.323 = (f32[2,1152]{1,0:T(2,128)}, f32[2,1152]{1,0:T(2,128)}, f32[8,1152]{1,0:T(8,128)}, bf16[16,144,512]{2,1,0:T(8,128)(2,1)}, bf16[8,144,512]{2,1,0:...) custom-call(bf16[256,1152]{1,0:T(8,128)(2,1)} %tokens.3, ...), custom_call_target="tpu_custom_call" | custom-call | tf_op jit(solution)/shard_map/pallas_call | solution.py:1479
  45.5 168.5 %shard_map.324 = (f32[36,3456]{1,0:T(8,128)}, f32[36,1152]{1,0:T(8,128)}, f32[36,4608]{1,0:T(8,128)}, f32[144,1152]{1,0:T(8,128)}, bf16[256,1152]{1,0:T(8,128)(2...) custom-call(bf16[16,144,512]{2,1,0:T(8,128)(2,1)} %get-tuple-element.58.lhs_zero, ...), custom_call_target="tpu_custom_call" | custom-call | tf_op jit(solution)/shard_map/pallas_call | solution.py:1074
  214.0 103.8 %shard_map.325 = (f32[36,3456]{1,0:T(8,128)}, f32[36,1152]{1,0:T(8,128)}, f32[36,4608]{1,0:T(8,128)}, f32[144,1152]{1,0:T(8,128)}, bf16[256,1152]{1,0:T(8,128)(2...) custom-call(f32[4,2,5248]{2,1,0:T(2,128)} %get-tuple-element.74.pack, ...), custom_call_target="tpu_custom_call" | custom-call | tf_op jit(solution)/shard_map/pallas_call | solution.py:1633
  (1 shorter events, 0.0 us)

commit v5 on v4

--- a/solution.py
+++ b/solution.py
@@ -1176,6 +1176,19 @@
     pre_out,
     cond_out,
     mods,
+    lhs_two_far,
+    lhs_one_far,
+    lhs_zero_far,
+    rhs_zero_far,
+    act_out_far,
+    slope_out_far,
+    heads_far,
+    cot_far,
+    resid_far,
+    attn_out_far,
+    ada_wide,
+    bias_keys,
+    onehot,
     lhs_two,
     lhs_one,
     lhs_zero,
@@ -1186,9 +1199,6 @@
     cot,
     resid,
     attn_out,
-    ada_wide,
-    bias_keys,
-    onehot,
     mine,
     gathered,
     flat,
@@ -1217,6 +1227,8 @@
     pair_send,
     pair_recv,
     fc_sem,
+    out_sem,
+    part_sem,
 ):
     at = coords()
     core = at["core"]
@@ -1237,6 +1249,34 @@
 
     fc_load(0).start()
     fc_load(1).start()
+    outs = [
+        pltpu.make_async_copy(source, target, out_sem.at[index])
+        for index, (source, target) in enumerate(
+            (
+                (cot, cot_far),
+                (heads, heads_far),
+                (attn_out, attn_out_far),
+                (resid, resid_far),
+                (lhs_two, lhs_two_far),
+                (rhs_zero, rhs_zero_far),
+                (lhs_one, lhs_one_far),
+            )
+        )
+    ]
+
+    def part_out(part):
+        rows, chips = pl.ds(part * 1152, 1152), pl.ds(part * 4, 4)
+        return [
+            pltpu.make_async_copy(source, target, part_sem.at[index, part])
+            for index, (source, target) in enumerate(
+                (
+                    (act_out.at[rows], act_out_far.at[rows]),
+                    (slope_out.at[rows], slope_out_far.at[rows]),
+                    (lhs_zero.at[chips], lhs_zero_far.at[chips]),
+                )
+            )
+        ]
+
     barrier = pltpu.get_barrier_semaphore()
 
     def hello(hop, _):
@@ -1310,6 +1350,7 @@
         return _
 
     lax.fori_loop(0, 4, first_norm, 0)
+    outs[0].start()
 
     def blank(row, _):
         flat[row] = jnp.zeros((1, 128), jnp.float32)
@@ -1383,6 +1424,7 @@
         return _
 
     lax.fori_loop(0, 16, one_head, 0, unroll=4)
+    outs[1].start()
     pair_b = to_sibling(1, send_b, got_b)
     pair_b.start()
     for part in range(8):
@@ -1403,6 +1445,8 @@
         return _
 
     lax.fori_loop(0, 4, second_norm, 0)
+    outs[2].start()
+    outs[3].start()
     send_d[...] = normed[...].T
     pair_d = to_sibling(3, send_d, got_d)
     pair_d.start()
@@ -1450,23 +1494,34 @@
         some = pl.ds(part * 4, 4)
         pair_e.append(to_sibling(4 + part, send_e.at[some], got_e.at[some]))
         pair_e[-1].start()
+        part_out(part)[0].start()
+        part_out(part)[1].start()
         if part == 0:
             pair_b.wait()
             for chip in range(8):
                 rows = got_b[chip * 144 : chip * 144 + 144]
                 lhs_two[chip + 8, :, 256:512] = rows.astype(jnp.bfloat16)
+            outs[4].start()
         if part == 1:
             pair_c.wait()
             rhs_zero[:, 256:512] = got_c[...].astype(jnp.bfloat16)
+            outs[5].start()
         if part == 2:
             pair_d.wait()
             for chip in range(8):
                 rows = got_d[chip * 144 : chip * 144 + 144]
                 lhs_one[chip, :, 256:512] = rows.astype(jnp.bfloat16)
+            outs[6].start()
     for part in range(4):
         pair_e[part].wait()
         for chip in range(part * 4, part * 4 + 4):
             lhs_zero[chip, :, 256:512] = got_e[chip].astype(jnp.bfloat16)
+        part_out(part)[2].start()
+    for copy in outs:
+        copy.wait()
+    for part in range(4):
+        for copy in part_out(part):
+            copy.wait()
 
 
 def forward(operands):
@@ -1501,8 +1556,18 @@
         + [anywhere, vmem] * 2
         + [vmem, vmem]
         + [anywhere, vmem] * 3,
-        out_specs=(vmem,) * 16,
+        out_specs=(vmem,) * 3 + (anywhere,) * 10 + (vmem,) * 3,
         scratch_shapes=[
+            pltpu.VMEM((16, 144, 512), small),
+            pltpu.VMEM((8, 144, 512), small),
+            pltpu.VMEM((16, 144, 512), small),
+            pltpu.VMEM((1152, 512), small),
+            pltpu.VMEM((4608, 256), small),
+            pltpu.VMEM((4608, 256), small),
+            pltpu.VMEM((48, 80, 256), small),
+            pltpu.VMEM((256, 1152), full),
+            pltpu.VMEM((256, 1152), full),
+            pltpu.VMEM((256, 1152), full),
             pltpu.VMEM((2, 1, 256), full),
             pltpu.VMEM((32, 1, 256), full),
             pltpu.VMEM((56, 1, 128), full),
@@ -1531,6 +1596,8 @@
             dma((8,)),
             dma((8,)),
             dma((2,)),
+            dma((7,)),
+            dma((3, 4)),
         ],
         compiler_params=pltpu.CompilerParams(
             collective_id=2, has_side_effects=True, vmem_limit_bytes=255 * 2**18
@@ -1651,7 +1718,7 @@
             out((144,), full),
             out((36,), full),
         ),
-        in_specs=[vmem, vmem] + [anywhere] * 6,
+        in_specs=[vmem] * 8,
         out_specs=(anywhere,) * 6 + (vmem,) * 11,
         scratch_shapes=[pltpu.SemaphoreType.DMA((6,))],
         compiler_params=pltpu.CompilerParams(vmem_limit_bytes=255 * 2**18),

time: 319 us -> 216 us (0.68)
  Pallas kernels: 316 us -> 213 us
    pallas_call x1, Pallas kernels: 104 us -> 4.97 us  [finish(): pl.pallas_call(finish_kernel, out_shape=(out((36, 3456), full), out((36,...]
    pallas_call x1, Pallas kernels: 43.4 us -> 39.2 us  [forward(): pl.pallas_call(forward_kernel, out_shape=(out((2, 1152), full), out((2, 1...]
where the time goes in v5:
time: 216 us; the launch traced here: 215 us
  Pallas kernels  213 us (99%)
    pallas_call x1, Pallas kernels, backward(): pl.pallas_call(backward_kernel, out_shape=(jax.ShapeDtypeStruct((36, 3456...  169 us
    pallas_call x1, Pallas kernels, forward(): pl.pallas_call(forward_kernel, out_shape=(out((2, 1152), full), out((2, 1...  39.2 us
    pallas_call x1, Pallas kernels, finish(): pl.pallas_call(finish_kernel, out_shape=(out((36, 3456), full), out((36,...  4.97 us

profile of v5, /device:TPU:1, one launch (start us, length us, event | category | flops | bytes accessed | tf_op | source)
XLA Modules:
  0.0 214.9 jit_solution(11892427587512750185)
XLA Ops:
  0.7 0.7 convert_element_type.3
  1.3 0.1 multiply_cosine_fusion
  1.4 0.6 pad_maximum_fusion.feats
  2.0 39.2 %shard_map.323 = (f32[2,1152]{1,0:T(2,128)}, f32[2,1152]{1,0:T(2,128)}, f32[8,1152]{1,0:T(8,128)}, bf16[16,144,512]{2,1,0:T(8,128)(2,1)}, bf16[8,144,512]{2,1,0:...) custom-call(bf16[256,1152]{1,0:T(8,128)(2,1)} %tokens.3, ...), custom_call_target="tpu_custom_call" | custom-call | tf_op jit(solution)/shard_map/pallas_call | solution.py:1534
  41.2 168.5 %shard_map.324 = (f32[36,3456]{1,0:T(8,128)}, f32[36,1152]{1,0:T(8,128)}, f32[36,4608]{1,0:T(8,128)}, f32[144,1152]{1,0:T(8,128)}, bf16[256,1152]{1,0:T(8,128)(2...) custom-call(bf16[16,144,512]{2,1,0:T(8,128)(2,1)} %get-tuple-element.58.lhs_zero, ...), custom_call_target="tpu_custom_call" | custom-call | tf_op jit(solution)/shard_map/pallas_call | solution.py:1074
  209.7 5.0 %shard_map.325 = (f32[36,3456]{1,0:T(8,128)}, f32[36,1152]{1,0:T(8,128)}, f32[36,4608]{1,0:T(8,128)}, f32[144,1152]{1,0:T(8,128)}, bf16[256,1152]{1,0:T(8,128)(2...) custom-call(f32[4,2,5248]{2,1,0:T(2,128)} %get-tuple-element.74.pack, ...), custom_call_target="tpu_custom_call" | custom-call | tf_op jit(solution)/shard_map/pallas_call | solution.py:1700
  (1 shorter events, 0.0 us)

commit v6 on v5

--- a/solution.py
+++ b/solution.py
@@ -231,13 +231,6 @@
     def group_peer(hop):
         return (lax.rem(at["y"] + hop, 4), place)
 
-    def hello(hop, _):
-        pl.semaphore_signal(barrier, inc=1, device_id=dp_peer(hop), device_id_type=MESH)
-        return _
-
-    lax.fori_loop(1, 32, hello, 0)
-    for hop in (1, 2, 3):
-        pl.semaphore_signal(barrier, inc=1, device_id=group_peer(hop), device_id_type=MESH)
     def swap():
         return pltpu.make_async_remote_copy(
             src_ref=leave,
@@ -292,6 +285,8 @@
                     parts[half, stream, block, low - first : high - first, :] = rows[
                         low - OWN * unit : high - OWN * unit, unit * 128 : unit * 128 + 128
                     ]
+            if y_slot == 3:
+                parts[half, stream, block, 48:56, :] = jnp.zeros((8, 128), jnp.float32)
 
     def halving(phase, stream, step):
         order, pairing = STREAMS[phase][stream]
@@ -358,7 +353,7 @@
                 send(phase, stream, step + 1)
 
     def products(phase):
-        together, stacked = (3, 2) if phase == 2 else (2, 4)
+        together, stacked = (3, 4) if phase == 2 else (2, 8)
         for group in range(6 // together):
             members = range(group * together, (group + 1) * together)
             if phase == 0:
@@ -403,16 +398,17 @@
                     stream += 3 * ((member - members[0]) % 2)
                 send(phase, stream, 0)
 
-    def ring(phase):
+    def ring(phase, late):
         mine = at["y"]
         copies = []
         for place, hop in enumerate((1, 3)):
+            half = pl.ds(3 - place * 3 if late else place * 3, 3)
             copies.append(
                 pltpu.make_async_remote_copy(
-                    src_ref=final.at[phase, mine],
-                    dst_ref=final.at[phase, mine],
-                    send_sem=ring_send.at[phase, place],
-                    recv_sem=ring_recv.at[phase, place],
+                    src_ref=final.at[phase, mine, half],
+                    dst_ref=final.at[phase, mine, half],
+                    send_sem=ring_send.at[phase, place + 4 * late],
+                    recv_sem=ring_recv.at[phase, place + 4 * late],
                     device_id=device_at({**at, "y": lax.rem(mine + hop, 4)}),
                     device_id_type=MESH,
                 )
@@ -494,29 +490,22 @@
             pl.semaphore_signal(other_credit, inc=1, device_id=sibling, device_id_type=MESH)
 
     def ring_start(phase):
-        for copy in ring(phase):
-            copy.start()
+        for late in (0, 1):
+            for copy in ring(phase, late):
+                copy.start()
 
     def ring_relay(phase):
-        for copy, onward in zip(ring(phase), relay(phase)):
+        for copy, onward in zip(ring(phase, 0), relay(phase)):
             copy.wait()
             onward.start()
 
     def ring_finish(phase):
-        for copy in relay(phase):
+        for copy in ring(phase, 1) + relay(phase):
             copy.wait()
         if phase == 2:
             pl.semaphore_wait(other_credit, 1)
         if phase:
             across(phase).start()
-
-    def clear(chip, _):
-        z_place, x_place = lax.div(chip, 4), lax.rem(chip, 4)
-        for half in range(2):
-            for stream in range(6):
-                block = base_of(half, stream, z_place, x_place, 3)
-                parts[half, stream, block, 48:56, :] = jnp.zeros((8, 128), jnp.float32)
-        return _
 
     ones = jnp.ones((8, 256), jnp.bfloat16)
 
@@ -856,8 +845,8 @@
         return pltpu.make_async_remote_copy(
             src_ref=shares.at[lax.rem(place + hop, 32)],
             dst_ref=got.at[place],
-            send_sem=share_send.at[hop],
-            recv_sem=share_recv.at[hop],
+            send_sem=share_send,
+            recv_sem=share_recv,
             device_id=dp_peer(hop),
             device_id_type=MESH,
         )
@@ -866,8 +855,8 @@
         return pltpu.make_async_remote_copy(
             src_ref=conds.at[place],
             dst_ref=conds.at[place],
-            send_sem=cond_send.at[hop],
-            recv_sem=cond_recv.at[hop],
+            send_sem=cond_send,
+            recv_sem=cond_recv,
             device_id=dp_peer(hop),
             device_id_type=MESH,
         )
@@ -892,6 +881,16 @@
 
         lax.fori_loop(1, 32, one, 0)
 
+    def wait_all(source, target, sent, arrived):
+        pltpu.make_async_remote_copy(
+            src_ref=source.at[pl.ds(0, 31)],
+            dst_ref=target.at[pl.ds(0, 31)],
+            send_sem=sent,
+            recv_sem=arrived,
+            device_id=sibling,
+            device_id_type=MESH,
+        ).wait()
+
     def tail_share():
         ada_load().start()
         vectors = [d_mod[row : row + 1] for row in range(6)]
@@ -919,7 +918,7 @@
         each(share_to, lambda copy: copy.start())
 
     def tail_cond():
-        each(share_to, lambda copy: copy.wait())
+        wait_all(shares, got, share_send, share_recv)
         first, second = got[0], got[16]
         for source in range(1, 16):
             first = first + got[source]
@@ -964,7 +963,7 @@
         return pltpu.make_async_copy(w_t2.at[rows], wa.at[chunk % 2], load_sem.at[0, chunk % 2])
 
     def tail_group():
-        each(cond_to, lambda copy: copy.wait())
+        wait_all(conds, conds, cond_send, cond_recv)
         total_cond = conds[0]
         for source in range(1, 32):
             total_cond = total_cond + conds[source]
@@ -992,9 +991,16 @@
     lhs_load(0).start()
     rhs_load().start()
     mlp_begin()
+
+    def hello(hop, _):
+        pl.semaphore_signal(barrier, inc=1, device_id=dp_peer(hop), device_id_type=MESH)
+        return _
+
+    lax.fori_loop(1, 32, hello, 0)
+    for hop in (1, 2, 3):
+        pl.semaphore_signal(barrier, inc=1, device_id=group_peer(hop), device_id_type=MESH)
     for copy in heads_load(0):
         copy.start()
-    lax.fori_loop(0, 16, clear, 0)
     lhs_load(0).wait()
     rhs_load().wait()
     pl.semaphore_wait(barrier, 34)
@@ -1006,10 +1012,10 @@
     middle_begin()
     middle_rows(0, 4)
     receive(0, 0)
+    swap_finish(1)
+    products(1)
     middle_rows(4, 8)
     middle_end()
-    swap_finish(1)
-    products(1)
     qkv_load(0).start()
     attention_backward(0, 4)
     receive(0, 1)
@@ -1128,8 +1134,8 @@
             dma,
             regular,
             dma((2,)),
-            dma((3, 4)),
-            dma((3, 4)),
+            dma((3, 6)),
+            dma((3, 6)),
             dma((2,)),
             dma((2,)),
             dma((4, 2)),
@@ -1137,10 +1143,10 @@
             dma((3, 2)),
             regular,
             dma((2, 2)),
-            dma((32,)),
-            dma((32,)),
-            dma((32,)),
-            dma((32,)),
+            dma,
+            dma,
+            dma,
+            dma,
             dma((2, 4)),
             dma((2, 4)),
         ],
@@ -1305,18 +1311,14 @@
         return pltpu.make_async_remote_copy(
             src_ref=mine.at[lax.div(target, 16)],
             dst_ref=gathered.at[place],
-            send_sem=send.at[hop],
-            recv_sem=recv.at[hop],
+            send_sem=send,
+            recv_sem=recv,
             device_id=dp_peer(hop),
             device_id_type=MESH,
         )
 
     def begin(hop, _):
         copy_to(hop).start()
-        return _
-
-    def finish(hop, _):
-        copy_to(hop).wait()
         return _
 
     def norm(values):
@@ -1357,7 +1359,14 @@
         return _
 
     lax.fori_loop(0, 56, blank, 0)
-    lax.fori_loop(1, 32, finish, 0)
+    pltpu.make_async_remote_copy(
+        src_ref=gathered.at[pl.ds(0, 31)],
+        dst_ref=gathered.at[pl.ds(0, 31)],
+        send_sem=send,
+        recv_sem=recv,
+        device_id=sibling,
+        device_id_type=MESH,
+    ).wait()
     for piece in range(32):
         row, shift = piece * 216 // 128, piece * 216 % 128
         wide = jnp.concatenate([gathered[piece], jnp.zeros((1, 128), jnp.float32)], axis=1)
@@ -1590,8 +1599,8 @@
             pltpu.VMEM((1152, 256), full),
             pltpu.VMEM((1152, 256), full),
             pltpu.VMEM((16, 144, 256), full),
-            dma((32,)),
-            dma((32,)),
+            dma,
+            dma,
             dma((4,)),
             dma((8,)),
             dma((8,)),

time: 216 us -> 213 us (0.986)
  Pallas kernels: 213 us -> 209 us
    pallas_call x1, Pallas kernels: 169 us -> 165 us  [backward(): pl.pallas_call(backward_kernel, out_shape=(jax.ShapeDtypeStruct((36, 3456...]
where the time goes in v6:
time: 213 us; the launch traced here: 211 us
  Pallas kernels  209 us (98%)
    pallas_call x1, Pallas kernels, backward(): pl.pallas_call(backward_kernel, out_shape=(jax.ShapeDtypeStruct((36, 3456...  165 us
    pallas_call x1, Pallas kernels, forward(): pl.pallas_call(forward_kernel, out_shape=(out((2, 1152), full), out((2, 1...  38.5 us
    pallas_call x1, Pallas kernels, finish(): pl.pallas_call(finish_kernel, out_shape=(out((36, 3456), full), out((36,...  4.97 us

profile of v6, /device:TPU:1, one launch (start us, length us, event | category | flops | bytes accessed | tf_op | source)
XLA Modules:
  0.0 211.1 jit_solution(11276721699661446692)
XLA Ops:
  0.7 0.7 convert_element_type.3
  1.3 0.1 multiply_cosine_fusion
  1.4 0.6 pad_maximum_fusion.feats
  2.0 38.5 %shard_map.323 = (f32[2,1152]{1,0:T(2,128)}, f32[2,1152]{1,0:T(2,128)}, f32[8,1152]{1,0:T(8,128)}, bf16[16,144,512]{2,1,0:T(8,128)(2,1)}, bf16[8,144,512]{2,1,0:...) custom-call(bf16[256,1152]{1,0:T(8,128)(2,1)} %tokens.3, ...), custom_call_target="tpu_custom_call" | custom-call | tf_op jit(solution)/shard_map/pallas_call | solution.py:1543
  40.5 165.5 %shard_map.324 = (f32[36,3456]{1,0:T(8,128)}, f32[36,1152]{1,0:T(8,128)}, f32[36,4608]{1,0:T(8,128)}, f32[144,1152]{1,0:T(8,128)}, bf16[256,1152]{1,0:T(8,128)(2...) custom-call(bf16[16,144,512]{2,1,0:T(8,128)(2,1)} %get-tuple-element.58.lhs_zero, ...), custom_call_target="tpu_custom_call" | custom-call | tf_op jit(solution)/shard_map/pallas_call | solution.py:1080
  206.0 5.0 %shard_map.325 = (f32[36,3456]{1,0:T(8,128)}, f32[36,1152]{1,0:T(8,128)}, f32[36,4608]{1,0:T(8,128)}, f32[144,1152]{1,0:T(8,128)}, bf16[256,1152]{1,0:T(8,128)(2...) custom-call(f32[4,2,5248]{2,1,0:T(2,128)} %get-tuple-element.74.pack, ...), custom_call_target="tpu_custom_call" | custom-call | tf_op jit(solution)/shard_map/pallas_call | solution.py:1709
  (1 shorter events, 0.0 us)

commit v7 on v6

--- a/solution.py
+++ b/solution.py
@@ -1432,7 +1432,7 @@
         send_b[rows, :] = dot_nn(value, weights)[0:72]
         return _
 
-    lax.fori_loop(0, 16, one_head, 0, unroll=4)
+    lax.fori_loop(0, 16, one_head, 0, unroll=8)
     outs[1].start()
     pair_b = to_sibling(1, send_b, got_b)
     pair_b.start()

time: 213 us -> 212 us (level)
  no operation moved by 1% of the time
where the time goes in v7:
time: 212 us; the launch traced here: 211 us
  Pallas kernels  209 us (99%)
    pallas_call x1, Pallas kernels, backward(): pl.pallas_call(backward_kernel, out_shape=(jax.ShapeDtypeStruct((36, 3456...  165 us
    pallas_call x1, Pallas kernels, forward(): pl.pallas_call(forward_kernel, out_shape=(out((2, 1152), full), out((2, 1...  38.1 us
    pallas_call x1, Pallas kernels, finish(): pl.pallas_call(finish_kernel, out_shape=(out((36, 3456), full), out((36,...  4.97 us

profile of v7, /device:TPU:1, one launch (start us, length us, event | category | flops | bytes accessed | tf_op | source)
XLA Modules:
  0.0 210.8 jit_solution(6013527051165929532)
XLA Ops:
  0.7 0.7 convert_element_type.3
  1.3 0.1 multiply_cosine_fusion
  1.4 0.6 pad_maximum_fusion.feats
  2.0 38.1 %shard_map.323 = (f32[2,1152]{1,0:T(2,128)}, f32[2,1152]{1,0:T(2,128)}, f32[8,1152]{1,0:T(8,128)}, bf16[16,144,512]{2,1,0:T(8,128)(2,1)}, bf16[8,144,512]{2,1,0:...) custom-call(bf16[256,1152]{1,0:T(8,128)(2,1)} %tokens.3, ...), custom_call_target="tpu_custom_call" | custom-call | tf_op jit(solution)/shard_map/pallas_call | solution.py:1543
  40.2 165.5 %shard_map.324 = (f32[36,3456]{1,0:T(8,128)}, f32[36,1152]{1,0:T(8,128)}, f32[36,4608]{1,0:T(8,128)}, f32[144,1152]{1,0:T(8,128)}, bf16[256,1152]{1,0:T(8,128)(2...) custom-call(bf16[16,144,512]{2,1,0:T(8,128)(2,1)} %get-tuple-element.58.lhs_zero, ...), custom_call_target="tpu_custom_call" | custom-call | tf_op jit(solution)/shard_map/pallas_call | solution.py:1080
  205.6 5.0 %shard_map.325 = (f32[36,3456]{1,0:T(8,128)}, f32[36,1152]{1,0:T(8,128)}, f32[36,4608]{1,0:T(8,128)}, f32[144,1152]{1,0:T(8,128)}, bf16[256,1152]{1,0:T(8,128)(2...) custom-call(f32[4,2,5248]{2,1,0:T(2,128)} %get-tuple-element.74.pack, ...), custom_call_target="tpu_custom_call" | custom-call | tf_op jit(solution)/shard_map/pallas_call | solution.py:1709
  (1 shorter events, 0.0 us)
